TPU v7x, 32 devices: a whole 2x2x4 slice. The times are simulated.
32 devices in a mesh: grp: 1, pool: 16 (over z, y, x), samp: 2 (over core).
Axes of the slice: x: 2, y: 2, z: 4, core: 2. Of those that a mesh axis runs over, the one named last changes fastest.
Arguments:
- samples: bfloat16 [2, 1024, 1024], P(('grp', 'samp'), 'pool'), may hold values from -11 to 11
- pool: bfloat16 [16384, 1024], P(('grp', 'pool')), may hold values from -11 to 11
- tile_list: int32 [2, 16, 4, 2], P(('grp', 'samp'), 'pool'), may hold values from 0 to 1, as said below
- tile_count: int32 [2, 16], P(('grp', 'samp'), 'pool'), may hold values from 1 to 4, as said below
Outputs:
- sample_potential: float32 [2, 1024], P(('grp', 'samp'), 'pool')
- pool_potential: float32 [16384], P(('grp', 'pool'))
Inputs may be any that keep to these rules, and one draw needn't show every extreme that they name: `tile_list`: entry [h, p, k] is a pair (sample tile of half h, 0 to 1; one of the 2 tiles of pool device p). The 4 pairs of one (h, p) are distinct, and among the counted pairs every sample tile and every pool tile appears at least once. The first tile_count[h, p] pairs of tile_list[h, p] count; 4 on at least one (h, p).
All inputs are finite; a program needn't handle non-finite values.
Results may differ from a plain program's by a relative error of at most 0.0003.
Values may be sent and summed in bfloat16 or wider, within the bound.
No kernel may reach another device: no remote copies, remote signals or barrier semaphores. Data moves between devices by JAX's collectives and lax.ppermute only.
A program may use at most 64 MiB of HBM per device.

v0:
```python
import math

import jax
import jax.numpy as jnp
from jax import lax
from jax.sharding import PartitionSpec as P

TILE = 512
CAP = 4
ITERS = 3


EPS = 0.02
NEG = -1e30


def distance_rows(rows, columns, column_norm):
    dots = jnp.einsum("id,jd->ij", rows, columns, preferred_element_type=jnp.float32)
    row_norm = jnp.sum(jnp.square(rows.astype(jnp.float32)), axis=1)
    return (row_norm[:, None] + column_norm[None, :] - 2.0 * dots) / rows.shape[1]


def merge_into(peak, total, low, tile_peak, scores, axis):
    tile_total = jnp.sum(jnp.exp(scores - jnp.expand_dims(tile_peak, axis)), axis=axis)
    old_peak = lax.dynamic_slice_in_dim(peak, low, TILE, 0)
    old_total = lax.dynamic_slice_in_dim(total, low, TILE, 0)
    new_peak = jnp.maximum(old_peak, tile_peak)
    new_total = old_total * jnp.exp(old_peak - new_peak) + tile_total * jnp.exp(
        tile_peak - new_peak
    )
    return (
        lax.dynamic_update_slice_in_dim(peak, new_peak, low, 0),
        lax.dynamic_update_slice_in_dim(total, new_total, low, 0),
    )


def body(samples, pool, tile_list, tile_count):
    own_rows = samples.shape[1]
    width = samples.shape[2]
    pool_size = lax.axis_size("pool")
    half_rows = own_rows * pool_size
    pool_rows = pool.shape[0]
    log_a = -math.log(half_rows * lax.axis_size("samp"))
    log_b = -math.log(pool_rows * pool_size)
    pairs = tile_list.reshape(CAP, 2)
    count = tile_count.reshape(())
    own_low = pairs[:, 0] * TILE
    own_col = pairs[:, 1] * TILE
    total_slots = own_low.shape[0]
    sequence = jnp.arange(total_slots, dtype=jnp.int32)
    order = jnp.where(sequence < count, sequence, sequence - count + CAP)
    column_norm = jnp.sum(jnp.square(pool.astype(jnp.float32)), axis=1)

    def source_block(slot):
        first = own_col[slot]
        return (
            lax.dynamic_slice_in_dim(pool, first, TILE, 0),
            lax.dynamic_slice_in_dim(column_norm, first, TILE, 0),
        )

    gathered = lax.all_gather(samples, "pool", axis=1, tiled=True).reshape(half_rows, width)

    def fetch(slot):
        rows = lax.dynamic_slice_in_dim(gathered, own_low[slot], TILE, 0)
        columns, norms = source_block(slot)
        return distance_rows(rows, columns, norms)

    pool_potential = jnp.zeros((pool_rows,), jnp.float32)
    sample_potential = jnp.zeros((half_rows,), jnp.float32)
    for step in range(ITERS):
        shift_source = pool_potential

        def row_advance(step_index, carry):
            slot = order[step_index]
            shift = lax.dynamic_slice_in_dim(shift_source, own_col[slot], TILE, 0)
            scores = (shift[None, :] - fetch(slot)) / EPS
            return merge_into(carry[0], carry[1], own_low[slot], jnp.max(scores, axis=1), scores, 1)

        row_start_state = (
            jnp.full((half_rows,), NEG, jnp.float32),
            jnp.zeros((half_rows,), jnp.float32),
        )
        row_peak, row_total = lax.fori_loop(0, count, row_advance, row_start_state)
        row_summit = lax.pmax(row_peak, "pool")
        row_total = lax.psum(row_total * jnp.exp(row_peak - row_summit), "pool")
        row_peak = row_summit
        sample_potential = EPS * (log_a - row_peak - jnp.log(row_total))

        def col_advance(step_index, carry):
            slot = order[step_index]
            shift = lax.dynamic_slice_in_dim(sample_potential, own_low[slot], TILE, 0)
            scores = (shift[:, None] - fetch(slot)) / EPS
            return merge_into(carry[0], carry[1], own_col[slot], jnp.max(scores, axis=0), scores, 0)

        start_state = (
            jnp.full((pool_rows,), NEG, jnp.float32),
            jnp.zeros((pool_rows,), jnp.float32),
        )
        peak_all, total_all = lax.fori_loop(0, count, col_advance, start_state)
        peak = peak_all
        total = total_all
        summit = lax.pmax(peak, "samp")
        total = lax.psum(total * jnp.exp(peak - summit), "samp")
        peak = summit
        pool_potential = EPS * (log_b - peak - jnp.log(total))
    own = lax.dynamic_slice_in_dim(sample_potential, lax.axis_index("pool") * own_rows, own_rows, 0)
    return (own.reshape(1, own_rows), pool_potential)


def solution(mesh):
    placed = (
        P(("grp", "samp"), "pool", None),
        P(("grp", "pool"), None),
        P(("grp", "samp"), "pool", None, None),
        P(("grp", "samp"), "pool"),
    )
    return jax.shard_map(
        body,
        mesh=mesh,
        in_specs=placed,
        out_specs=(P(("grp", "samp"), "pool"), P(("grp", "pool"))),
        check_vma=False,
    )
```

profile of v0, /device:TPU:5, one launch (start us, length us, event | category | flops | bytes accessed | tf_op | source)
XLA Modules:
  0.0 615.5 jit_solution(11274466057587811868)
XLA Ops:
  11.4 60.9 %all-gather.2.cloned.1.call-done = bf16[1,1024,1024]{2,1,0:T(8,128)(2,1)} async-done(((bf16[1,64,1024]{2,1,0:T(8,128)(2,1)}), bf16[1,1024,1024]{2,1,0:T(8,128)(2,1)}) %all-gather.2.cloned.1.call-update) | async-done | bytes 2097168 | tf_op jit(solution)/shard_map/all_gather | solution.py:61
  72.3 50.4 %while.72 = (s32[]{:T(128)}, f32[1024]{0:T(1024)S(1)}, f32[1024]{0:T(1024)S(1)}, s32[]{:T(128)}, s32[4]{0:T(128)S(1)}, /*index=5*/s32[4]{0:T(128)S(1)}, bf16[102...) while((s32[]{:T(128)}, f32[1024]{0:T(1024)S(1)}, ...), condition=%wide.region_5.6_spmd, body=%wide.region_1.5_spmd.sunk | while | flops 540804608 | bytes 5271877 | solution.py:83
  82.2 2.1 fusion.54
  107.1 2.1 fusion.54
  122.7 28.5 %pmax.42 = f32[1024]{0:T(1024)S(1)} all-reduce(f32[1024]{0:T(1024)S(1)} %get-tuple-element.351), channel_id=1, replica_groups=mesh['grp'=1,'pool'=16,'samp'=2] {'pool'}, use_global_device_ids=true, to_apply=%region_6.7 | all-reduce | flops 1024 | bytes 8192 | tf_op jit(solution)/shard_map/pmax | solution.py:84
  151.2 30.3 %psum.42 = f32[1024]{0:T(1024)S(1)} all-reduce(f32[1024]{0:T(1024)S(1)} %exponential_multiply_fusion.5), channel_id=1, replica_groups=mesh['grp'=1,'pool'=16,'samp'=2] {'pool'}, use_global_device_ids=true, to_apply=%region_7.8 | all-reduce | flops 1024 | bytes 8192 | tf_op jit(solution)/shard_map/psum | solution.py:85
  181.6 47.0 %while.73 = (s32[]{:T(128)}, f32[1024]{0:T(1024)S(1)}, f32[1024]{0:T(1024)S(1)}, s32[]{:T(128)}, s32[4]{0:T(128)S(1)}, /*index=5*/s32[4]{0:T(128)S(1)}, s32[4]{0...) while((s32[]{:T(128)}, f32[1024]{0:T(1024)S(1)}, ...), condition=%wide.region_12.13_spmd, body=%wide.region_8.12_spmd.sunk | while | flops 540804608 | bytes 5278033 | solution.py:99
  228.6 15.3 %pmax.43 = f32[1024]{0:T(1024)S(1)} all-reduce(f32[1024]{0:T(1024)S(1)} %get-tuple-element.353), channel_id=1, replica_groups=mesh['grp'=1,'pool'=16,'samp'=2] {'samp'}, use_global_device_ids=true, to_apply=%region_13.14 | all-reduce | flops 1024 | bytes 8192 | tf_op jit(solution)/shard_map/pmax | solution.py:102
  243.8 2.5 psum.43
  246.3 50.0 %while.74 = (s32[]{:T(128)}, f32[1024]{0:T(1024)S(1)}, f32[1024]{0:T(1024)S(1)}, s32[]{:T(128)}, s32[4]{0:T(128)S(1)}, /*index=5*/s32[4]{0:T(128)S(1)}, s32[4]{0...) while((s32[]{:T(128)}, f32[1024]{0:T(1024)S(1)}, ...), condition=%wide.region_19.20_spmd, body=%wide.region_15.19_spmd.sunk | while | flops 540804608 | bytes 5278033 | solution.py:83
  256.1 2.1 fusion.56
  280.8 2.1 fusion.56
  296.3 23.4 %pmax.44 = f32[1024]{0:T(1024)S(1)} all-reduce(f32[1024]{0:T(1024)S(1)} %get-tuple-element.355), channel_id=1, replica_groups=mesh['grp'=1,'pool'=16,'samp'=2] {'pool'}, use_global_device_ids=true, to_apply=%region_20.21 | all-reduce | flops 1024 | bytes 8192 | tf_op jit(solution)/shard_map/pmax | solution.py:84
  319.8 31.6 %psum.44 = f32[1024]{0:T(1024)S(1)} all-reduce(f32[1024]{0:T(1024)S(1)} %exponential_multiply_fusion.3), channel_id=1, replica_groups=mesh['grp'=1,'pool'=16,'samp'=2] {'pool'}, use_global_device_ids=true, to_apply=%region_21.22 | all-reduce | flops 1024 | bytes 8192 | tf_op jit(solution)/shard_map/psum | solution.py:85
  351.4 49.9 %while.75 = (s32[]{:T(128)}, f32[1024]{0:T(1024)S(1)}, f32[1024]{0:T(1024)S(1)}, s32[]{:T(128)}, s32[4]{0:T(128)S(1)}, /*index=5*/s32[4]{0:T(128)S(1)}, s32[4]{0...) while((s32[]{:T(128)}, f32[1024]{0:T(1024)S(1)}, ...), condition=%wide.region_26.27_spmd, body=%wide.region_22.26_spmd.sunk | while | flops 540804608 | bytes 5278033 | solution.py:99
  401.3 22.6 %pmax.45 = f32[1024]{0:T(1024)S(1)} all-reduce(f32[1024]{0:T(1024)S(1)} %get-tuple-element.357), channel_id=1, replica_groups=mesh['grp'=1,'pool'=16,'samp'=2] {'samp'}, use_global_device_ids=true, to_apply=%region_27.28 | all-reduce | flops 1024 | bytes 8192 | tf_op jit(solution)/shard_map/pmax | solution.py:102
  423.9 2.5 psum.45
  426.4 50.0 %while.76 = (s32[]{:T(128)}, f32[1024]{0:T(1024)S(1)}, f32[1024]{0:T(1024)S(1)}, s32[]{:T(128)}, s32[4]{0:T(128)S(1)}, /*index=5*/s32[4]{0:T(128)S(1)}, s32[4]{0...) while((s32[]{:T(128)}, f32[1024]{0:T(1024)S(1)}, ...), condition=%wide.region_33.34_spmd, body=%wide.region_29.33_spmd.sunk | while | flops 540804608 | bytes 5278033 | solution.py:83
  460.9 2.1 fusion.58
  476.4 23.4 %pmax.46 = f32[1024]{0:T(1024)S(1)} all-reduce(f32[1024]{0:T(1024)S(1)} %get-tuple-element.359), channel_id=1, replica_groups=mesh['grp'=1,'pool'=16,'samp'=2] {'pool'}, use_global_device_ids=true, to_apply=%region_34.35 | all-reduce | flops 1024 | bytes 8192 | tf_op jit(solution)/shard_map/pmax | solution.py:84
  499.9 31.6 %psum.46 = f32[1024]{0:T(1024)S(1)} all-reduce(f32[1024]{0:T(1024)S(1)} %exponential_multiply_fusion.1), channel_id=1, replica_groups=mesh['grp'=1,'pool'=16,'samp'=2] {'pool'}, use_global_device_ids=true, to_apply=%region_35.36 | all-reduce | flops 1024 | bytes 8192 | tf_op jit(solution)/shard_map/psum | solution.py:85
  531.5 51.0 %while.77 = (s32[]{:T(128)}, f32[1024]{0:T(1024)S(1)}, f32[1024]{0:T(1024)S(1)}, s32[]{:T(128)}, s32[4]{0:T(128)S(1)}, /*index=5*/s32[4]{0:T(128)S(1)}, s32[4]{0...) while((s32[]{:T(128)}, f32[1024]{0:T(1024)S(1)}, ...), condition=%wide.region_40.41_spmd, body=%wide.region_36.40_spmd.sunk | while | flops 540804608 | bytes 5278033 | solution.py:99
  582.5 22.6 %pmax.47 = f32[1024]{0:T(1024)S(1)} all-reduce(f32[1024]{0:T(1024)S(1)} %get-tuple-element.361), channel_id=1, replica_groups=mesh['grp'=1,'pool'=16,'samp'=2] {'samp'}, use_global_device_ids=true, to_apply=%region_41.42 | all-reduce | flops 1024 | bytes 8192 | tf_op jit(solution)/shard_map/pmax | solution.py:102
  605.0 2.5 psum.47
  (239 shorter events, 140.6 us)
Async XLA Ops:
  7.2 65.1 %copy-start = (bf16[1024,1024]{1,0:T(8,128)(2,1)S(1)}, bf16[1024,1024]{1,0:T(8,128)(2,1)}, u32[]{:S(2)}) copy-start(bf16[1024,1024]{1,0:T(8,128)(2,1)} %param.17) | copy-start | bytes 6291460
  7.2 65.1 %all-gather.2.cloned.1.call-start = ((), (), s32[]{:S(2)}) async-start(), calls=%async_computation | async-start | bytes 2228224 | tf_op jit(solution)/shard_map/all_gather | solution.py:61
Sparse Core Ops, SparseCore 0:
  10.8 61.4 all-gather.1
where the time goes:
time: 616 us
  blocking collectives  237 us (38%)
  loops' own time  152 us (25%)
  waiting for transfers between devices  61.5 us (10%)
  other arithmetic  53.1 us (9%)
  matrix products  50.2 us (8%)
  local copies, waits for them, and re-layouts  47 us (8%)
  between operations  14.8 us (2%)
    psum x3, blocking collectives, body(): row_total = lax.psum(row_total * jnp.exp(row_peak - row_summit), 'pool')  93.6 us
    another operation x3, loops' own time, body(): row_peak, row_total = lax.fori_loop(0, count, row_advance, row_start_state)  77 us
    pmax x3, blocking collectives, body(): row_summit = lax.pmax(row_peak, 'pool')  75.3 us
    another operation x3, loops' own time, body(): peak_all, total_all = lax.fori_loop(0, count, col_advance, start_state)  75.1 us
    all_gather x1, waiting for transfers between devices, body(): lax.all_gather(samples, 'pool', axis=1, tiled=True)  60.9 us
    pmax x3, blocking collectives, body(): summit = lax.pmax(peak, 'samp')  60.4 us
    dot_general x24, matrix products, distance_rows(): jnp.einsum('id,jd->ij', rows, columns, preferred_element_type=jnp.float32)  50.2 us
    reduce_sum x24, other arithmetic, distance_rows(): row_norm = jnp.sum(jnp.square(rows.astype(jnp.float32)), axis=1)  39.8 us
  transfers between devices with their start and end apart: 1, of which 1 were waited for; matrix products, arithmetic and copies ran while one was open for 0% of the time, Pallas kernels for 0%

commit v1 on v0

v1 whole, which is shorter than its diff:
```python
import functools
import math

import jax
import jax.numpy as jnp
from jax import lax
from jax.experimental import pallas as pl
from jax.experimental.pallas import tpu as pltpu
from jax.sharding import PartitionSpec as P

TILE = 512
CAP = 4
ITERS = 3


EPS = 0.02
NEG = -1e30
LN2 = math.log(2.0)
VMEM_LIMIT = 32 * 1024 * 1024


def log2_sum(values):
    peak = functools.reduce(jnp.maximum, values)
    total = functools.reduce(jnp.add, [jnp.exp2(v - peak) for v in values])
    return peak + jnp.log(total) * (1.0 / LN2)


def score_kernel(rel, scale, own_rows, me_ref, list_ref, count_ref, *refs):
    pool_ref, out_ref = refs[-2:]
    me = me_ref[0]
    tiles = pool_ref.shape[0] // TILE
    first = 0
    for rows_ref in refs[:-2]:
        dots = lax.dot_general(
            rows_ref[...],
            pool_ref[...],
            (((1,), (1,)), ((), ())),
            preferred_element_type=jnp.float32,
        )
        for part in range(rows_ref.shape[0] // own_rows):
            tile = lax.div((me ^ rel[first + part]) * own_rows, TILE)
            low = (first + part) * own_rows
            for u in range(tiles):
                counted = jnp.int32(0)
                for k in range(CAP):
                    hit = (k < count_ref[0]) & (list_ref[k, 0] == tile) & (list_ref[k, 1] == u)
                    counted += jnp.where(hit, 1, 0)
                offset = jnp.where(counted > 0, 0.0, NEG)
                block = dots[part * own_rows : (part + 1) * own_rows, u * TILE : (u + 1) * TILE]
                out_ref[low : low + own_rows, u * TILE : (u + 1) * TILE] = block * scale + offset
        first += rows_ref.shape[0] // own_rows


def diagonal(size):
    rows = lax.broadcasted_iota(jnp.int32, (size, size), 0)
    return rows == lax.broadcasted_iota(jnp.int32, (size, size), 1)


def row_kernel(rels, own_rows, me_ref, shift_ref, *refs):
    out_ref = refs[-1]
    me = me_ref[0]
    shift = shift_ref[...]
    eye = diagonal(own_rows)
    for ref, rel in zip(refs[:-1], rels):
        for part, source in enumerate(rel):
            block = ref[part * own_rows : (part + 1) * own_rows, :] + shift
            peak = jnp.max(block, axis=1, keepdims=True)
            total = jnp.sum(jnp.exp2(block - peak), axis=1, keepdims=True)
            column = peak + jnp.log(total) * (1.0 / LN2)
            row = jnp.sum(jnp.where(eye, column, 0.0), axis=0, keepdims=True)
            out_ref[pl.ds(me ^ source, 1), :] = row


def column_kernel(rels, own_rows, me_ref, shift_ref, *refs):
    out_ref = refs[-1]
    me = me_ref[0]
    eye = diagonal(own_rows)
    columns = []
    peak = None
    for ref, rel in zip(refs[:-1], rels):
        for part, source in enumerate(rel):
            row = shift_ref[pl.ds(me ^ source, 1), :]
            column = jnp.sum(jnp.where(eye, row, 0.0), axis=1, keepdims=True)
            columns.append(column)
            block = ref[part * own_rows : (part + 1) * own_rows, :] + column
            high = jnp.max(block.reshape(own_rows // 8, 8, block.shape[1]), axis=0)
            peak = high if peak is None else jnp.maximum(peak, high)
    peak = jnp.max(peak, axis=0, keepdims=True)
    total = jnp.zeros((8, peak.shape[1]), jnp.float32)
    for ref, rel in zip(refs[:-1], rels):
        for part, source in enumerate(rel):
            column = columns.pop(0)
            block = ref[part * own_rows : (part + 1) * own_rows, :] + (column - peak)
            total += jnp.sum(jnp.exp2(block).reshape(own_rows // 8, 8, block.shape[1]), axis=0)
    total = jnp.sum(total, axis=0, keepdims=True)
    out_ref[...] = peak + jnp.log(total) * (1.0 / LN2)


def call(kernel, out_shape, scalars, arrays, flops, name):
    smem = pl.BlockSpec(memory_space=pltpu.SMEM)
    vmem = pl.BlockSpec(memory_space=pltpu.VMEM)
    moved = sum(a.size * a.dtype.itemsize for a in arrays) + 4 * math.prod(out_shape)
    return pl.pallas_call(
        kernel,
        out_shape=jax.ShapeDtypeStruct(out_shape, jnp.float32),
        in_specs=[smem] * len(scalars) + [vmem] * len(arrays),
        out_specs=vmem,
        compiler_params=pltpu.CompilerParams(vmem_limit_bytes=VMEM_LIMIT),
        cost_estimate=pl.CostEstimate(flops=flops, bytes_accessed=moved, transcendentals=0),
        name=name,
    )(*scalars, *arrays)


def body(samples, pool, tile_list, tile_count):
    own_rows, width = samples.shape[1:]
    size = lax.axis_size("pool")
    half_rows = own_rows * size
    pool_rows = pool.shape[0]
    unit = EPS * LN2
    log_a = -math.log2(half_rows * lax.axis_size("samp"))
    log_b = -math.log2(pool_rows * size)
    me = lax.axis_index("pool").astype(jnp.int32).reshape(1)
    scalars = [me, tile_list.reshape(CAP, 2), tile_count.reshape(1)]
    own = samples.reshape(own_rows, width)

    def swap(value, mask):
        return lax.ppermute(value, "pool", [(i, i ^ mask) for i in range(size)])

    def score(pieces, rels):
        rel = sum(rels, ())
        shape = (len(rel) * own_rows, pool_rows)
        flops = 2 * shape[0] * pool_rows * width
        kernel = functools.partial(score_kernel, rel, 2.0 / (width * unit), own_rows)
        return call(kernel, shape, scalars, pieces + [pool], flops, "score"), rel

    outer = tuple(range(0, size, 4))
    plane = jnp.concatenate([own] + [swap(own, m) for m in outer[1:]], axis=0)
    half = plane.shape[0] // 2
    first, second = outer[: size // 8], outer[size // 8 :]
    by_x = swap(plane, 1)
    by_y = swap(plane, 2)
    low = swap(by_x[:half], 2)
    high = swap(by_y[half:], 1)
    parts = [
        score([plane], [outer]),
        score([by_x, by_y], [tuple(m ^ 1 for m in outer), tuple(m ^ 2 for m in outer)]),
        score([low, high], [tuple(m ^ 3 for m in first), tuple(m ^ 3 for m in second)]),
    ]
    scores = [p[0] for p in parts]
    rels = [p[1] for p in parts]

    own_norm = jnp.sum(jnp.square(own.astype(jnp.float32)), axis=1) / width
    pool_norm = jnp.sum(jnp.square(pool.astype(jnp.float32)), axis=1) / width
    shift = pool_norm.reshape(1, pool_rows) * (-1.0 / unit)
    flops = 8 * half_rows * pool_rows
    for _ in range(ITERS):
        kernel = functools.partial(row_kernel, rels, own_rows)
        value = call(kernel, (size, own_rows), [me], [shift] + scores, flops, "rows")
        step = 1
        while step < size:
            masks = [m * step for m in range(1, min(4, size // step))]
            value = log2_sum([value] + [swap(value, m) for m in masks])
            step *= 4
        sample_shift = log_a - value
        kernel = functools.partial(column_kernel, rels, own_rows)
        value = call(kernel, (1, pool_rows), [me], [sample_shift] + scores, flops, "columns")
        pairs = [(i, i ^ 1) for i in range(2)]
        shift = log_b - log2_sum([value, lax.ppermute(value, "samp", pairs)])
    mine = lax.dynamic_slice_in_dim(sample_shift, me[0], 1, 0)
    return mine * unit + own_norm[None, :], shift.reshape(pool_rows) * unit + pool_norm


def solution(mesh):
    placed = (
        P(("grp", "samp"), "pool", None),
        P(("grp", "pool"), None),
        P(("grp", "samp"), "pool", None, None),
        P(("grp", "samp"), "pool"),
    )
    return jax.shard_map(
        body,
        mesh=mesh,
        in_specs=placed,
        out_specs=(P(("grp", "samp"), "pool"), P(("grp", "pool"))),
        check_vma=False,
    )
```

time: 616 us -> 100 us (0.16)
  the two profiles are of different devices: /device:TPU:5 before, /device:TPU:0 now
where the time goes in v1:
time: 100 us; the launch traced here: 99.7 us
  waiting for transfers between devices  39.2 us (39%)
  starting transfers between devices  37.4 us (37%)
  Pallas kernels  12.1 us (12%)
  local copies, waits for them, and re-layouts  4.84 us (5%)
  other arithmetic  4.51 us (5%)
  between operations  1.67 us (2%)
    ppermute x25, starting transfers between devices, swap(): return lax.ppermute(value, 'pool', [(i, i ^ mask) for i in range(size)])  37.2 us
    ppermute x25, waiting for transfers between devices, swap(): return lax.ppermute(value, 'pool', [(i, i ^ mask) for i in range(size)])  36.2 us
    pallas_call x9, Pallas kernels, call(): pl.pallas_call(kernel, out_shape=jax.ShapeDtypeStruct(out_shape, jnp.floa...  12.1 us
    unnamed x24, local copies, waits for them, and re-layouts  3.19 us
    ppermute x3, waiting for transfers between devices, body(): shift = log_b - log2_sum([value, lax.ppermute(value, 'samp', pairs)])  2.93 us
    reduce_sum x1, other arithmetic, body(): pool_norm = jnp.sum(jnp.square(pool.astype(jnp.float32)), axis=1) / width  2.07 us
  transfers between devices with their start and end apart: 28, of which 22 were waited for; matrix products, arithmetic and copies ran while one was open for 4% of the time, Pallas kernels for 3%

profile of v1, /device:TPU:0, one launch (start us, length us, event | category | flops | bytes accessed | tf_op | source)
XLA Modules:
  0.0 99.7 jit_solution(12202964905827848029)
XLA Ops:
  0.7 3.1 %collective-permute-start = (bf16[64,1024]{1,0:T(8,128)(2,1)}, bf16[64,1024]{1,0:T(8,128)(2,1)S(1)}, u32[]{:S(2)}, u32[]{:S(2)}) collective-permute-start(bf16[64,1024]{1,0:T(8,128)(2,1)} %bitcast.13), channel_id=1, source_target_pairs={{0,8},{2,10},{4,12},{6,14},{8,0},{10,2},{12,4},{14,6},{16,24},{18,... | collective-permute-start | bytes 393224 | tf_op jit(solution)/shard_map/ppermute | solution.py:127
  3.7 2.6 %collective-permute-start.1 = (bf16[64,1024]{1,0:T(8,128)(2,1)}, bf16[64,1024]{1,0:T(8,128)(2,1)S(1)}, u32[]{:S(2)}, u32[]{:S(2)}) collective-permute-start(bf16[64,1024]{1,0:T(8,128)(2,1)} %bitcast.14), channel_id=1, source_target_pairs={{0,16},{2,18},{4,20},{6,22},{8,24},{10,26},{12,28},{14,30},{16,0},... | collective-permute-start | bytes 393224 | tf_op jit(solution)/shard_map/ppermute | solution.py:127
  6.3 2.7 %collective-permute-done = bf16[64,1024]{1,0:T(8,128)(2,1)S(1)} collective-permute-done((bf16[64,1024]{1,0:T(8,128)(2,1)}, bf16[64,1024]{1,0:T(8,128)(2,1)S(1)}, u32[]{:S(2)}, u32[]{:S(2)}) %collective-permute-start) | collective-permute-done | bytes 131104 | tf_op jit(solution)/shard_map/ppermute | solution.py:127
  9.0 7.9 %collective-permute-done.1 = bf16[64,1024]{1,0:T(8,128)(2,1)S(1)} collective-permute-done((bf16[64,1024]{1,0:T(8,128)(2,1)}, bf16[64,1024]{1,0:T(8,128)(2,1)S(1)}, u32[]{:S(2)}, u32[]{:S(2)}) %collective-permute-start.1) | collective-permute-done | bytes 131104 | tf_op jit(solution)/shard_map/ppermute | solution.py:127
  17.8 1.6 %collective-permute-start.3 = (bf16[256,1024]{1,0:T(8,128)(2,1)S(1)}, bf16[256,1024]{1,0:T(8,128)(2,1)S(1)}, u32[]{:S(2)}, u32[]{:S(2)}) collective-permute-start(bf16[256,1024]{1,0:T(8,128)(2,1)S(1)} %pad_maximum_fusion.refs_0_), channel_id=1, source_target_pairs={{0,2},{2,0},{4,6},{6,4},{8,10},{10,8},{12,14},{14,12},{16,18},{18,... | collective-permute-start | bytes 1572872 | tf_op jit(solution)/shard_map/ppermute | solution.py:127
  19.4 1.5 %collective-permute-start.4 = (bf16[256,1024]{1,0:T(8,128)(2,1)S(1)}, bf16[256,1024]{1,0:T(8,128)(2,1)S(1)}, u32[]{:S(2)}, u32[]{:S(2)}) collective-permute-start(bf16[256,1024]{1,0:T(8,128)(2,1)S(1)} %pad_maximum_fusion.refs_0_), channel_id=1, source_target_pairs={{0,4},{2,6},{4,0},{6,2},{8,12},{10,14},{12,8},{14,10},{16,20},{18,... | collective-permute-start | bytes 1572872 | tf_op jit(solution)/shard_map/ppermute | solution.py:127
  21.7 2.1 %multiply_reduce_fusion = f32[1024]{0:T(1024)S(1)} fusion(bf16[1024,1024]{1,0:T(8,128)(2,1)} %refs_2_.3), kind=kLoop, calls=%fused_computation | loop fusion | flops 3144704 | bytes 2101248 | tf_op jit(solution)/shard_map/reduce_sum | solution.py:153
  23.8 5.3 %collective-permute-done.3.refs_0_ = bf16[256,1024]{1,0:T(8,128)(2,1)S(1)} collective-permute-done((bf16[256,1024]{1,0:T(8,128)(2,1)S(1)}, bf16[256,1024]{1,0:T(8,128)(2,1)S(1)}, u32[]{:S(2)}, u32[]{:S(2)}) %collective-permute-start.3) | collective-permute-done | bytes 524320 | tf_op jit(solution)/shard_map/ppermute | solution.py:127
  29.9 1.5 %collective-permute-start.5 = (bf16[128,1024]{1,0:T(8,128)(2,1)}, bf16[128,1024]{1,0:T(8,128)(2,1)S(1)}, u32[]{:S(2)}, u32[]{:S(2)}) collective-permute-start(bf16[128,1024]{1,0:T(8,128)(2,1)} %slice.8), channel_id=1, source_target_pairs={{0,4},{2,6},{4,0},{6,2},{8,12},{10,14},{12,8},{14,10},{16,20},{18,... | collective-permute-start | bytes 786440 | tf_op jit(solution)/shard_map/ppermute | solution.py:127
  37.1 1.9 %score.4.refs_1_ = f32[512,1024]{1,0:T(8,128)S(1)} custom-call(s32[1]{0:T(128)} %bitcast.me_ref, s32[4,2]{1,0:T(4,128)S(1)} %copy.6.list_ref, s32[1]{0:T(128)} %bitcast.10.count_ref, bf16[256,1024]{1,0:T(8,128)(2,1)S(1)} %copy-done.7, bf16[256,1024]{1,0:T(8,128)(2,1)S(1)} %copy-done.9, bf16[1024,1024]{1,0:T(8,128)(2,1)S(1)} %copy-done.3), custom_call_target="tpu_custom_call" | custom-call | flops 1073741824 | bytes 5242880 | tf_op jit(solution)/shard_map/score/pallas_call | solution.py:103
  39.0 2.5 %score.5.refs_2_ = f32[256,1024]{1,0:T(8,128)S(1)} custom-call(s32[1]{0:T(128)} %bitcast.me_ref, s32[4,2]{1,0:T(4,128)S(1)} %copy.6.list_ref, s32[1]{0:T(128)} %bitcast.11.count_ref, bf16[128,1024]{1,0:T(8,128)(2,1)S(1)} %collective-permute-done.5.refs_0_, bf16[128,1024]{1,0:T(8,128)(2,1)} %collective-permute-done.6.refs_1_, bf16[1024,1024]{1,0:T(8,128)(2,1)S(1)} %copy-done.3), custom_call_target="tpu_custom_call" | custom-call | flops 536870912 | bytes 3670016 | tf_op jit(solution)/shard_map/score/pallas_call | solution.py:103
  42.6 1.5 %collective-permute-start.7 = (f32[16,64]{1,0:T(8,128)S(1)}, f32[16,64]{1,0:T(8,128)S(1)}, u32[]{:S(2)}, u32[]{:S(2)}) collective-permute-start(f32[16,64]{1,0:T(8,128)S(1)} %rows.3), channel_id=1, source_target_pairs={{0,2},{2,0},{4,6},{6,4},{8,10},{10,8},{12,14},{14,12},{16,18},{18,... | collective-permute-start | bytes 12296 | tf_op jit(solution)/shard_map/ppermute | solution.py:127
  49.3 3.0 %collective-permute-start.10 = (f32[16,64]{1,0:T(8,128)S(1)}, f32[16,64]{1,0:T(8,128)S(1)}, u32[]{:S(2)}, u32[]{:S(2)}) collective-permute-start(f32[16,64]{1,0:T(8,128)S(1)} %multiply_add_fusion.2), channel_id=1, source_target_pairs={{0,8},{2,10},{4,12},{6,14},{8,0},{10,2},{12,4},{14,6},{16,24},{18,... | collective-permute-start | bytes 12296 | tf_op jit(solution)/shard_map/ppermute | solution.py:127
  52.3 1.5 %collective-permute-start.11 = (f32[16,64]{1,0:T(8,128)S(1)}, f32[16,64]{1,0:T(8,128)S(1)}, u32[]{:S(2)}, u32[]{:S(2)}) collective-permute-start(f32[16,64]{1,0:T(8,128)S(1)} %multiply_add_fusion.2), channel_id=1, source_target_pairs={{0,16},{2,18},{4,20},{6,22},{8,24},{10,26},{12,28},{14,30},{16,0},... | collective-permute-start | bytes 12296 | tf_op jit(solution)/shard_map/ppermute | solution.py:127
  55.2 1.6 %collective-permute-done.11 = f32[16,64]{1,0:T(8,128)S(1)} collective-permute-done((f32[16,64]{1,0:T(8,128)S(1)}, f32[16,64]{1,0:T(8,128)S(1)}, u32[]{:S(2)}, u32[]{:S(2)}) %collective-permute-start.11) | collective-permute-done | bytes 4128 | tf_op jit(solution)/shard_map/ppermute | solution.py:127
  56.9 2.4 %collective-permute-done.12 = f32[16,64]{1,0:T(8,128)S(1)} collective-permute-done((f32[16,64]{1,0:T(8,128)S(1)}, f32[16,64]{1,0:T(8,128)S(1)}, u32[]{:S(2)}, u32[]{:S(2)}) %collective-permute-start.12) | collective-permute-done | bytes 4128 | tf_op jit(solution)/shard_map/ppermute | solution.py:127
  63.4 1.5 %collective-permute-start.15 = (f32[16,64]{1,0:T(8,128)S(1)}, f32[16,64]{1,0:T(8,128)S(1)}, u32[]{:S(2)}, u32[]{:S(2)}) collective-permute-start(f32[16,64]{1,0:T(8,128)S(1)} %rows.4), channel_id=1, source_target_pairs={{0,4},{2,6},{4,0},{6,2},{8,12},{10,14},{12,8},{14,10},{16,20},{18,... | collective-permute-start | bytes 12296 | tf_op jit(solution)/shard_map/ppermute | solution.py:127
  67.0 2.4 %collective-permute-done.16 = f32[16,64]{1,0:T(8,128)S(1)} collective-permute-done((f32[16,64]{1,0:T(8,128)S(1)}, f32[16,64]{1,0:T(8,128)S(1)}, u32[]{:S(2)}, u32[]{:S(2)}) %collective-permute-start.16) | collective-permute-done | bytes 4128 | tf_op jit(solution)/shard_map/ppermute | solution.py:127
  69.7 1.8 %collective-permute-start.18 = (f32[16,64]{1,0:T(8,128)S(1)}, f32[16,64]{1,0:T(8,128)S(1)}, u32[]{:S(2)}, u32[]{:S(2)}) collective-permute-start(f32[16,64]{1,0:T(8,128)S(1)} %multiply_add_fusion.1), channel_id=1, source_target_pairs={{0,16},{2,18},{4,20},{6,22},{8,24},{10,26},{12,28},{14,30},{16,0},... | collective-permute-start | bytes 12296 | tf_op jit(solution)/shard_map/ppermute | solution.py:127
  71.5 2.4 %collective-permute-start.19 = (f32[16,64]{1,0:T(8,128)S(1)}, f32[16,64]{1,0:T(8,128)S(1)}, u32[]{:S(2)}, u32[]{:S(2)}) collective-permute-start(f32[16,64]{1,0:T(8,128)S(1)} %multiply_add_fusion.1), channel_id=1, source_target_pairs={{0,24},{2,26},{4,28},{6,30},{8,16},{10,18},{12,20},{14,22},{16,8},... | collective-permute-start | bytes 12296 | tf_op jit(solution)/shard_map/ppermute | solution.py:127
  74.2 2.7 %collective-permute-done.19 = f32[16,64]{1,0:T(8,128)S(1)} collective-permute-done((f32[16,64]{1,0:T(8,128)S(1)}, f32[16,64]{1,0:T(8,128)S(1)}, u32[]{:S(2)}, u32[]{:S(2)}) %collective-permute-start.19) | collective-permute-done | bytes 4128 | tf_op jit(solution)/shard_map/ppermute | solution.py:127
  80.4 1.6 %collective-permute-start.21 = (f32[16,64]{1,0:T(8,128)S(1)}, f32[16,64]{1,0:T(8,128)S(1)}, u32[]{:S(2)}, u32[]{:S(2)}) collective-permute-start(f32[16,64]{1,0:T(8,128)S(1)} %rows.5), channel_id=1, source_target_pairs={{0,2},{2,0},{4,6},{6,4},{8,10},{10,8},{12,14},{14,12},{16,18},{18,... | collective-permute-start | bytes 12296 | tf_op jit(solution)/shard_map/ppermute | solution.py:127
  87.1 3.0 %collective-permute-start.25 = (f32[16,64]{1,0:T(8,128)S(1)}, f32[16,64]{1,0:T(8,128)S(1)}, u32[]{:S(2)}, u32[]{:S(2)}) collective-permute-start(f32[16,64]{1,0:T(8,128)S(1)} %multiply_add_fusion), channel_id=1, source_target_pairs={{0,16},{2,18},{4,20},{6,22},{8,24},{10,26},{12,28},{14,30},{16,0},... | collective-permute-start | bytes 12296 | tf_op jit(solution)/shard_map/ppermute | solution.py:127
  91.7 3.8 %collective-permute-done.26 = f32[16,64]{1,0:T(8,128)S(1)} collective-permute-done((f32[16,64]{1,0:T(8,128)S(1)}, f32[16,64]{1,0:T(8,128)S(1)}, u32[]{:S(2)}, u32[]{:S(2)}) %collective-permute-start.26) | collective-permute-done | bytes 4128 | tf_op jit(solution)/shard_map/ppermute | solution.py:127
  (83 shorter events, 36.1 us)
Async XLA Ops:
  0.7 8.3 %collective-permute-start = (bf16[64,1024]{1,0:T(8,128)(2,1)}, bf16[64,1024]{1,0:T(8,128)(2,1)S(1)}, u32[]{:S(2)}, u32[]{:S(2)}) collective-permute-start(bf16[64,1024]{1,0:T(8,128)(2,1)} %bitcast.13), channel_id=1, source_target_pairs={{0,8},{2,10},{4,12},{6,14},{8,0},{10,2},{12,4},{14,6},{16,24},{18,... | collective-permute-start | bytes 393224 | tf_op jit(solution)/shard_map/ppermute | solution.py:127
  3.7 13.2 %collective-permute-start.1 = (bf16[64,1024]{1,0:T(8,128)(2,1)}, bf16[64,1024]{1,0:T(8,128)(2,1)S(1)}, u32[]{:S(2)}, u32[]{:S(2)}) collective-permute-start(bf16[64,1024]{1,0:T(8,128)(2,1)} %bitcast.14), channel_id=1, source_target_pairs={{0,16},{2,18},{4,20},{6,22},{8,24},{10,26},{12,28},{14,30},{16,0},... | collective-permute-start | bytes 393224 | tf_op jit(solution)/shard_map/ppermute | solution.py:127
  6.3 10.6 %collective-permute-start.2 = (bf16[64,1024]{1,0:T(8,128)(2,1)}, bf16[64,1024]{1,0:T(8,128)(2,1)S(1)}, u32[]{:S(2)}, u32[]{:S(2)}) collective-permute-start(bf16[64,1024]{1,0:T(8,128)(2,1)} %bitcast.15), channel_id=1, source_target_pairs={{0,24},{2,26},{4,28},{6,30},{8,16},{10,18},{12,20},{14,22},{16,8},... | collective-permute-start | bytes 393224 | tf_op jit(solution)/shard_map/ppermute | solution.py:127
  17.8 11.3 %collective-permute-start.3 = (bf16[256,1024]{1,0:T(8,128)(2,1)S(1)}, bf16[256,1024]{1,0:T(8,128)(2,1)S(1)}, u32[]{:S(2)}, u32[]{:S(2)}) collective-permute-start(bf16[256,1024]{1,0:T(8,128)(2,1)S(1)} %pad_maximum_fusion.refs_0_), channel_id=1, source_target_pairs={{0,2},{2,0},{4,6},{6,4},{8,10},{10,8},{12,14},{14,12},{16,18},{18,... | collective-permute-start | bytes 1572872 | tf_op jit(solution)/shard_map/ppermute | solution.py:127
  19.4 12.0 %collective-permute-start.4 = (bf16[256,1024]{1,0:T(8,128)(2,1)S(1)}, bf16[256,1024]{1,0:T(8,128)(2,1)S(1)}, u32[]{:S(2)}, u32[]{:S(2)}) collective-permute-start(bf16[256,1024]{1,0:T(8,128)(2,1)S(1)} %pad_maximum_fusion.refs_0_), channel_id=1, source_target_pairs={{0,4},{2,6},{4,0},{6,2},{8,12},{10,14},{12,8},{14,10},{16,20},{18,... | collective-permute-start | bytes 1572872 | tf_op jit(solution)/shard_map/ppermute | solution.py:127
  29.9 9.1 %collective-permute-start.5 = (bf16[128,1024]{1,0:T(8,128)(2,1)}, bf16[128,1024]{1,0:T(8,128)(2,1)S(1)}, u32[]{:S(2)}, u32[]{:S(2)}) collective-permute-start(bf16[128,1024]{1,0:T(8,128)(2,1)} %slice.8), channel_id=1, source_target_pairs={{0,4},{2,6},{4,0},{6,2},{8,12},{10,14},{12,8},{14,10},{16,20},{18,... | collective-permute-start | bytes 786440 | tf_op jit(solution)/shard_map/ppermute | solution.py:127
  32.3 6.7 %collective-permute-start.6 = (bf16[128,1024]{1,0:T(8,128)(2,1)}, bf16[128,1024]{1,0:T(8,128)(2,1)}, u32[]{:S(2)}, u32[]{:S(2)}) collective-permute-start(bf16[128,1024]{1,0:T(8,128)(2,1)} %slice.9), channel_id=1, source_target_pairs={{0,2},{2,0},{4,6},{6,4},{8,10},{10,8},{12,14},{14,12},{16,18},{18,... | collective-permute-start | bytes 786440 | tf_op jit(solution)/shard_map/ppermute | solution.py:127
  42.6 3.7 %collective-permute-start.7 = (f32[16,64]{1,0:T(8,128)S(1)}, f32[16,64]{1,0:T(8,128)S(1)}, u32[]{:S(2)}, u32[]{:S(2)}) collective-permute-start(f32[16,64]{1,0:T(8,128)S(1)} %rows.3), channel_id=1, source_target_pairs={{0,2},{2,0},{4,6},{6,4},{8,10},{10,8},{12,14},{14,12},{16,18},{18,... | collective-permute-start | bytes 12296 | tf_op jit(solution)/shard_map/ppermute | solution.py:127
  44.7 4.5 %collective-permute-start.9 = (f32[16,64]{1,0:T(8,128)S(1)}, f32[16,64]{1,0:T(8,128)S(1)}, u32[]{:S(2)}, u32[]{:S(2)}) collective-permute-start(f32[16,64]{1,0:T(8,128)S(1)} %rows.3), channel_id=1, source_target_pairs={{0,6},{2,4},{4,2},{6,0},{8,14},{10,12},{12,10},{14,8},{16,22},{18,... | collective-permute-start | bytes 12296 | tf_op jit(solution)/shard_map/ppermute | solution.py:127
  49.3 5.9 %collective-permute-start.10 = (f32[16,64]{1,0:T(8,128)S(1)}, f32[16,64]{1,0:T(8,128)S(1)}, u32[]{:S(2)}, u32[]{:S(2)}) collective-permute-start(f32[16,64]{1,0:T(8,128)S(1)} %multiply_add_fusion.2), channel_id=1, source_target_pairs={{0,8},{2,10},{4,12},{6,14},{8,0},{10,2},{12,4},{14,6},{16,24},{18,... | collective-permute-start | bytes 12296 | tf_op jit(solution)/shard_map/ppermute | solution.py:127
  52.3 4.5 %collective-permute-start.11 = (f32[16,64]{1,0:T(8,128)S(1)}, f32[16,64]{1,0:T(8,128)S(1)}, u32[]{:S(2)}, u32[]{:S(2)}) collective-permute-start(f32[16,64]{1,0:T(8,128)S(1)} %multiply_add_fusion.2), channel_id=1, source_target_pairs={{0,16},{2,18},{4,20},{6,22},{8,24},{10,26},{12,28},{14,30},{16,0},... | collective-permute-start | bytes 12296 | tf_op jit(solution)/shard_map/ppermute | solution.py:127
  53.9 5.4 %collective-permute-start.12 = (f32[16,64]{1,0:T(8,128)S(1)}, f32[16,64]{1,0:T(8,128)S(1)}, u32[]{:S(2)}, u32[]{:S(2)}) collective-permute-start(f32[16,64]{1,0:T(8,128)S(1)} %multiply_add_fusion.2), channel_id=1, source_target_pairs={{0,24},{2,26},{4,28},{6,30},{8,16},{10,18},{12,20},{14,22},{16,8},... | collective-permute-start | bytes 12296 | tf_op jit(solution)/shard_map/ppermute | solution.py:127
  62.8 3.7 %collective-permute-start.14 = (f32[16,64]{1,0:T(8,128)S(1)}, f32[16,64]{1,0:T(8,128)S(1)}, u32[]{:S(2)}, u32[]{:S(2)}) collective-permute-start(f32[16,64]{1,0:T(8,128)S(1)} %rows.4), channel_id=1, source_target_pairs={{0,2},{2,0},{4,6},{6,4},{8,10},{10,8},{12,14},{14,12},{16,18},{18,... | collective-permute-start | bytes 12296 | tf_op jit(solution)/shard_map/ppermute | solution.py:127
  63.4 3.7 %collective-permute-start.15 = (f32[16,64]{1,0:T(8,128)S(1)}, f32[16,64]{1,0:T(8,128)S(1)}, u32[]{:S(2)}, u32[]{:S(2)}) collective-permute-start(f32[16,64]{1,0:T(8,128)S(1)} %rows.4), channel_id=1, source_target_pairs={{0,4},{2,6},{4,0},{6,2},{8,12},{10,14},{12,8},{14,10},{16,20},{18,... | collective-permute-start | bytes 12296 | tf_op jit(solution)/shard_map/ppermute | solution.py:127
  64.9 4.5 %collective-permute-start.16 = (f32[16,64]{1,0:T(8,128)S(1)}, f32[16,64]{1,0:T(8,128)S(1)}, u32[]{:S(2)}, u32[]{:S(2)}) collective-permute-start(f32[16,64]{1,0:T(8,128)S(1)} %rows.4), channel_id=1, source_target_pairs={{0,6},{2,4},{4,2},{6,0},{8,14},{10,12},{12,10},{14,8},{16,22},{18,... | collective-permute-start | bytes 12296 | tf_op jit(solution)/shard_map/ppermute | solution.py:127
  69.5 4.5 %collective-permute-start.17 = (f32[16,64]{1,0:T(8,128)S(1)}, f32[16,64]{1,0:T(8,128)S(1)}, u32[]{:S(2)}, u32[]{:S(2)}) collective-permute-start(f32[16,64]{1,0:T(8,128)S(1)} %multiply_add_fusion.1), channel_id=1, source_target_pairs={{0,8},{2,10},{4,12},{6,14},{8,0},{10,2},{12,4},{14,6},{16,24},{18,... | collective-permute-start | bytes 12296 | tf_op jit(solution)/shard_map/ppermute | solution.py:127
  69.7 4.5 %collective-permute-start.18 = (f32[16,64]{1,0:T(8,128)S(1)}, f32[16,64]{1,0:T(8,128)S(1)}, u32[]{:S(2)}, u32[]{:S(2)}) collective-permute-start(f32[16,64]{1,0:T(8,128)S(1)} %multiply_add_fusion.1), channel_id=1, source_target_pairs={{0,16},{2,18},{4,20},{6,22},{8,24},{10,26},{12,28},{14,30},{16,0},... | collective-permute-start | bytes 12296 | tf_op jit(solution)/shard_map/ppermute | solution.py:127
  71.5 5.4 %collective-permute-start.19 = (f32[16,64]{1,0:T(8,128)S(1)}, f32[16,64]{1,0:T(8,128)S(1)}, u32[]{:S(2)}, u32[]{:S(2)}) collective-permute-start(f32[16,64]{1,0:T(8,128)S(1)} %multiply_add_fusion.1), channel_id=1, source_target_pairs={{0,24},{2,26},{4,28},{6,30},{8,16},{10,18},{12,20},{14,22},{16,8},... | collective-permute-start | bytes 12296 | tf_op jit(solution)/shard_map/ppermute | solution.py:127
  80.4 3.7 %collective-permute-start.21 = (f32[16,64]{1,0:T(8,128)S(1)}, f32[16,64]{1,0:T(8,128)S(1)}, u32[]{:S(2)}, u32[]{:S(2)}) collective-permute-start(f32[16,64]{1,0:T(8,128)S(1)} %rows.5), channel_id=1, source_target_pairs={{0,2},{2,0},{4,6},{6,4},{8,10},{10,8},{12,14},{14,12},{16,18},{18,... | collective-permute-start | bytes 12296 | tf_op jit(solution)/shard_map/ppermute | solution.py:127
  81.9 3.7 %collective-permute-start.22 = (f32[16,64]{1,0:T(8,128)S(1)}, f32[16,64]{1,0:T(8,128)S(1)}, u32[]{:S(2)}, u32[]{:S(2)}) collective-permute-start(f32[16,64]{1,0:T(8,128)S(1)} %rows.5), channel_id=1, source_target_pairs={{0,4},{2,6},{4,0},{6,2},{8,12},{10,14},{12,8},{14,10},{16,20},{18,... | collective-permute-start | bytes 12296 | tf_op jit(solution)/shard_map/ppermute | solution.py:127
  82.5 4.5 %collective-permute-start.23 = (f32[16,64]{1,0:T(8,128)S(1)}, f32[16,64]{1,0:T(8,128)S(1)}, u32[]{:S(2)}, u32[]{:S(2)}) collective-permute-start(f32[16,64]{1,0:T(8,128)S(1)} %rows.5), channel_id=1, source_target_pairs={{0,6},{2,4},{4,2},{6,0},{8,14},{10,12},{12,10},{14,8},{16,22},{18,... | collective-permute-start | bytes 12296 | tf_op jit(solution)/shard_map/ppermute | solution.py:127
  87.0 4.6 %collective-permute-start.24 = (f32[16,64]{1,0:T(8,128)S(1)}, f32[16,64]{1,0:T(8,128)S(1)}, u32[]{:S(2)}, u32[]{:S(2)}) collective-permute-start(f32[16,64]{1,0:T(8,128)S(1)} %multiply_add_fusion), channel_id=1, source_target_pairs={{0,8},{2,10},{4,12},{6,14},{8,0},{10,2},{12,4},{14,6},{16,24},{18,... | collective-permute-start | bytes 12296 | tf_op jit(solution)/shard_map/ppermute | solution.py:127
  87.1 4.6 %collective-permute-start.25 = (f32[16,64]{1,0:T(8,128)S(1)}, f32[16,64]{1,0:T(8,128)S(1)}, u32[]{:S(2)}, u32[]{:S(2)}) collective-permute-start(f32[16,64]{1,0:T(8,128)S(1)} %multiply_add_fusion), channel_id=1, source_target_pairs={{0,16},{2,18},{4,20},{6,22},{8,24},{10,26},{12,28},{14,30},{16,0},... | collective-permute-start | bytes 12296 | tf_op jit(solution)/shard_map/ppermute | solution.py:127
  90.1 5.4 %collective-permute-start.26 = (f32[16,64]{1,0:T(8,128)S(1)}, f32[16,64]{1,0:T(8,128)S(1)}, u32[]{:S(2)}, u32[]{:S(2)}) collective-permute-start(f32[16,64]{1,0:T(8,128)S(1)} %multiply_add_fusion), channel_id=1, source_target_pairs={{0,24},{2,26},{4,28},{6,30},{8,16},{10,18},{12,20},{14,22},{16,8},... | collective-permute-start | bytes 12296 | tf_op jit(solution)/shard_map/ppermute | solution.py:127
  (16 other events, 136.7 us)

commit v2 on v1

--- a/solution.py
+++ b/solution.py
@@ -16,6 +16,7 @@
 EPS = 0.02
 NEG = -1e30
 LN2 = math.log(2.0)
+LANES = 128
 VMEM_LIMIT = 32 * 1024 * 1024
 
 
@@ -57,29 +58,41 @@
 
 
 def row_kernel(rels, own_rows, me_ref, shift_ref, *refs):
-    out_ref = refs[-1]
+    out_ref, held_ref = refs[-2:]
     me = me_ref[0]
     shift = shift_ref[...]
     eye = diagonal(own_rows)
-    for ref, rel in zip(refs[:-1], rels):
+    for ref, rel in zip(refs[:-2], rels):
         for part, source in enumerate(rel):
             block = ref[part * own_rows : (part + 1) * own_rows, :] + shift
             peak = jnp.max(block, axis=1, keepdims=True)
             total = jnp.sum(jnp.exp2(block - peak), axis=1, keepdims=True)
             column = peak + jnp.log(total) * (1.0 / LN2)
             row = jnp.sum(jnp.where(eye, column, 0.0), axis=0, keepdims=True)
-            out_ref[pl.ds(me ^ source, 1), :] = row
-
-
-def column_kernel(rels, own_rows, me_ref, shift_ref, *refs):
-    out_ref = refs[-1]
+            held_ref[pl.ds(me ^ source, 1), :] = row
+    across = out_ref.shape[2] // own_rows
+    for line in range(out_ref.shape[1]):
+        sources = [held_ref[line * across + k : line * across + k + 1, :] for k in range(across)]
+        wide = jnp.concatenate(sources, axis=1)
+        out_ref[:, line, :] = jnp.broadcast_to(wide, (out_ref.shape[0], out_ref.shape[2]))
+
+
+def column_kernel(rels, own_rows, log_a, me_ref, value_ref, *refs):
+    out_ref, held_ref = refs[-2:]
     me = me_ref[0]
+    shift = log_a - log2_sum([value_ref[k] for k in range(value_ref.shape[0])])
+    across = shift.shape[1] // own_rows
+    for source in range(held_ref.shape[0]):
+        line, place = source // across, source % across
+        held_ref[source : source + 1, :] = shift[
+            line : line + 1, place * own_rows : (place + 1) * own_rows
+        ]
     eye = diagonal(own_rows)
     columns = []
     peak = None
-    for ref, rel in zip(refs[:-1], rels):
+    for ref, rel in zip(refs[:-2], rels):
         for part, source in enumerate(rel):
-            row = shift_ref[pl.ds(me ^ source, 1), :]
+            row = held_ref[pl.ds(me ^ source, 1), :]
             column = jnp.sum(jnp.where(eye, row, 0.0), axis=1, keepdims=True)
             columns.append(column)
             block = ref[part * own_rows : (part + 1) * own_rows, :] + column
@@ -87,7 +100,7 @@
             peak = high if peak is None else jnp.maximum(peak, high)
     peak = jnp.max(peak, axis=0, keepdims=True)
     total = jnp.zeros((8, peak.shape[1]), jnp.float32)
-    for ref, rel in zip(refs[:-1], rels):
+    for ref, rel in zip(refs[:-2], rels):
         for part, source in enumerate(rel):
             column = columns.pop(0)
             block = ref[part * own_rows : (part + 1) * own_rows, :] + (column - peak)
@@ -96,15 +109,16 @@
     out_ref[...] = peak + jnp.log(total) * (1.0 / LN2)
 
 
-def call(kernel, out_shape, scalars, arrays, flops, name):
+def call(kernel, shapes, scratch, scalars, arrays, flops, name):
     smem = pl.BlockSpec(memory_space=pltpu.SMEM)
     vmem = pl.BlockSpec(memory_space=pltpu.VMEM)
-    moved = sum(a.size * a.dtype.itemsize for a in arrays) + 4 * math.prod(out_shape)
+    moved = sum(a.size * a.dtype.itemsize for a in arrays) + 4 * sum(map(math.prod, shapes))
     return pl.pallas_call(
         kernel,
-        out_shape=jax.ShapeDtypeStruct(out_shape, jnp.float32),
+        out_shape=[jax.ShapeDtypeStruct(s, jnp.float32) for s in shapes],
         in_specs=[smem] * len(scalars) + [vmem] * len(arrays),
-        out_specs=vmem,
+        out_specs=[vmem] * len(shapes),
+        scratch_shapes=scratch,
         compiler_params=pltpu.CompilerParams(vmem_limit_bytes=VMEM_LIMIT),
         cost_estimate=pl.CostEstimate(flops=flops, bytes_accessed=moved, transcendentals=0),
         name=name,
@@ -131,7 +145,7 @@
         shape = (len(rel) * own_rows, pool_rows)
         flops = 2 * shape[0] * pool_rows * width
         kernel = functools.partial(score_kernel, rel, 2.0 / (width * unit), own_rows)
-        return call(kernel, shape, scalars, pieces + [pool], flops, "score"), rel
+        return call(kernel, [shape], [], scalars, pieces + [pool], flops, "score")[0], rel
 
     outer = tuple(range(0, size, 4))
     plane = jnp.concatenate([own] + [swap(own, m) for m in outer[1:]], axis=0)
@@ -139,34 +153,42 @@
     first, second = outer[: size // 8], outer[size // 8 :]
     by_x = swap(plane, 1)
     by_y = swap(plane, 2)
+    center = score([plane], [outer])
+    by_x, by_y, center_score = lax.optimization_barrier((by_x, by_y, center[0]))
     low = swap(by_x[:half], 2)
     high = swap(by_y[half:], 1)
-    parts = [
-        score([plane], [outer]),
-        score([by_x, by_y], [tuple(m ^ 1 for m in outer), tuple(m ^ 2 for m in outer)]),
-        score([low, high], [tuple(m ^ 3 for m in first), tuple(m ^ 3 for m in second)]),
-    ]
+    sides = score([by_x, by_y], [tuple(m ^ 1 for m in outer), tuple(m ^ 2 for m in outer)])
+    low, high, sides_score = lax.optimization_barrier((low, high, sides[0]))
+    corner = score([low, high], [tuple(m ^ 3 for m in first), tuple(m ^ 3 for m in second)])
+    parts = [(center_score, center[1]), (sides_score, sides[1]), corner]
     scores = [p[0] for p in parts]
     rels = [p[1] for p in parts]
 
     own_norm = jnp.sum(jnp.square(own.astype(jnp.float32)), axis=1) / width
     pool_norm = jnp.sum(jnp.square(pool.astype(jnp.float32)), axis=1) / width
     shift = pool_norm.reshape(1, pool_rows) * (-1.0 / unit)
+    lines = half_rows // LANES
+    held = [pltpu.VMEM((size, own_rows), jnp.float32)]
     flops = 8 * half_rows * pool_rows
     for _ in range(ITERS):
         kernel = functools.partial(row_kernel, rels, own_rows)
-        value = call(kernel, (size, own_rows), [me], [shift] + scores, flops, "rows")
-        step = 1
-        while step < size:
-            masks = [m * step for m in range(1, min(4, size // step))]
-            value = log2_sum([value] + [swap(value, m) for m in masks])
-            step *= 4
-        sample_shift = log_a - value
-        kernel = functools.partial(column_kernel, rels, own_rows)
-        value = call(kernel, (1, pool_rows), [me], [sample_shift] + scores, flops, "columns")
+        (value,) = call(
+            kernel, [(size, lines, LANES)], held, [me], [shift] + scores, flops, "rows"
+        )
+        value = lax.all_to_all(value, "pool", 0, 0, tiled=True)
+        kernel = functools.partial(column_kernel, rels, own_rows, log_a)
+        value, potential = call(
+            kernel,
+            [(1, pool_rows), (size, own_rows)],
+            [],
+            [me],
+            [value] + scores,
+            flops,
+            "columns",
+        )
         pairs = [(i, i ^ 1) for i in range(2)]
         shift = log_b - log2_sum([value, lax.ppermute(value, "samp", pairs)])
-    mine = lax.dynamic_slice_in_dim(sample_shift, me[0], 1, 0)
+    mine = lax.dynamic_slice_in_dim(potential, me[0], 1, 0)
     return mine * unit + own_norm[None, :], shift.reshape(pool_rows) * unit + pool_norm
 
 

time: 100 us -> 91.4 us (0.914)
  blocking collectives: 0 us -> 23.3 us
  starting transfers between devices: 37.4 us -> 14.6 us
  waiting for transfers between devices: 39.2 us -> 28.5 us
  Pallas kernels: 12.1 us -> 14.1 us
    ppermute x25 -> x7, starting transfers between devices: 37.2 us -> 10.8 us  [swap(): return lax.ppermute(value, 'pool', [(i, i ^ mask) for i in range(size)])]
    all_to_all x0 -> x2, blocking collectives: none -> 23.3 us  [body(): value = lax.all_to_all(value, 'pool', 0, 0, tiled=True)]
    ppermute x25 -> x7, waiting for transfers between devices: 36.2 us -> 18.2 us  [swap(): return lax.ppermute(value, 'pool', [(i, i ^ mask) for i in range(size)])]
    all_to_all x0 -> x1, waiting for transfers between devices: none -> 7.36 us  [body(): value = lax.all_to_all(value, 'pool', 0, 0, tiled=True)]
    all_to_all x0 -> x1, starting transfers between devices: none -> 3.5 us  [body(): value = lax.all_to_all(value, 'pool', 0, 0, tiled=True)]
    pallas_call x9, Pallas kernels: 12.1 us -> 14.1 us  [call(): pl.pallas_call(kernel, out_shape=[jax.ShapeDtypeStruct(s, jnp.float32) fo...]
    unnamed x24 -> x10, local copies, waits for them, and re-layouts: 3.19 us -> 1.25 us
  transfers between devices with their start and end apart: 28 -> 11, of which waited for: 22 -> 10; matrix products, arithmetic and copies ran while one was open for 4% -> 5% of each run, Pallas kernels for 3% -> 5%
where the time goes in v2:
time: 91.4 us; the launch traced here: 91 us
  waiting for transfers between devices  28.5 us (31%)
  blocking collectives  23.3 us (25%)
  starting transfers between devices  14.6 us (16%)
  Pallas kernels  14.1 us (15%)
  other arithmetic  5.15 us (6%)
  local copies, waits for them, and re-layouts  3.95 us (4%)
  between operations  1.46 us (2%)
    all_to_all x2, blocking collectives, body(): value = lax.all_to_all(value, 'pool', 0, 0, tiled=True)  23.3 us
    ppermute x7, waiting for transfers between devices, swap(): return lax.ppermute(value, 'pool', [(i, i ^ mask) for i in range(size)])  18.2 us
    pallas_call x9, Pallas kernels, call(): pl.pallas_call(kernel, out_shape=[jax.ShapeDtypeStruct(s, jnp.float32) fo...  14.1 us
    ppermute x7, starting transfers between devices, swap(): return lax.ppermute(value, 'pool', [(i, i ^ mask) for i in range(size)])  10.8 us
    all_to_all x1, waiting for transfers between devices, body(): value = lax.all_to_all(value, 'pool', 0, 0, tiled=True)  7.36 us
    all_to_all x1, starting transfers between devices, body(): value = lax.all_to_all(value, 'pool', 0, 0, tiled=True)  3.5 us
    ppermute x3, waiting for transfers between devices, body(): shift = log_b - log2_sum([value, lax.ppermute(value, 'samp', pairs)])  2.93 us
    reduce_sum x1, other arithmetic, body(): pool_norm = jnp.sum(jnp.square(pool.astype(jnp.float32)), axis=1) / width  2.07 us
  transfers between devices with their start and end apart: 11, of which 10 were waited for; matrix products, arithmetic and copies ran while one was open for 5% of the time, Pallas kernels for 5%

profile of v2, /device:TPU:0, one launch (start us, length us, event | category | flops | bytes accessed | tf_op | source)
XLA Modules:
  0.0 91.0 jit_solution(7864427009328647084)
XLA Ops:
  0.6 3.1 %collective-permute-start = (bf16[64,1024]{1,0:T(8,128)(2,1)}, bf16[64,1024]{1,0:T(8,128)(2,1)S(1)}, u32[]{:S(2)}, u32[]{:S(2)}) collective-permute-start(bf16[64,1024]{1,0:T(8,128)(2,1)} %bitcast.13), channel_id=1, source_target_pairs={{0,8},{2,10},{4,12},{6,14},{8,0},{10,2},{12,4},{14,6},{16,24},{18,... | collective-permute-start | bytes 393224 | tf_op jit(solution)/shard_map/ppermute | solution.py:141
  3.7 2.6 %collective-permute-start.1 = (bf16[64,1024]{1,0:T(8,128)(2,1)}, bf16[64,1024]{1,0:T(8,128)(2,1)S(1)}, u32[]{:S(2)}, u32[]{:S(2)}) collective-permute-start(bf16[64,1024]{1,0:T(8,128)(2,1)} %bitcast.14), channel_id=1, source_target_pairs={{0,16},{2,18},{4,20},{6,22},{8,24},{10,26},{12,28},{14,30},{16,0},... | collective-permute-start | bytes 393224 | tf_op jit(solution)/shard_map/ppermute | solution.py:141
  6.3 2.7 %collective-permute-done = bf16[64,1024]{1,0:T(8,128)(2,1)S(1)} collective-permute-done((bf16[64,1024]{1,0:T(8,128)(2,1)}, bf16[64,1024]{1,0:T(8,128)(2,1)S(1)}, u32[]{:S(2)}, u32[]{:S(2)}) %collective-permute-start) | collective-permute-done | bytes 131104 | tf_op jit(solution)/shard_map/ppermute | solution.py:141
  9.0 7.9 %collective-permute-done.1 = bf16[64,1024]{1,0:T(8,128)(2,1)S(1)} collective-permute-done((bf16[64,1024]{1,0:T(8,128)(2,1)}, bf16[64,1024]{1,0:T(8,128)(2,1)S(1)}, u32[]{:S(2)}, u32[]{:S(2)}) %collective-permute-start.1) | collective-permute-done | bytes 131104 | tf_op jit(solution)/shard_map/ppermute | solution.py:141
  16.9 1.7 %pad_maximum_fusion.refs_0_ = bf16[256,1024]{1,0:T(8,128)(2,1)} fusion(bf16[64,1024]{1,0:T(8,128)(2,1)S(1)} %collective-permute-done.2, bf16[64,1024]{1,0:T(8,128)(2,1)S(1)} %collective-permute-done.1, bf16[64,1024]{1,0:T(8,128)(2,1)S(1)} %collective-permute-done, bf16[64,1024]{1,0:T(8,128)(2,1)} %bitcast.16), kind=kLoop, calls=%fused_computation.1 | loop fusion | flops 2097152 | bytes 1048576 | tf_op jit(solution)/shard_map/concatenate | solution.py:151
  18.6 1.5 %collective-permute-start.3 = (bf16[256,1024]{1,0:T(8,128)(2,1)}, bf16[256,1024]{1,0:T(8,128)(2,1)}, u32[]{:S(2)}, u32[]{:S(2)}) collective-permute-start(bf16[256,1024]{1,0:T(8,128)(2,1)} %pad_maximum_fusion.refs_0_), channel_id=1, source_target_pairs={{0,2},{2,0},{4,6},{6,4},{8,10},{10,8},{12,14},{14,12},{16,18},{18,... | collective-permute-start | bytes 1572872 | tf_op jit(solution)/shard_map/ppermute | solution.py:141
  20.1 1.5 %collective-permute-start.4 = (bf16[256,1024]{1,0:T(8,128)(2,1)}, bf16[256,1024]{1,0:T(8,128)(2,1)}, u32[]{:S(2)}, u32[]{:S(2)}) collective-permute-start(bf16[256,1024]{1,0:T(8,128)(2,1)} %pad_maximum_fusion.refs_0_), channel_id=1, source_target_pairs={{0,4},{2,6},{4,0},{6,2},{8,12},{10,14},{12,8},{14,10},{16,20},{18,... | collective-permute-start | bytes 1572872 | tf_op jit(solution)/shard_map/ppermute | solution.py:141
  23.0 2.1 %multiply_reduce_fusion = f32[1024]{0:T(1024)S(1)} fusion(bf16[1024,1024]{1,0:T(8,128)(2,1)} %refs_2_.3), kind=kLoop, calls=%fused_computation | loop fusion | flops 3144704 | bytes 2101248 | tf_op jit(solution)/shard_map/reduce_sum | solution.py:168
  25.1 1.9 %score.3.refs_0_ = f32[256,1024]{1,0:T(8,128)S(1)} custom-call(s32[1]{0:T(128)} %bitcast.me_ref, s32[4,2]{1,0:T(4,128)S(1)} %copy.6.list_ref, s32[1]{0:T(128)} %bitcast.9.count_ref, bf16[256,1024]{1,0:T(8,128)(2,1)} %pad_maximum_fusion.refs_0_, bf16[1024,1024]{1,0:T(8,128)(2,1)S(1)} %copy-done.2), custom_call_target="tpu_custom_call" | custom-call | flops 536870912 | bytes 3670016 | tf_op jit(solution)/shard_map/score/pallas_call | solution.py:116
  27.1 3.0 %collective-permute-done.3.refs_0_ = bf16[256,1024]{1,0:T(8,128)(2,1)} collective-permute-done((bf16[256,1024]{1,0:T(8,128)(2,1)}, bf16[256,1024]{1,0:T(8,128)(2,1)}, u32[]{:S(2)}, u32[]{:S(2)}) %collective-permute-start.3) | collective-permute-done | bytes 524320 | tf_op jit(solution)/shard_map/ppermute | solution.py:141
  30.1 1.2 %collective-permute-done.4.refs_1_ = bf16[256,1024]{1,0:T(8,128)(2,1)} collective-permute-done((bf16[256,1024]{1,0:T(8,128)(2,1)}, bf16[256,1024]{1,0:T(8,128)(2,1)}, u32[]{:S(2)}, u32[]{:S(2)}) %collective-permute-start.4) | collective-permute-done | bytes 524320 | tf_op jit(solution)/shard_map/ppermute | solution.py:141
  32.3 1.6 %collective-permute-start.5 = (bf16[128,1024]{1,0:T(8,128)(2,1)S(1)}, bf16[128,1024]{1,0:T(8,128)(2,1)S(1)}, u32[]{:S(2)}, u32[]{:S(2)}) collective-permute-start(bf16[128,1024]{1,0:T(8,128)(2,1)S(1)} %slice.6), channel_id=1, source_target_pairs={{0,4},{2,6},{4,0},{6,2},{8,12},{10,14},{12,8},{14,10},{16,20},{18,... | collective-permute-start | bytes 786440 | tf_op jit(solution)/shard_map/ppermute | solution.py:141
  35.5 2.5 %score.4.refs_1_ = f32[512,1024]{1,0:T(8,128)S(1)} custom-call(s32[1]{0:T(128)} %bitcast.me_ref, s32[4,2]{1,0:T(4,128)S(1)} %copy.6.list_ref, s32[1]{0:T(128)} %bitcast.10.count_ref, bf16[256,1024]{1,0:T(8,128)(2,1)} %collective-permute-done.3.refs_0_, bf16[256,1024]{1,0:T(8,128)(2,1)} %collective-permute-done.4.refs_1_, bf16[1024,1024]{1,0:T(8,128)(2,1)S(1)} %copy-done.3), custom_call_target="tpu_custom_call" | custom-call | flops 1073741824 | bytes 5242880 | tf_op jit(solution)/shard_map/score/pallas_call | solution.py:116
  38.8 2.6 %collective-permute-done.6.refs_1_ = bf16[128,1024]{1,0:T(8,128)(2,1)S(1)} collective-permute-done((bf16[128,1024]{1,0:T(8,128)(2,1)S(1)}, bf16[128,1024]{1,0:T(8,128)(2,1)S(1)}, u32[]{:S(2)}, u32[]{:S(2)}) %collective-permute-start.6) | collective-permute-done | bytes 262176 | tf_op jit(solution)/shard_map/ppermute | solution.py:141
  41.3 2.1 %score.5.refs_2_ = f32[256,1024]{1,0:T(8,128)S(1)} custom-call(s32[1]{0:T(128)} %bitcast.me_ref, s32[4,2]{1,0:T(4,128)S(1)} %copy.6.list_ref, s32[1]{0:T(128)} %bitcast.11.count_ref, bf16[128,1024]{1,0:T(8,128)(2,1)S(1)} %collective-permute-done.5.refs_0_, bf16[128,1024]{1,0:T(8,128)(2,1)S(1)} %collective-permute-done.6.refs_1_, bf16[1024,1024]{1,0:T(8,128)(2,1)S(1)} %copy-done.3), custom_call_target="tpu_custom_call" | custom-call | flops 536870912 | bytes 3670016 | tf_op jit(solution)/shard_map/score/pallas_call | solution.py:116
  44.5 13.2 %all_to_all.15.value_ref = f32[16,8,128]{2,1,0:T(8,128)S(1)} all-to-all(f32[16,8,128]{2,1,0:T(8,128)S(1)} %rows.3), channel_id=1, replica_groups=mesh['grp'=1,'pool'=16,'samp'=2] {'pool'}, dimensions={0} | all-to-all | bytes 131072 | tf_op jit(solution)/shard_map/all_to_all | solution.py:178
  57.7 1.2 %columns.3 = (f32[1,1024]{1,0:T(1,128)S(1)}, f32[16,64]{1,0:T(8,128)}) custom-call(s32[1]{0:T(128)} %bitcast.me_ref, f32[16,8,128]{2,1,0:T(8,128)S(1)} %all_to_all.15.value_ref, f32[256,1024]{1,0:T(8,128)S(1)} %score.3.refs_0_, f32[512,1024]{1,0:T(8,128)S(1)} %score.4.refs_1_, f32[256,1024]{1,0:T(8,128)S(1)} %score.5.refs_2_), custom_call_target="tpu_custom_call" | custom-call | flops 8388608 | bytes 4268032 | tf_op jit(solution)/shard_map/columns/pallas_call | solution.py:116
  61.3 10.1 %all_to_all.16.value_ref = f32[16,8,128]{2,1,0:T(8,128)S(1)} all-to-all(f32[16,8,128]{2,1,0:T(8,128)S(1)} %rows.4), channel_id=1, replica_groups=mesh['grp'=1,'pool'=16,'samp'=2] {'pool'}, dimensions={0} | all-to-all | bytes 131072 | tf_op jit(solution)/shard_map/all_to_all | solution.py:178
  71.4 1.2 %columns.4 = (f32[1,1024]{1,0:T(1,128)S(1)}, f32[16,64]{1,0:T(8,128)}) custom-call(s32[1]{0:T(128)} %bitcast.me_ref, f32[16,8,128]{2,1,0:T(8,128)S(1)} %all_to_all.16.value_ref, f32[256,1024]{1,0:T(8,128)S(1)} %score.3.refs_0_, f32[512,1024]{1,0:T(8,128)S(1)} %score.4.refs_1_, f32[256,1024]{1,0:T(8,128)S(1)} %score.5.refs_2_), custom_call_target="tpu_custom_call" | custom-call | flops 8388608 | bytes 4268032 | tf_op jit(solution)/shard_map/columns/pallas_call | solution.py:116
  73.9 1.7 %rows.5 = f32[16,8,128]{2,1,0:T(8,128)} custom-call(s32[1]{0:T(128)} %bitcast.me_ref, f32[1,1024]{1,0:T(1,128)S(1)} %add_subtract_fusion.shift_ref, f32[256,1024]{1,0:T(8,128)S(1)} %score.3.refs_0_, f32[512,1024]{1,0:T(8,128)S(1)} %score.4.refs_1_, f32[256,1024]{1,0:T(8,128)S(1)} %score.5.refs_2_), custom_call_target="tpu_custom_call" | custom-call | flops 8388608 | bytes 4263936 | tf_op jit(solution)/shard_map/rows/pallas_call | solution.py:116
  75.7 3.5 %all-to-all-start.2 = ((f32[16,8,128]{2,1,0:T(8,128)}), f32[16,8,128]{2,1,0:T(8,128)S(1)}, u32[]{:S(2)}, u32[]{:S(2)}) async-start(f32[16,8,128]{2,1,0:T(8,128)} %rows.5), calls=%async_computation.2 | async-start | bytes 131072 | tf_op jit(solution)/shard_map/all_to_all | solution.py:178
  79.3 7.4 %all-to-all-done.2.value_ref = f32[16,8,128]{2,1,0:T(8,128)S(1)} async-done(((f32[16,8,128]{2,1,0:T(8,128)}), f32[16,8,128]{2,1,0:T(8,128)S(1)}, u32[]{:S(2)}, u32[]{:S(2)}) %all-to-all-start.2) | async-done | bytes 65568 | tf_op jit(solution)/shard_map/all_to_all | solution.py:178
  86.7 1.2 %copy-done.1 = f32[256,1024]{1,0:T(8,128)S(1)} copy-done((f32[256,1024]{1,0:T(8,128)S(1)}, f32[256,1024]{1,0:T(8,128)}, u32[]{:S(2)}) %copy-start.1) | copy-done | bytes 1048600
  87.9 1.2 %columns.5 = (f32[1,1024]{1,0:T(1,128)S(1)}, f32[16,64]{1,0:T(8,128)S(1)}) custom-call(s32[1]{0:T(128)} %bitcast.me_ref, f32[16,8,128]{2,1,0:T(8,128)S(1)} %all-to-all-done.2.value_ref, f32[256,1024]{1,0:T(8,128)S(1)} %score.3.refs_0_, f32[512,1024]{1,0:T(8,128)S(1)} %score.4.refs_1_, f32[256,1024]{1,0:T(8,128)S(1)} %copy-done.1), custom_call_target="tpu_custom_call" | custom-call | flops 8388608 | bytes 4268032 | tf_op jit(solution)/shard_map/columns/pallas_call | solution.py:116
  (31 shorter events, 10.8 us)
Async XLA Ops:
  0.6 24.5 %copy-start.2 = (bf16[1024,1024]{1,0:T(8,128)(2,1)S(1)}, bf16[1024,1024]{1,0:T(8,128)(2,1)}, u32[]{:S(2)}) copy-start(bf16[1024,1024]{1,0:T(8,128)(2,1)} %refs_2_.3) | copy-start | bytes 6291460
  0.6 8.3 %collective-permute-start = (bf16[64,1024]{1,0:T(8,128)(2,1)}, bf16[64,1024]{1,0:T(8,128)(2,1)S(1)}, u32[]{:S(2)}, u32[]{:S(2)}) collective-permute-start(bf16[64,1024]{1,0:T(8,128)(2,1)} %bitcast.13), channel_id=1, source_target_pairs={{0,8},{2,10},{4,12},{6,14},{8,0},{10,2},{12,4},{14,6},{16,24},{18,... | collective-permute-start | bytes 393224 | tf_op jit(solution)/shard_map/ppermute | solution.py:141
  3.7 13.2 %collective-permute-start.1 = (bf16[64,1024]{1,0:T(8,128)(2,1)}, bf16[64,1024]{1,0:T(8,128)(2,1)S(1)}, u32[]{:S(2)}, u32[]{:S(2)}) collective-permute-start(bf16[64,1024]{1,0:T(8,128)(2,1)} %bitcast.14), channel_id=1, source_target_pairs={{0,16},{2,18},{4,20},{6,22},{8,24},{10,26},{12,28},{14,30},{16,0},... | collective-permute-start | bytes 393224 | tf_op jit(solution)/shard_map/ppermute | solution.py:141
  6.3 10.6 %collective-permute-start.2 = (bf16[64,1024]{1,0:T(8,128)(2,1)}, bf16[64,1024]{1,0:T(8,128)(2,1)S(1)}, u32[]{:S(2)}, u32[]{:S(2)}) collective-permute-start(bf16[64,1024]{1,0:T(8,128)(2,1)} %bitcast.15), channel_id=1, source_target_pairs={{0,24},{2,26},{4,28},{6,30},{8,16},{10,18},{12,20},{14,22},{16,8},... | collective-permute-start | bytes 393224 | tf_op jit(solution)/shard_map/ppermute | solution.py:141
  18.6 11.5 %collective-permute-start.3 = (bf16[256,1024]{1,0:T(8,128)(2,1)}, bf16[256,1024]{1,0:T(8,128)(2,1)}, u32[]{:S(2)}, u32[]{:S(2)}) collective-permute-start(bf16[256,1024]{1,0:T(8,128)(2,1)} %pad_maximum_fusion.refs_0_), channel_id=1, source_target_pairs={{0,2},{2,0},{4,6},{6,4},{8,10},{10,8},{12,14},{14,12},{16,18},{18,... | collective-permute-start | bytes 1572872 | tf_op jit(solution)/shard_map/ppermute | solution.py:141
  20.1 11.3 %collective-permute-start.4 = (bf16[256,1024]{1,0:T(8,128)(2,1)}, bf16[256,1024]{1,0:T(8,128)(2,1)}, u32[]{:S(2)}, u32[]{:S(2)}) collective-permute-start(bf16[256,1024]{1,0:T(8,128)(2,1)} %pad_maximum_fusion.refs_0_), channel_id=1, source_target_pairs={{0,4},{2,6},{4,0},{6,2},{8,12},{10,14},{12,8},{14,10},{16,20},{18,... | collective-permute-start | bytes 1572872 | tf_op jit(solution)/shard_map/ppermute | solution.py:141
  25.1 10.3 %copy-start.3 = (bf16[1024,1024]{1,0:T(8,128)(2,1)S(1)}, bf16[1024,1024]{1,0:T(8,128)(2,1)}, u32[]{:S(2)}) copy-start(bf16[1024,1024]{1,0:T(8,128)(2,1)} %refs_2_.3) | copy-start | bytes 6291460
  32.3 6.4 %collective-permute-start.5 = (bf16[128,1024]{1,0:T(8,128)(2,1)S(1)}, bf16[128,1024]{1,0:T(8,128)(2,1)S(1)}, u32[]{:S(2)}, u32[]{:S(2)}) collective-permute-start(bf16[128,1024]{1,0:T(8,128)(2,1)S(1)} %slice.6), channel_id=1, source_target_pairs={{0,4},{2,6},{4,0},{6,2},{8,12},{10,14},{12,8},{14,10},{16,20},{18,... | collective-permute-start | bytes 786440 | tf_op jit(solution)/shard_map/ppermute | solution.py:141
  34.9 6.4 %collective-permute-start.6 = (bf16[128,1024]{1,0:T(8,128)(2,1)S(1)}, bf16[128,1024]{1,0:T(8,128)(2,1)S(1)}, u32[]{:S(2)}, u32[]{:S(2)}) collective-permute-start(bf16[128,1024]{1,0:T(8,128)(2,1)S(1)} %slice.7), channel_id=1, source_target_pairs={{0,2},{2,0},{4,6},{6,4},{8,10},{10,8},{12,14},{14,12},{16,18},{18,... | collective-permute-start | bytes 786440 | tf_op jit(solution)/shard_map/ppermute | solution.py:141
  43.4 30.5 %copy-start = (f32[256,1024]{1,0:T(8,128)}, f32[256,1024]{1,0:T(8,128)S(1)}, u32[]{:S(2)}) copy-start(f32[256,1024]{1,0:T(8,128)S(1)} %score.5.refs_2_) | copy-start | bytes 3145732
  58.9 1.2 %collective-permute-start.7 = (f32[1,1024]{1,0:T(1,128)S(1)}, f32[1,1024]{1,0:T(1,128)S(1)}, u32[]{:S(2)}, u32[]{:S(2)}) collective-permute-start(f32[1,1024]{1,0:T(1,128)S(1)} %get-tuple-element.18), channel_id=1, source_target_pairs={{0,1},{1,0},{2,3},{3,2},{4,5},{5,4},{6,7},{7,6},{8,9},{9,8},{10,11... | collective-permute-start | bytes 12296 | tf_op jit(solution)/shard_map/ppermute | solution.py:190
  72.6 1.2 %collective-permute-start.8 = (f32[1,1024]{1,0:T(1,128)S(1)}, f32[1,1024]{1,0:T(1,128)S(1)}, u32[]{:S(2)}, u32[]{:S(2)}) collective-permute-start(f32[1,1024]{1,0:T(1,128)S(1)} %get-tuple-element.19), channel_id=1, source_target_pairs={{0,1},{1,0},{2,3},{3,2},{4,5},{5,4},{6,7},{7,6},{8,9},{9,8},{10,11... | collective-permute-start | bytes 12296 | tf_op jit(solution)/shard_map/ppermute | solution.py:190
  73.9 5.3 %copy-start.4 = (bf16[1,64,1024]{2,1,0:T(8,128)(2,1)S(1)}, bf16[1,64,1024]{2,1,0:T(8,128)(2,1)}, u32[]{:S(2)}) copy-start(bf16[1,64,1024]{2,1,0:T(8,128)(2,1)} %param.4) | copy-start | bytes 393220
  75.7 11.0 %all-to-all-start.2 = ((f32[16,8,128]{2,1,0:T(8,128)}), f32[16,8,128]{2,1,0:T(8,128)S(1)}, u32[]{:S(2)}, u32[]{:S(2)}) async-start(f32[16,8,128]{2,1,0:T(8,128)} %rows.5), calls=%async_computation.2 | async-start | bytes 131072 | tf_op jit(solution)/shard_map/all_to_all | solution.py:178
  86.7 1.2 %copy-start.1 = (f32[256,1024]{1,0:T(8,128)S(1)}, f32[256,1024]{1,0:T(8,128)}, u32[]{:S(2)}) copy-start(f32[256,1024]{1,0:T(8,128)} %copy-done) | copy-start | bytes 3145732
  89.1 1.2 %collective-permute-start.9 = (f32[1,1024]{1,0:T(1,128)S(1)}, f32[1,1024]{1,0:T(1,128)S(1)}, u32[]{:S(2)}, u32[]{:S(2)}) collective-permute-start(f32[1,1024]{1,0:T(1,128)S(1)} %get-tuple-element.21), channel_id=1, source_target_pairs={{0,1},{1,0},{2,3},{3,2},{4,5},{5,4},{6,7},{7,6},{8,9},{9,8},{10,11... | collective-permute-start | bytes 12296 | tf_op jit(solution)/shard_map/ppermute | solution.py:190

commit v3 on v2

v3 whole, which is shorter than its diff:
```python
import functools
import math

import jax
import jax.numpy as jnp
from jax import lax
from jax.experimental import pallas as pl
from jax.experimental.pallas import tpu as pltpu
from jax.sharding import PartitionSpec as P

TILE = 512
CAP = 4
ITERS = 3


EPS = 0.02
NEG = -1e30
LN2 = math.log(2.0)
LANES = 128
VMEM_LIMIT = 20 * 1024 * 1024


def log2_sum(values):
    peak = functools.reduce(jnp.maximum, values)
    total = functools.reduce(jnp.add, [jnp.exp2(v - peak) for v in values])
    return peak + jnp.log(total) * (1.0 / LN2)


def diagonal(size):
    rows = lax.broadcasted_iota(jnp.int32, (size, size), 0)
    return rows == lax.broadcasted_iota(jnp.int32, (size, size), 1)


def row_sums(block):
    peak = jnp.max(block, axis=1, keepdims=True)
    total = jnp.sum(jnp.exp2(block - peak), axis=1, keepdims=True)
    column = peak + jnp.log(total) * (1.0 / LN2)
    return jnp.sum(jnp.where(diagonal(block.shape[0]), column, 0.0), axis=0, keepdims=True)


def copy_out(held_ref, out_ref):
    across = out_ref.shape[2] // held_ref.shape[1]
    for line in range(out_ref.shape[1]):
        sources = [held_ref[line * across + k : line * across + k + 1, :] for k in range(across)]
        wide = jnp.concatenate(sources, axis=1)
        out_ref[:, line, :] = jnp.broadcast_to(wide, (out_ref.shape[0], out_ref.shape[2]))


def score_kernel(pieces, blocks, own_rows, scale, me_ref, list_ref, count_ref, *refs):
    rows_refs = refs[:pieces]
    pool_ref, shift_ref, before_ref, score_ref, held_ref = refs[pieces : pieces + 5]
    me = me_ref[0]
    shift = shift_ref[...]
    tiles = pool_ref.shape[0] // TILE
    rows = rows_refs[0]
    if pieces > 1:
        rows = refs[-1]
        low = 0
        for ref in rows_refs:
            rows[low : low + ref.shape[0], :] = ref[...]
            low += ref.shape[0]
    dots = lax.dot_general(
        rows[...],
        pool_ref[...],
        (((1,), (1,)), ((), ())),
        preferred_element_type=jnp.float32,
    )
    held_ref[...] = before_ref[...]
    low = 0
    for source, first, count in blocks:
        owner = me ^ source
        tile = lax.div(owner * own_rows, TILE)
        parts = []
        for u in range(tiles):
            counted = jnp.int32(0)
            for k in range(CAP):
                hit = (k < count_ref[0]) & (list_ref[k, 0] == tile) & (list_ref[k, 1] == u)
                counted += jnp.where(hit, 1, 0)
            offset = jnp.where(counted > 0, 0.0, NEG)
            parts.append(dots[low : low + count, u * TILE : (u + 1) * TILE] * scale + offset)
        block = jnp.concatenate(parts, axis=1)
        score_ref[low : low + count, :] = block
        held_ref[pl.ds(owner, 1), first : first + count] = row_sums(block + shift)
        low += count


def last_score_kernel(pieces, blocks, own_rows, scale, *refs):
    inputs = pieces + 6
    score_ref, out_ref, held_ref = refs[inputs : inputs + 3]
    head = refs[:inputs] + (score_ref, held_ref)
    score_kernel(pieces, blocks, own_rows, scale, *head, *refs[inputs + 3 :])
    copy_out(held_ref, out_ref)


def row_kernel(parts, me_ref, shift_ref, *refs):
    out_ref, held_ref = refs[-2:]
    me = me_ref[0]
    shift = shift_ref[...]
    for ref, blocks in zip(refs[:-2], parts):
        low = 0
        for source, first, count in blocks:
            sums = row_sums(ref[low : low + count, :] + shift)
            held_ref[pl.ds(me ^ source, 1), first : first + count] = sums
            low += count
    copy_out(held_ref, out_ref)


def column_kernel(parts, log_a, me_ref, value_ref, *refs):
    out_ref, held_ref = refs[-2:]
    me = me_ref[0]
    shift = log_a - log2_sum([value_ref[k] for k in range(value_ref.shape[0])])
    own_rows = held_ref.shape[1]
    across = shift.shape[1] // own_rows
    for source in range(held_ref.shape[0]):
        line, place = source // across, source % across
        held_ref[source : source + 1, :] = shift[
            line : line + 1, place * own_rows : (place + 1) * own_rows
        ]
    columns = []
    peak = None
    for ref, blocks in zip(refs[:-2], parts):
        low = 0
        for source, first, count in blocks:
            row = held_ref[pl.ds(me ^ source, 1), first : first + count]
            column = jnp.sum(jnp.where(diagonal(count), row, 0.0), axis=1, keepdims=True)
            columns.append(column)
            block = ref[low : low + count, :] + column
            high = jnp.max(block.reshape(count // 8, 8, block.shape[1]), axis=0)
            peak = high if peak is None else jnp.maximum(peak, high)
            low += count
    peak = jnp.max(peak, axis=0, keepdims=True)
    total = jnp.zeros((8, peak.shape[1]), jnp.float32)
    for ref, blocks in zip(refs[:-2], parts):
        low = 0
        for source, first, count in blocks:
            block = ref[low : low + count, :] + (columns.pop(0) - peak)
            total += jnp.sum(jnp.exp2(block).reshape(count // 8, 8, block.shape[1]), axis=0)
            low += count
    total = jnp.sum(total, axis=0, keepdims=True)
    out_ref[...] = peak + jnp.log(total) * (1.0 / LN2)


def call(kernel, shapes, scratch, scalars, arrays, flops, name):
    smem = pl.BlockSpec(memory_space=pltpu.SMEM)
    vmem = pl.BlockSpec(memory_space=pltpu.VMEM)
    moved = sum(a.size * a.dtype.itemsize for a in arrays) + 4 * sum(map(math.prod, shapes))
    return pl.pallas_call(
        kernel,
        out_shape=[jax.ShapeDtypeStruct(s, jnp.float32) for s in shapes],
        in_specs=[smem] * len(scalars) + [vmem] * len(arrays),
        out_specs=[vmem] * len(shapes),
        scratch_shapes=scratch,
        compiler_params=pltpu.CompilerParams(vmem_limit_bytes=VMEM_LIMIT),
        cost_estimate=pl.CostEstimate(flops=flops, bytes_accessed=moved, transcendentals=0),
        name=name,
    )(*scalars, *arrays)


def body(samples, pool, tile_list, tile_count):
    own_rows, width = samples.shape[1:]
    size = lax.axis_size("pool")
    half_rows = own_rows * size
    pool_rows = pool.shape[0]
    unit = EPS * LN2
    log_a = -math.log2(half_rows * lax.axis_size("samp"))
    log_b = -math.log2(pool_rows * size)
    me = lax.axis_index("pool").astype(jnp.int32).reshape(1)
    own = samples.reshape(own_rows, width)

    def swap(value, mask):
        return lax.ppermute(value, "pool", [(i, i ^ mask) for i in range(size)])

    def score(pieces, blocks, before, last=False):
        count = sum(b[2] for b in blocks)
        shapes = [(count, pool_rows)] + [(size, lines, LANES)] * last + [(size, own_rows)]
        kernel = last_score_kernel if last else score_kernel
        return call(
            functools.partial(kernel, len(pieces), blocks, own_rows, 2.0 / (width * unit)),
            shapes,
            [pltpu.VMEM((count, width), samples.dtype)] * (len(pieces) > 1),
            [me, tile_list.reshape(CAP, 2), tile_count.reshape(1)],
            pieces + [pool, shift, before],
            2 * count * pool_rows * width,
            "score",
        )

    lines = half_rows // LANES
    own_norm = jnp.sum(jnp.square(own.astype(jnp.float32)), axis=1) / width
    pool_norm = jnp.sum(jnp.square(pool.astype(jnp.float32)), axis=1) / width
    shift = pool_norm.reshape(1, pool_rows) * (-1.0 / unit)
    near = (1, 2, 3)
    far = tuple(range(4, size, 4))
    cut = own_rows * 3 // 4
    rest = own_rows - cut
    top = own[:cut]
    by_far = [swap(top, m) for m in far]
    by_near = [swap(own, m) for m in near]
    blocks0 = [(m, 0, own_rows) for m in (0,) + near]
    score0, held = score([own] + by_near, blocks0, jnp.zeros((size, own_rows), jnp.float32))
    *by_far, score0, held = lax.optimization_barrier((*by_far, score0, held))
    band = jnp.concatenate(by_far, axis=0)
    foot = jnp.concatenate([own[cut:]] + [piece[cut:] for piece in by_near], axis=0)
    foot_far = [swap(foot, m) for m in far]
    band_near = [swap(band, m) for m in near]
    blocks1 = [(m, 0, cut) for m in far]
    score1, held = score([band], blocks1, held)
    barrier = lax.optimization_barrier((*foot_far, *band_near, score1, held))
    *pieces, score1, held = barrier
    blocks2 = [(f ^ m, cut, rest) for f in far for m in (0,) + near]
    blocks2 += [(f ^ m, 0, cut) for m in near for f in far]
    score2, value, _ = score(pieces, blocks2, held, last=True)
    scores = [score0, score1, score2]
    parts = [blocks0, blocks1, blocks2]
    held = [pltpu.VMEM((size, own_rows), jnp.float32)]
    flops = 8 * half_rows * pool_rows
    for step in range(ITERS):
        if step > 0:
            kernel = functools.partial(row_kernel, parts)
            (value,) = call(
                kernel, [(size, lines, LANES)], held, [me], [shift] + scores, flops, "rows"
            )
        value = lax.all_to_all(value, "pool", 0, 0, tiled=True)
        kernel = functools.partial(column_kernel, parts, log_a)
        value, potential = call(
            kernel,
            [(1, pool_rows), (size, own_rows)],
            [],
            [me],
            [value] + scores,
            flops,
            "columns",
        )
        pairs = [(i, i ^ 1) for i in range(2)]
        shift = log_b - log2_sum([value, lax.ppermute(value, "samp", pairs)])
    mine = lax.dynamic_slice_in_dim(potential, me[0], 1, 0)
    return mine * unit + own_norm[None, :], shift.reshape(pool_rows) * unit + pool_norm


def solution(mesh):
    placed = (
        P(("grp", "samp"), "pool", None),
        P(("grp", "pool"), None),
        P(("grp", "samp"), "pool", None, None),
        P(("grp", "samp"), "pool"),
    )
    return jax.shard_map(
        body,
        mesh=mesh,
        in_specs=placed,
        out_specs=(P(("grp", "samp"), "pool"), P(("grp", "pool"))),
        check_vma=False,
    )
```

time: 91.4 us -> 88.5 us (0.968)
  waiting for transfers between devices: 28.5 us -> 19.5 us
  starting transfers between devices: 14.6 us -> 21 us
  other arithmetic: 5.15 us -> 3.43 us
    ppermute x7 -> x12, waiting for transfers between devices: 18.2 us -> 9.18 us  [swap(): return lax.ppermute(value, 'pool', [(i, i ^ mask) for i in range(size)])]
    ppermute x7 -> x12, starting transfers between devices: 10.8 us -> 17.3 us  [swap(): return lax.ppermute(value, 'pool', [(i, i ^ mask) for i in range(size)])]
    concatenate x1, other arithmetic: 1.73 us -> 0.01 us  [body(): jnp.concatenate([own[cut:]] + [piece[cut:] for piece in by_near], axis=0)]
    unnamed x10 -> x14, local copies, waits for them, and re-layouts: 1.25 us -> 2.16 us
    pallas_call x9 -> x8, Pallas kernels: 14.1 us -> 14.8 us  [call(): pl.pallas_call(kernel, out_shape=[jax.ShapeDtypeStruct(s, jnp.float32) fo...]
    slice x2 -> x5, local copies, waits for them, and re-layouts: 1.93 us -> 1.72 us  [the longest x1 0.94 us: body(): top = own[:cut]]
  transfers between devices with their start and end apart: 11 -> 16, of which waited for: 10 -> 7; matrix products, arithmetic and copies ran while one was open for 5% -> 6% of each run, Pallas kernels for 5% -> 4%
where the time goes in v3:
time: 88.5 us; the launch traced here: 88 us
  blocking collectives  23.1 us (26%)
  starting transfers between devices  21 us (24%)
  waiting for transfers between devices  19.5 us (22%)
  Pallas kernels  14.8 us (17%)
  local copies, waits for them, and re-layouts  4.66 us (5%)
  other arithmetic  3.43 us (4%)
  between operations  1.54 us (2%)
    all_to_all x2, blocking collectives, body(): value = lax.all_to_all(value, 'pool', 0, 0, tiled=True)  23.1 us
    ppermute x12, starting transfers between devices, swap(): return lax.ppermute(value, 'pool', [(i, i ^ mask) for i in range(size)])  17.3 us
    pallas_call x8, Pallas kernels, call(): pl.pallas_call(kernel, out_shape=[jax.ShapeDtypeStruct(s, jnp.float32) fo...  14.8 us
    ppermute x12, waiting for transfers between devices, swap(): return lax.ppermute(value, 'pool', [(i, i ^ mask) for i in range(size)])  9.18 us
    all_to_all x1, waiting for transfers between devices, body(): value = lax.all_to_all(value, 'pool', 0, 0, tiled=True)  7.36 us
    all_to_all x1, starting transfers between devices, body(): value = lax.all_to_all(value, 'pool', 0, 0, tiled=True)  3.49 us
    ppermute x3, waiting for transfers between devices, body(): shift = log_b - log2_sum([value, lax.ppermute(value, 'samp', pairs)])  2.93 us
    unnamed x14, local copies, waits for them, and re-layouts  2.16 us
  transfers between devices with their start and end apart: 16, of which 7 were waited for; matrix products, arithmetic and copies ran while one was open for 6% of the time, Pallas kernels for 4%

profile of v3, /device:TPU:0, one launch (start us, length us, event | category | flops | bytes accessed | tf_op | source)
XLA Modules:
  0.0 88.0 jit_solution(4067946116100841010)
XLA Ops:
  0.6 3.0 %collective-permute-start = (bf16[64,1024]{1,0:T(8,128)(2,1)}, bf16[64,1024]{1,0:T(8,128)(2,1)S(1)}, u32[]{:S(2)}, u32[]{:S(2)}) collective-permute-start(bf16[64,1024]{1,0:T(8,128)(2,1)} %bitcast.16), channel_id=1, source_target_pairs={{0,2},{2,0},{4,6},{6,4},{8,10},{10,8},{12,14},{14,12},{16,18},{18,... | collective-permute-start | bytes 393224 | tf_op jit(solution)/shard_map/ppermute | solution.py:171
  3.6 1.5 %collective-permute-start.1 = (bf16[64,1024]{1,0:T(8,128)(2,1)}, bf16[64,1024]{1,0:T(8,128)(2,1)S(1)}, u32[]{:S(2)}, u32[]{:S(2)}) collective-permute-start(bf16[64,1024]{1,0:T(8,128)(2,1)} %bitcast.17), channel_id=1, source_target_pairs={{0,4},{2,6},{4,0},{6,2},{8,12},{10,14},{12,8},{14,10},{16,20},{18,... | collective-permute-start | bytes 393224 | tf_op jit(solution)/shard_map/ppermute | solution.py:171
  6.1 2.0 %collective-permute-start.6 = (bf16[48,1024]{1,0:T(8,128)(2,1)S(1)}, bf16[48,1024]{1,0:T(8,128)(2,1)S(1)}, u32[]{:S(2)}, u32[]{:S(2)}) collective-permute-start(bf16[48,1024]{1,0:T(8,128)(2,1)S(1)} %slice_bitcast_fusion), channel_id=1, source_target_pairs={{0,8},{2,10},{4,12},{6,14},{8,0},{10,2},{12,4},{14,6},{16,24},{18,... | collective-permute-start | bytes 294920 | tf_op jit(solution)/shard_map/ppermute | solution.py:171
  8.2 2.6 %collective-permute-start.7 = (bf16[48,1024]{1,0:T(8,128)(2,1)S(1)}, bf16[48,1024]{1,0:T(8,128)(2,1)S(1)}, u32[]{:S(2)}, u32[]{:S(2)}) collective-permute-start(bf16[48,1024]{1,0:T(8,128)(2,1)S(1)} %slice_bitcast_fusion), channel_id=1, source_target_pairs={{0,16},{2,18},{4,20},{6,22},{8,24},{10,26},{12,28},{14,30},{16,0},... | collective-permute-start | bytes 294920 | tf_op jit(solution)/shard_map/ppermute | solution.py:171
  10.7 2.1 %multiply_reduce_fusion = f32[1024]{0:T(1024)S(1)} fusion(bf16[1024,1024]{1,0:T(8,128)(2,1)} %refs_9_.1), kind=kLoop, calls=%fused_computation | loop fusion | flops 3144704 | bytes 2101248 | tf_op jit(solution)/shard_map/reduce_sum | solution.py:189
  16.0 1.6 %score.3 = (f32[256,1024]{1,0:T(8,128)S(1)}, f32[16,64]{1,0:T(8,128)S(1)}) custom-call(s32[1]{0:T(128)} %bitcast.me_ref.refs_0_, s32[4,2]{1,0:T(4,128)S(1)} %copy.8.list_ref.refs_1_, s32[1]{0:T(128)} %bitcast.13.count_ref, bf16[64,1024]{1,0:T(8,128)(2,1)S(1)} %bitcast.19, bf16[64,1024]{1,0:T(8,128)(2,1)S(1)} %collective-permute-done.refs_1_, ...), custom_call_target="tpu_custom_call" | custom-call | flops 536870912 | bytes 3682304 | tf_op jit(solution)/shard_map/score/pallas_call | solution.py:147
  17.6 2.4 %collective-permute-done.8 = bf16[48,1024]{1,0:T(8,128)(2,1)S(1)} collective-permute-done((bf16[48,1024]{1,0:T(8,128)(2,1)S(1)}, bf16[48,1024]{1,0:T(8,128)(2,1)S(1)}, u32[]{:S(2)}, u32[]{:S(2)}) %collective-permute-start.8) | collective-permute-done | bytes 98336 | tf_op jit(solution)/shard_map/ppermute | solution.py:171
  20.0 1.6 %collective-permute-start.10 = (bf16[144,1024]{1,0:T(8,128)(2,1)S(1)}, bf16[144,1024]{1,0:T(8,128)(2,1)S(1)}, u32[]{:S(2)}, u32[]{:S(2)}) collective-permute-start(bf16[144,1024]{1,0:T(8,128)(2,1)S(1)} %constant_dynamic-update-slice_fusion.refs_0_), channel_id=1, source_target_pairs={{0,4},{2,6},{4,0},{6,2},{8,12},{10,14},{12,8},{14,10},{16,20},{18,... | collective-permute-start | bytes 884744 | tf_op jit(solution)/shard_map/ppermute | solution.py:171
  21.6 1.4 %collective-permute-start.11 = (bf16[144,1024]{1,0:T(8,128)(2,1)S(1)}, bf16[144,1024]{1,0:T(8,128)(2,1)S(1)}, u32[]{:S(2)}, u32[]{:S(2)}) collective-permute-start(bf16[144,1024]{1,0:T(8,128)(2,1)S(1)} %constant_dynamic-update-slice_fusion.refs_0_), channel_id=1, source_target_pairs={{0,6},{2,4},{4,2},{6,0},{8,14},{10,12},{12,10},{14,8},{16,22},{18,... | collective-permute-start | bytes 884744 | tf_op jit(solution)/shard_map/ppermute | solution.py:171
  23.7 1.9 %collective-permute-start.4 = (bf16[64,1024]{1,0:T(8,128)(2,1)S(1)}, bf16[64,1024]{1,0:T(8,128)(2,1)S(1)}, u32[]{:S(2)}, u32[]{:S(2)}) collective-permute-start(bf16[64,1024]{1,0:T(8,128)(2,1)S(1)} %pad_maximum_fusion), channel_id=1, source_target_pairs={{0,16},{2,18},{4,20},{6,22},{8,24},{10,26},{12,28},{14,30},{16,0},... | collective-permute-start | bytes 393224 | tf_op jit(solution)/shard_map/ppermute | solution.py:171
  25.6 4.1 %collective-permute-done.3.refs_3_ = bf16[64,1024]{1,0:T(8,128)(2,1)S(1)} collective-permute-done((bf16[64,1024]{1,0:T(8,128)(2,1)S(1)}, bf16[64,1024]{1,0:T(8,128)(2,1)S(1)}, u32[]{:S(2)}, u32[]{:S(2)}) %collective-permute-start.3) | collective-permute-done | bytes 131104 | tf_op jit(solution)/shard_map/ppermute | solution.py:171
  29.7 2.6 %collective-permute-start.5 = (bf16[64,1024]{1,0:T(8,128)(2,1)S(1)}, bf16[64,1024]{1,0:T(8,128)(2,1)S(1)}, u32[]{:S(2)}, u32[]{:S(2)}) collective-permute-start(bf16[64,1024]{1,0:T(8,128)(2,1)S(1)} %pad_maximum_fusion), channel_id=1, source_target_pairs={{0,24},{2,26},{4,28},{6,30},{8,16},{10,18},{12,20},{14,22},{16,8},... | collective-permute-start | bytes 393224 | tf_op jit(solution)/shard_map/ppermute | solution.py:171
  32.3 1.6 %score.4 = (f32[144,1024]{1,0:T(8,128)S(1)}, f32[16,64]{1,0:T(8,128)S(1)}) custom-call(s32[1]{0:T(128)} %bitcast.me_ref.refs_0_, s32[4,2]{1,0:T(4,128)S(1)} %copy.8.list_ref.refs_1_, s32[1]{0:T(128)} %bitcast.14.count_ref, bf16[144,1024]{1,0:T(8,128)(2,1)S(1)} %constant_dynamic-update-slice_fusion.refs_0_, bf16[1024,1024]{1,0:T(8,128)(2,1)S(1)} %copy-done.2, ...), custom_call_target="tpu_custom_call" | custom-call | flops 301989888 | bytes 2994176 | tf_op jit(solution)/shard_map/score/pallas_call | solution.py:147
  33.9 2.7 %collective-permute-done.5.refs_5_ = bf16[64,1024]{1,0:T(8,128)(2,1)S(1)} collective-permute-done((bf16[64,1024]{1,0:T(8,128)(2,1)S(1)}, bf16[64,1024]{1,0:T(8,128)(2,1)S(1)}, u32[]{:S(2)}, u32[]{:S(2)}) %collective-permute-start.5) | collective-permute-done | bytes 131104 | tf_op jit(solution)/shard_map/ppermute | solution.py:171
  36.6 3.4 %score.5 = (f32[624,1024]{1,0:T(8,128)S(1)}, f32[16,8,128]{2,1,0:T(8,128)S(1)}, f32[16,64]{1,0:T(8,128)}) custom-call(s32[1]{0:T(128)} %bitcast.me_ref.refs_0_, s32[4,2]{1,0:T(4,128)S(1)} %copy.8.list_ref.refs_1_, s32[1]{0:T(128)} %bitcast.15.refs_2_, bf16[64,1024]{1,0:T(8,128)(2,1)S(1)} %collective-permute-done.3.refs_3_, ...), custom_call_target="tpu_custom_call" | custom-call | flops 1308622848 | bytes 6008832 | tf_op jit(solution)/shard_map/score/pallas_call | solution.py:147
  40.0 13.0 %all_to_all.15.value_ref = f32[16,8,128]{2,1,0:T(8,128)S(1)} all-to-all(f32[16,8,128]{2,1,0:T(8,128)S(1)} %get-tuple-element.40), channel_id=1, replica_groups=mesh['grp'=1,'pool'=16,'samp'=2] {'pool'}, dimensions={0} | all-to-all | bytes 131072 | tf_op jit(solution)/shard_map/all_to_all | solution.py:222
  54.1 1.2 %collective-permute-done.12 = f32[1,1024]{1,0:T(1,128)S(1)} collective-permute-done((f32[1,1024]{1,0:T(1,128)S(1)}, f32[1,1024]{1,0:T(1,128)S(1)}, u32[]{:S(2)}, u32[]{:S(2)}) %collective-permute-start.12) | collective-permute-done | bytes 4128 | tf_op jit(solution)/shard_map/ppermute | solution.py:234
  55.3 2.1 %rows.2 = f32[16,8,128]{2,1,0:T(8,128)S(1)} custom-call(s32[1]{0:T(128)} %bitcast.me_ref.refs_0_, f32[1,1024]{1,0:T(1,128)S(1)} %add_subtract_fusion.1.shift_ref, f32[256,1024]{1,0:T(8,128)S(1)} %get-tuple-element.41.refs_0_, f32[144,1024]{1,0:T(8,128)S(1)} %get-tuple-element.42.refs_1_, f32[624,1024]{1,0:T(8,128)S(1)} %get-tuple-element.43.refs_2_), custom_call_target="tpu_custom_call" | custom-call | flops 8388608 | bytes 4263936 | tf_op jit(solution)/shard_map/rows/pallas_call | solution.py:147
  57.5 10.1 %all_to_all.16.value_ref = f32[16,8,128]{2,1,0:T(8,128)S(1)} all-to-all(f32[16,8,128]{2,1,0:T(8,128)S(1)} %rows.2), channel_id=1, replica_groups=mesh['grp'=1,'pool'=16,'samp'=2] {'pool'}, dimensions={0} | all-to-all | bytes 131072 | tf_op jit(solution)/shard_map/all_to_all | solution.py:222
  68.8 1.2 %collective-permute-done.13 = f32[1,1024]{1,0:T(1,128)S(1)} collective-permute-done((f32[1,1024]{1,0:T(1,128)S(1)}, f32[1,1024]{1,0:T(1,128)S(1)}, u32[]{:S(2)}, u32[]{:S(2)}) %collective-permute-start.13) | collective-permute-done | bytes 4128 | tf_op jit(solution)/shard_map/ppermute | solution.py:234
  70.0 2.7 %rows.3 = f32[16,8,128]{2,1,0:T(8,128)} custom-call(s32[1]{0:T(128)} %bitcast.me_ref.refs_0_, f32[1,1024]{1,0:T(1,128)S(1)} %add_subtract_fusion.shift_ref, f32[256,1024]{1,0:T(8,128)S(1)} %get-tuple-element.41.refs_0_, f32[144,1024]{1,0:T(8,128)S(1)} %get-tuple-element.42.refs_1_, f32[624,1024]{1,0:T(8,128)S(1)} %get-tuple-element.43.refs_2_), custom_call_target="tpu_custom_call" | custom-call | flops 8388608 | bytes 4263936 | tf_op jit(solution)/shard_map/rows/pallas_call | solution.py:147
  72.8 3.5 %all-to-all-start.2 = ((f32[16,8,128]{2,1,0:T(8,128)}), f32[16,8,128]{2,1,0:T(8,128)S(1)}, u32[]{:S(2)}, u32[]{:S(2)}) async-start(f32[16,8,128]{2,1,0:T(8,128)} %rows.3), calls=%async_computation.2 | async-start | bytes 131072 | tf_op jit(solution)/shard_map/all_to_all | solution.py:222
  76.4 7.4 %all-to-all-done.2.value_ref = f32[16,8,128]{2,1,0:T(8,128)S(1)} async-done(((f32[16,8,128]{2,1,0:T(8,128)}), f32[16,8,128]{2,1,0:T(8,128)S(1)}, u32[]{:S(2)}, u32[]{:S(2)}) %all-to-all-start.2) | async-done | bytes 65568 | tf_op jit(solution)/shard_map/all_to_all | solution.py:222
  83.8 1.2 %copy-done.1 = f32[256,1024]{1,0:T(8,128)S(1)} copy-done((f32[256,1024]{1,0:T(8,128)S(1)}, f32[256,1024]{1,0:T(8,128)}, u32[]{:S(2)}) %copy-start.1) | copy-done | bytes 1048600
  (49 shorter events, 9.7 us)
Async XLA Ops:
  0.6 14.4 %copy-start.2 = (bf16[1024,1024]{1,0:T(8,128)(2,1)S(1)}, bf16[1024,1024]{1,0:T(8,128)(2,1)}, u32[]{:S(2)}) copy-start(bf16[1024,1024]{1,0:T(8,128)(2,1)} %refs_9_.1) | copy-start | bytes 6291460
  0.6 12.9 %collective-permute-start = (bf16[64,1024]{1,0:T(8,128)(2,1)}, bf16[64,1024]{1,0:T(8,128)(2,1)S(1)}, u32[]{:S(2)}, u32[]{:S(2)}) collective-permute-start(bf16[64,1024]{1,0:T(8,128)(2,1)} %bitcast.16), channel_id=1, source_target_pairs={{0,2},{2,0},{4,6},{6,4},{8,10},{10,8},{12,14},{14,12},{16,18},{18,... | collective-permute-start | bytes 393224 | tf_op jit(solution)/shard_map/ppermute | solution.py:171
  3.6 11.4 %collective-permute-start.1 = (bf16[64,1024]{1,0:T(8,128)(2,1)}, bf16[64,1024]{1,0:T(8,128)(2,1)S(1)}, u32[]{:S(2)}, u32[]{:S(2)}) collective-permute-start(bf16[64,1024]{1,0:T(8,128)(2,1)} %bitcast.17), channel_id=1, source_target_pairs={{0,4},{2,6},{4,0},{6,2},{8,12},{10,14},{12,8},{14,10},{16,20},{18,... | collective-permute-start | bytes 393224 | tf_op jit(solution)/shard_map/ppermute | solution.py:171
  5.2 9.9 %collective-permute-start.2 = (bf16[64,1024]{1,0:T(8,128)(2,1)}, bf16[64,1024]{1,0:T(8,128)(2,1)S(1)}, u32[]{:S(2)}, u32[]{:S(2)}) collective-permute-start(bf16[64,1024]{1,0:T(8,128)(2,1)} %bitcast.18), channel_id=1, source_target_pairs={{0,6},{2,4},{4,2},{6,0},{8,14},{10,12},{12,10},{14,8},{16,22},{18,... | collective-permute-start | bytes 393224 | tf_op jit(solution)/shard_map/ppermute | solution.py:171
  6.1 11.4 %collective-permute-start.6 = (bf16[48,1024]{1,0:T(8,128)(2,1)S(1)}, bf16[48,1024]{1,0:T(8,128)(2,1)S(1)}, u32[]{:S(2)}, u32[]{:S(2)}) collective-permute-start(bf16[48,1024]{1,0:T(8,128)(2,1)S(1)} %slice_bitcast_fusion), channel_id=1, source_target_pairs={{0,8},{2,10},{4,12},{6,14},{8,0},{10,2},{12,4},{14,6},{16,24},{18,... | collective-permute-start | bytes 294920 | tf_op jit(solution)/shard_map/ppermute | solution.py:171
  8.2 9.4 %collective-permute-start.7 = (bf16[48,1024]{1,0:T(8,128)(2,1)S(1)}, bf16[48,1024]{1,0:T(8,128)(2,1)S(1)}, u32[]{:S(2)}, u32[]{:S(2)}) collective-permute-start(bf16[48,1024]{1,0:T(8,128)(2,1)S(1)} %slice_bitcast_fusion), channel_id=1, source_target_pairs={{0,16},{2,18},{4,20},{6,22},{8,24},{10,26},{12,28},{14,30},{16,0},... | collective-permute-start | bytes 294920 | tf_op jit(solution)/shard_map/ppermute | solution.py:171
  13.6 6.4 %collective-permute-start.8 = (bf16[48,1024]{1,0:T(8,128)(2,1)S(1)}, bf16[48,1024]{1,0:T(8,128)(2,1)S(1)}, u32[]{:S(2)}, u32[]{:S(2)}) collective-permute-start(bf16[48,1024]{1,0:T(8,128)(2,1)S(1)} %slice_bitcast_fusion), channel_id=1, source_target_pairs={{0,24},{2,26},{4,28},{6,30},{8,16},{10,18},{12,20},{14,22},{16,8},... | collective-permute-start | bytes 294920 | tf_op jit(solution)/shard_map/ppermute | solution.py:171
  15.1 0.9 %copy-start.4 = (bf16[1,64,1024]{2,1,0:T(8,128)(2,1)S(1)}, bf16[1,64,1024]{2,1,0:T(8,128)(2,1)}, u32[]{:S(2)}) copy-start(bf16[1,64,1024]{2,1,0:T(8,128)(2,1)} %param.4) | copy-start | bytes 393220
  16.0 20.6 %copy-start.3 = (bf16[1024,1024]{1,0:T(8,128)(2,1)S(1)}, bf16[1024,1024]{1,0:T(8,128)(2,1)}, u32[]{:S(2)}) copy-start(bf16[1024,1024]{1,0:T(8,128)(2,1)} %refs_9_.1) | copy-start | bytes 6291460
  17.5 52.5 %copy-start = (f32[256,1024]{1,0:T(8,128)}, f32[256,1024]{1,0:T(8,128)S(1)}, u32[]{:S(2)}) copy-start(f32[256,1024]{1,0:T(8,128)S(1)} %get-tuple-element.41.refs_0_) | copy-start | bytes 3145732
  20.0 16.5 %collective-permute-start.10 = (bf16[144,1024]{1,0:T(8,128)(2,1)S(1)}, bf16[144,1024]{1,0:T(8,128)(2,1)S(1)}, u32[]{:S(2)}, u32[]{:S(2)}) collective-permute-start(bf16[144,1024]{1,0:T(8,128)(2,1)S(1)} %constant_dynamic-update-slice_fusion.refs_0_), channel_id=1, source_target_pairs={{0,4},{2,6},{4,0},{6,2},{8,12},{10,14},{12,8},{14,10},{16,20},{18,... | collective-permute-start | bytes 884744 | tf_op jit(solution)/shard_map/ppermute | solution.py:171
  21.6 15.0 %collective-permute-start.11 = (bf16[144,1024]{1,0:T(8,128)(2,1)S(1)}, bf16[144,1024]{1,0:T(8,128)(2,1)S(1)}, u32[]{:S(2)}, u32[]{:S(2)}) collective-permute-start(bf16[144,1024]{1,0:T(8,128)(2,1)S(1)} %constant_dynamic-update-slice_fusion.refs_0_), channel_id=1, source_target_pairs={{0,6},{2,4},{4,2},{6,0},{8,14},{10,12},{12,10},{14,8},{16,22},{18,... | collective-permute-start | bytes 884744 | tf_op jit(solution)/shard_map/ppermute | solution.py:171
  23.1 13.5 %collective-permute-start.9 = (bf16[144,1024]{1,0:T(8,128)(2,1)S(1)}, bf16[144,1024]{1,0:T(8,128)(2,1)S(1)}, u32[]{:S(2)}, u32[]{:S(2)}) collective-permute-start(bf16[144,1024]{1,0:T(8,128)(2,1)S(1)} %constant_dynamic-update-slice_fusion.refs_0_), channel_id=1, source_target_pairs={{0,2},{2,0},{4,6},{6,4},{8,10},{10,8},{12,14},{14,12},{16,18},{18,... | collective-permute-start | bytes 884744 | tf_op jit(solution)/shard_map/ppermute | solution.py:171
  23.6 6.1 %collective-permute-start.3 = (bf16[64,1024]{1,0:T(8,128)(2,1)S(1)}, bf16[64,1024]{1,0:T(8,128)(2,1)S(1)}, u32[]{:S(2)}, u32[]{:S(2)}) collective-permute-start(bf16[64,1024]{1,0:T(8,128)(2,1)S(1)} %pad_maximum_fusion), channel_id=1, source_target_pairs={{0,8},{2,10},{4,12},{6,14},{8,0},{10,2},{12,4},{14,6},{16,24},{18,... | collective-permute-start | bytes 393224 | tf_op jit(solution)/shard_map/ppermute | solution.py:171
  23.7 10.2 %collective-permute-start.4 = (bf16[64,1024]{1,0:T(8,128)(2,1)S(1)}, bf16[64,1024]{1,0:T(8,128)(2,1)S(1)}, u32[]{:S(2)}, u32[]{:S(2)}) collective-permute-start(bf16[64,1024]{1,0:T(8,128)(2,1)S(1)} %pad_maximum_fusion), channel_id=1, source_target_pairs={{0,16},{2,18},{4,20},{6,22},{8,24},{10,26},{12,28},{14,30},{16,0},... | collective-permute-start | bytes 393224 | tf_op jit(solution)/shard_map/ppermute | solution.py:171
  29.7 6.9 %collective-permute-start.5 = (bf16[64,1024]{1,0:T(8,128)(2,1)S(1)}, bf16[64,1024]{1,0:T(8,128)(2,1)S(1)}, u32[]{:S(2)}, u32[]{:S(2)}) collective-permute-start(bf16[64,1024]{1,0:T(8,128)(2,1)S(1)} %pad_maximum_fusion), channel_id=1, source_target_pairs={{0,24},{2,26},{4,28},{6,30},{8,16},{10,18},{12,20},{14,22},{16,8},... | collective-permute-start | bytes 393224 | tf_op jit(solution)/shard_map/ppermute | solution.py:171
  54.1 1.2 %collective-permute-start.12 = (f32[1,1024]{1,0:T(1,128)S(1)}, f32[1,1024]{1,0:T(1,128)S(1)}, u32[]{:S(2)}, u32[]{:S(2)}) collective-permute-start(f32[1,1024]{1,0:T(1,128)S(1)} %get-tuple-element.44), channel_id=1, source_target_pairs={{0,1},{1,0},{2,3},{3,2},{4,5},{5,4},{6,7},{7,6},{8,9},{9,8},{10,11... | collective-permute-start | bytes 12296 | tf_op jit(solution)/shard_map/ppermute | solution.py:234
  68.7 7.5 %copy-start.5 = (bf16[1,64,1024]{2,1,0:T(8,128)(2,1)S(1)}, bf16[1,64,1024]{2,1,0:T(8,128)(2,1)}, u32[]{:S(2)}) copy-start(bf16[1,64,1024]{2,1,0:T(8,128)(2,1)} %param.4) | copy-start | bytes 393220
  68.8 1.2 %collective-permute-start.13 = (f32[1,1024]{1,0:T(1,128)S(1)}, f32[1,1024]{1,0:T(1,128)S(1)}, u32[]{:S(2)}, u32[]{:S(2)}) collective-permute-start(f32[1,1024]{1,0:T(1,128)S(1)} %get-tuple-element.45), channel_id=1, source_target_pairs={{0,1},{1,0},{2,3},{3,2},{4,5},{5,4},{6,7},{7,6},{8,9},{9,8},{10,11... | collective-permute-start | bytes 12296 | tf_op jit(solution)/shard_map/ppermute | solution.py:234
  72.8 11.0 %all-to-all-start.2 = ((f32[16,8,128]{2,1,0:T(8,128)}), f32[16,8,128]{2,1,0:T(8,128)S(1)}, u32[]{:S(2)}, u32[]{:S(2)}) async-start(f32[16,8,128]{2,1,0:T(8,128)} %rows.3), calls=%async_computation.2 | async-start | bytes 131072 | tf_op jit(solution)/shard_map/all_to_all | solution.py:222
  83.8 1.2 %copy-start.1 = (f32[256,1024]{1,0:T(8,128)S(1)}, f32[256,1024]{1,0:T(8,128)}, u32[]{:S(2)}) copy-start(f32[256,1024]{1,0:T(8,128)} %copy-done) | copy-start | bytes 3145732
  86.2 1.2 %collective-permute-start.14 = (f32[1,1024]{1,0:T(1,128)S(1)}, f32[1,1024]{1,0:T(1,128)S(1)}, u32[]{:S(2)}, u32[]{:S(2)}) collective-permute-start(f32[1,1024]{1,0:T(1,128)S(1)} %get-tuple-element.47), channel_id=1, source_target_pairs={{0,1},{1,0},{2,3},{3,2},{4,5},{5,4},{6,7},{7,6},{8,9},{9,8},{10,11... | collective-permute-start | bytes 12296 | tf_op jit(solution)/shard_map/ppermute | solution.py:234

commit v4 on v2

v4 whole, which is shorter than its diff:
```python
import functools
import math

import jax
import jax.numpy as jnp
from jax import lax
from jax.experimental import pallas as pl
from jax.experimental.pallas import tpu as pltpu
from jax.sharding import PartitionSpec as P

TILE = 512
CAP = 4
ITERS = 3


EPS = 0.02
NEG = -1e30
LN2 = math.log(2.0)
LANES = 128
SUBLANES = 8


def log2(value):
    return jnp.log(value) * (1.0 / LN2)


def log2_sum(values):
    peak = functools.reduce(jnp.maximum, values)
    total = functools.reduce(jnp.add, [jnp.exp2(v - peak) for v in values])
    return peak + log2(total)


def columns_of(width):
    return [slice(low, low + LANES) for low in range(0, width, LANES)]


def row_norms(ref):
    rows, width = ref.shape
    norms = []
    for low in range(0, rows, LANES):
        high = min(low + LANES, rows)
        folded = None
        for cut in columns_of(width):
            part = ref[low:high, cut].astype(jnp.float32)
            folded = part * part if folded is None else folded + part * part
        norms.append(jnp.sum(folded.T, axis=0, keepdims=True) * (1.0 / width))
    return norms[0] if len(norms) == 1 else jnp.concatenate(norms, axis=1)


def fill_scores(first, scale, owner_ref, list_ref, count_ref, piece_refs, pool_ref, joined, out):
    own_rows = piece_refs[0].shape[0]
    for k, ref in enumerate(piece_refs):
        joined[k * own_rows : (k + 1) * own_rows, :] = ref[...]
    dots = lax.dot_general(
        joined[...],
        pool_ref[...],
        (((1,), (1,)), ((), ())),
        preferred_element_type=jnp.float32,
    )
    for k in range(len(piece_refs)):
        tile = lax.div(owner_ref[first + k] * own_rows, TILE)
        rows = slice(k * own_rows, (k + 1) * own_rows)
        for u in range(pool_ref.shape[0] // TILE):
            counted = jnp.int32(0)
            for j in range(CAP):
                hit = (list_ref[0, 0, j, 0] == tile) & (list_ref[0, 0, j, 1] == u)
                counted += jnp.where(hit & (j < count_ref[0, 0]), 1, 0)
            offset = jnp.where(counted > 0, 0.0, NEG)
            cut = slice(u * TILE, (u + 1) * TILE)
            out[rows, cut] = dots[rows, cut] * scale + offset


def row_pass(first, owner_ref, shift, score_ref, held_ref):
    own_rows = held_ref.shape[1]
    across = LANES // own_rows
    for low in range(0, score_ref.shape[0], LANES):
        cuts = columns_of(score_ref.shape[1])
        rows = slice(low, low + LANES)
        peak = functools.reduce(jnp.maximum, [score_ref[rows, c] + shift[:, c] for c in cuts])
        terms = [jnp.exp2(score_ref[rows, c] + shift[:, c] - peak) for c in cuts]
        total = functools.reduce(jnp.add, terms)
        peak, total = peak.T, total.T
        top = jnp.max(peak, axis=0, keepdims=True)
        sums = top + log2(jnp.sum(total * jnp.exp2(peak - top), axis=0, keepdims=True))
        for k in range(across):
            owner = owner_ref[first + low // own_rows + k]
            held_ref[pl.ds(owner, 1), :] = sums[:, k * own_rows : (k + 1) * own_rows]


def copy_out(held_ref, out_ref):
    across = LANES // held_ref.shape[1]
    for line in range(out_ref.shape[1]):
        sources = [held_ref[line * across + k : line * across + k + 1, :] for k in range(across)]
        wide = jnp.concatenate(sources, axis=1)
        out_ref[:, line, :] = jnp.broadcast_to(wide, (out_ref.shape[0], LANES))


def early_kernel(count, scale, unit, owner_ref, list_ref, count_ref, *refs):
    pieces, pool_ref = refs[:count], refs[count]
    score_ref, held_ref, own_norm_ref, pool_norm_ref, joined = refs[count + 1 :]
    fill_scores(0, scale, owner_ref, list_ref, count_ref, pieces, pool_ref, joined, score_ref)
    own_norm_ref[...] = row_norms(pieces[0])
    norm = row_norms(pool_ref)
    pool_norm_ref[...] = norm
    held_ref[...] = jnp.zeros_like(held_ref)
    row_pass(0, owner_ref, norm * (-1.0 / unit), score_ref, held_ref)


def late_kernel(first, count, scale, unit, owner_ref, list_ref, count_ref, *refs):
    pieces, (pool_ref, norm_ref, before_ref) = refs[:count], refs[count : count + 3]
    score_ref, out_ref, joined, held_ref = refs[count + 3 :]
    fill_scores(first, scale, owner_ref, list_ref, count_ref, pieces, pool_ref, joined, score_ref)
    held_ref[...] = before_ref[...]
    row_pass(first, owner_ref, norm_ref[...] * (-1.0 / unit), score_ref, held_ref)
    copy_out(held_ref, out_ref)


def row_kernel(owner_ref, shift_ref, *refs):
    out_ref, held_ref = refs[-2:]
    shift = shift_ref[...]
    first = 0
    for ref in refs[:-2]:
        row_pass(first, owner_ref, shift, ref, held_ref)
        first += ref.shape[0] // held_ref.shape[1]
    copy_out(held_ref, out_ref)


def column_kernel(log_a, unit, owner_ref, value_ref, norm_ref, *refs):
    scores, (out_ref, own_ref, held_ref) = refs[:-3], refs[-3:]
    shift = log_a - log2_sum([value_ref[k] for k in range(value_ref.shape[0])])
    own_rows = held_ref.shape[1]
    across = LANES // own_rows
    for source in range(held_ref.shape[0]):
        line, place = source // across, source % across
        held_ref[source : source + 1, :] = shift[
            line : line + 1, place * own_rows : (place + 1) * own_rows
        ]
    own_ref[...] = held_ref[pl.ds(owner_ref[0], 1), :] * unit + norm_ref[...]
    cuts = columns_of(out_ref.shape[1])
    peaks = [jnp.full((SUBLANES, LANES), NEG, jnp.float32) for _ in cuts]
    spread = []
    k = 0
    for ref in scores:
        for low in range(0, ref.shape[0], LANES):
            rows = [held_ref[pl.ds(owner_ref[k + j], 1), :] for j in range(across)]
            k += across
            row = jnp.concatenate(rows, axis=1)
            spread.append(jnp.broadcast_to(row, (LANES, LANES)).T)
            for c, cut in enumerate(cuts):
                block = ref[low : low + LANES, cut] + spread[-1]
                block = block.reshape(LANES // SUBLANES, SUBLANES, LANES)
                peaks[c] = jnp.maximum(peaks[c], jnp.max(block, axis=0))
    totals = [jnp.zeros((SUBLANES, LANES), jnp.float32) for _ in cuts]
    for ref in scores:
        for low in range(0, ref.shape[0], LANES):
            add = spread.pop(0)
            for c, cut in enumerate(cuts):
                block = ref[low : low + LANES, cut] + add
                block = block.reshape(LANES // SUBLANES, SUBLANES, LANES)
                totals[c] += jnp.sum(jnp.exp2(block - peaks[c]), axis=0)
    for peak, total, cut in zip(peaks, totals, cuts):
        top = jnp.max(peak, axis=0, keepdims=True)
        out_ref[:, cut] = top + log2(jnp.sum(total * jnp.exp2(peak - top), axis=0, keepdims=True))


def call(kernel, shapes, scratch, scalars, arrays, flops, name):
    smem = pl.BlockSpec(memory_space=pltpu.SMEM)
    vmem = pl.BlockSpec(memory_space=pltpu.VMEM)
    moved = sum(a.size * a.dtype.itemsize for a in arrays) + 4 * sum(map(math.prod, shapes))
    return pl.pallas_call(
        kernel,
        out_shape=[jax.ShapeDtypeStruct(s, jnp.float32) for s in shapes],
        in_specs=[smem] * len(scalars) + [vmem] * len(arrays),
        out_specs=[vmem] * len(shapes),
        scratch_shapes=scratch,
        compiler_params=pltpu.CompilerParams(vmem_limit_bytes=3 * moved + (4 << 20)),
        cost_estimate=pl.CostEstimate(flops=flops, bytes_accessed=moved, transcendentals=0),
        name=name,
    )(*scalars, *arrays)


def body(samples, pool, tile_list, tile_count):
    own_rows, width = samples.shape[1:]
    size = lax.axis_size("pool")
    cores = lax.axis_size("samp")
    half_rows = own_rows * size
    pool_rows = pool.shape[0]
    lines = half_rows // LANES
    unit = EPS * LN2
    scale = 2.0 / (width * unit)
    log_a = -math.log2(half_rows * cores)
    log_b = -math.log2(pool_rows * size)
    own = samples.reshape(own_rows, width)

    def swap(value, masks):
        pairs = [
            (i * cores + c, (i ^ masks[c % 2]) * cores + c)
            for i in range(size)
            for c in range(cores)
        ]
        return lax.ppermute(value, ("pool", "samp"), pairs)

    def side_a(value):
        return swap(value, (1, 2))

    def side_b(value):
        return swap(value, (2, 1))

    def far(value, mask):
        return swap(value, (mask, mask))

    far12, far4 = far(own, 12), far(own, 4)
    a, b = side_a(own), side_b(own)
    corner = side_b(a)
    far8 = far(far12, 4)
    a4, b4 = side_a(far4), side_b(far4)
    a12, b12 = side_a(far12), side_b(far12)
    a8, b8 = side_a(far8), side_b(far8)
    corner12, corner4 = far(corner, 12), far(corner, 4)
    corner8 = far(corner12, 4)
    early = [own, a, b, corner, far4, far12, far8, a4, b4, a12, b12, b8]
    late = [a8, corner4, corner12, corner8]
    mask_a = 1 + lax.axis_index("samp") % 2
    mask_b = 3 - mask_a
    masks = [0, mask_a, mask_b, 3, 4, 12, 8, 4 + mask_a, 4 + mask_b, 12 + mask_a, 12 + mask_b]
    masks += [8 + mask_b, 8 + mask_a, 7, 15, 11]
    step = 16
    while step < size:
        late += [far(piece, step) for piece in early + late]
        masks += [m + step for m in masks]
        step *= 2
    owner = lax.axis_index("pool").astype(jnp.int32) ^ jnp.stack([jnp.int32(m) for m in masks])
    scalars = [owner, tile_list, tile_count]

    count = len(early)
    score0, held, own_norm, pool_norm = call(
        functools.partial(early_kernel, count, scale, unit),
        [(count * own_rows, pool_rows), (size, own_rows), (1, own_rows), (1, pool_rows)],
        [pltpu.VMEM((count * own_rows, width), samples.dtype)],
        scalars,
        early + [pool],
        2 * count * own_rows * pool_rows * width,
        "early_scores",
    )
    *late, score0, held, own_norm, pool_norm = lax.optimization_barrier(
        (*late, score0, held, own_norm, pool_norm)
    )
    rest = len(late)
    score1, value = call(
        functools.partial(late_kernel, count, rest, scale, unit),
        [(rest * own_rows, pool_rows), (size, lines, LANES)],
        [
            pltpu.VMEM((rest * own_rows, width), samples.dtype),
            pltpu.VMEM((size, own_rows), jnp.float32),
        ],
        scalars,
        late + [pool, pool_norm, held],
        2 * rest * own_rows * pool_rows * width,
        "late_scores",
    )
    scores = [score0, score1]
    flops = 8 * half_rows * pool_rows
    held = [pltpu.VMEM((size, own_rows), jnp.float32)]
    for iteration in range(ITERS):
        if iteration > 0:
            shapes = [(size, lines, LANES)]
            (value,) = call(row_kernel, shapes, held, [owner], [shift] + scores, flops, "rows")
        value = lax.all_to_all(value, "pool", 0, 0, tiled=True)
        value, sample_potential = call(
            functools.partial(column_kernel, log_a, unit),
            [(1, pool_rows), (1, own_rows)],
            held,
            [owner],
            [value, own_norm] + scores,
            flops,
            "columns",
        )
        pairs = [(i, i ^ 1) for i in range(cores)]
        shift = log_b - log2_sum([value, lax.ppermute(value, "samp", pairs)])
    return sample_potential, (shift * unit + pool_norm).reshape(pool_rows)


def solution(mesh):
    placed = (
        P(("grp", "samp"), "pool", None),
        P(("grp", "pool"), None),
        P(("grp", "samp"), "pool", None, None),
        P(("grp", "samp"), "pool"),
    )
    return jax.shard_map(
        body,
        mesh=mesh,
        in_specs=placed,
        out_specs=(P(("grp", "samp"), "pool"), P(("grp", "pool"))),
        check_vma=False,
    )
```

time: 91.4 us -> 82.3 us (0.900)
  waiting for transfers between devices: 28.5 us -> 8.07 us
  blocking collectives: 23.3 us -> 34 us
  starting transfers between devices: 14.6 us -> 20.7 us
  other arithmetic: 5.15 us -> 0.69 us
    ppermute x7 -> x15, waiting for transfers between devices: 18.2 us -> 4.58 us  [swap(): return lax.ppermute(value, ('pool', 'samp'), pairs)]
    all_to_all x2 -> x3, blocking collectives: 23.3 us -> 34 us  [body(): value = lax.all_to_all(value, 'pool', 0, 0, tiled=True)]
    ppermute x7 -> x15, starting transfers between devices: 10.8 us -> 20.7 us  [swap(): return lax.ppermute(value, ('pool', 'samp'), pairs)]
    all_to_all x1 -> x0, waiting for transfers between devices: 7.36 us -> none  [body(): value = lax.all_to_all(value, 'pool', 0, 0, tiled=True)]
    all_to_all x1 -> x0, starting transfers between devices: 3.5 us -> none  [body(): value = lax.all_to_all(value, 'pool', 0, 0, tiled=True)]
    reduce_sum x2 -> x0, other arithmetic: 2.2 us -> none  [the longest x1 2.07 us: body(): pool_norm = jnp.sum(jnp.square(pool.astype(jnp.float32)), axis=1) / width]
    unnamed x10 -> x5, local copies, waits for them, and re-layouts: 1.25 us -> 3.25 us
    slice x2 -> x0, local copies, waits for them, and re-layouts: 1.93 us -> none  [the longest x1 0.97 us: body(): low = swap(by_x[:half], 2)]
  transfers between devices with their start and end apart: 11 -> 18, of which waited for: 10 -> 5; matrix products, arithmetic and copies ran while one was open for 5% -> 1% of each run, Pallas kernels for 5% -> 4%
where the time goes in v4:
time: 82.3 us; the launch traced here: 82 us
  blocking collectives  34 us (41%)
  starting transfers between devices  20.7 us (25%)
  Pallas kernels  13.8 us (17%)
  waiting for transfers between devices  8.07 us (10%)
  local copies, waits for them, and re-layouts  3.35 us (4%)
  between operations  1.36 us (2%)
    all_to_all x3, blocking collectives, body(): value = lax.all_to_all(value, 'pool', 0, 0, tiled=True)  34 us
    ppermute x15, starting transfers between devices, swap(): return lax.ppermute(value, ('pool', 'samp'), pairs)  20.7 us
    pallas_call x7, Pallas kernels, call(): pl.pallas_call(kernel, out_shape=[jax.ShapeDtypeStruct(s, jnp.float32) fo...  13.8 us
    ppermute x15, waiting for transfers between devices, swap(): return lax.ppermute(value, ('pool', 'samp'), pairs)  4.58 us
    ppermute x3, waiting for transfers between devices, body(): shift = log_b - log2_sum([value, lax.ppermute(value, 'samp', pairs)])  3.49 us
    unnamed x5, local copies, waits for them, and re-layouts  3.25 us
  transfers between devices with their start and end apart: 18, of which 5 were waited for; matrix products, arithmetic and copies ran while one was open for 1% of the time, Pallas kernels for 4%

profile of v4, /device:TPU:0, one launch (start us, length us, event | category | flops | bytes accessed | tf_op | source)
XLA Modules:
  0.0 82.0 jit_solution(15971700927570471906)
XLA Ops:
  0.6 5.1 %collective-permute-start = (bf16[64,1024]{1,0:T(8,128)(2,1)}, bf16[64,1024]{1,0:T(8,128)(2,1)S(1)}, u32[]{:S(2)}, u32[]{:S(2)}) collective-permute-start(bf16[64,1024]{1,0:T(8,128)(2,1)} %bitcast.10), channel_id=1, source_target_pairs={{0,24},{1,25},{2,26},{3,27},{4,28},{5,29},{6,30},{7,31},{8,16},{9,... | collective-permute-start | bytes 393224 | tf_op jit(solution)/shard_map/ppermute | solution.py:201
  5.7 1.5 %collective-permute-start.3 = (bf16[64,1024]{1,0:T(8,128)(2,1)}, bf16[64,1024]{1,0:T(8,128)(2,1)S(1)}, u32[]{:S(2)}, u32[]{:S(2)}) collective-permute-start(bf16[64,1024]{1,0:T(8,128)(2,1)} %bitcast.11), channel_id=1, source_target_pairs={{0,2},{1,5},{2,0},{3,7},{4,6},{5,1},{6,4},{7,3},{8,10},{9,13},{10,... | collective-permute-start | bytes 393224 | tf_op jit(solution)/shard_map/ppermute | solution.py:201
  7.2 1.5 %collective-permute-start.8 = (bf16[64,1024]{1,0:T(8,128)(2,1)}, bf16[64,1024]{1,0:T(8,128)(2,1)S(1)}, u32[]{:S(2)}, u32[]{:S(2)}) collective-permute-start(bf16[64,1024]{1,0:T(8,128)(2,1)} %bitcast.13), channel_id=1, source_target_pairs={{0,4},{1,3},{2,6},{3,1},{4,0},{5,7},{6,2},{7,5},{8,12},{9,11},{10,... | collective-permute-start | bytes 393224 | tf_op jit(solution)/shard_map/ppermute | solution.py:201
  8.8 1.6 %collective-permute-done.refs_5_ = bf16[64,1024]{1,0:T(8,128)(2,1)S(1)} collective-permute-done((bf16[64,1024]{1,0:T(8,128)(2,1)}, bf16[64,1024]{1,0:T(8,128)(2,1)S(1)}, u32[]{:S(2)}, u32[]{:S(2)}) %collective-permute-start) | collective-permute-done | bytes 131104 | tf_op jit(solution)/shard_map/ppermute | solution.py:201
  10.3 1.6 %collective-permute-start.1 = (bf16[64,1024]{1,0:T(8,128)(2,1)S(1)}, bf16[64,1024]{1,0:T(8,128)(2,1)S(1)}, u32[]{:S(2)}, u32[]{:S(2)}) collective-permute-start(bf16[64,1024]{1,0:T(8,128)(2,1)S(1)} %collective-permute-done.refs_5_), channel_id=1, source_target_pairs={{0,8},{1,9},{2,10},{3,11},{4,12},{5,13},{6,14},{7,15},{8,0},{9,1},... | collective-permute-start | bytes 393224 | tf_op jit(solution)/shard_map/ppermute | solution.py:201
  12.0 1.5 %collective-permute-start.12 = (bf16[64,1024]{1,0:T(8,128)(2,1)S(1)}, bf16[64,1024]{1,0:T(8,128)(2,1)S(1)}, u32[]{:S(2)}, u32[]{:S(2)}) collective-permute-start(bf16[64,1024]{1,0:T(8,128)(2,1)S(1)} %collective-permute-done.refs_5_), channel_id=1, source_target_pairs={{0,2},{1,5},{2,0},{3,7},{4,6},{5,1},{6,4},{7,3},{8,10},{9,13},{10,... | collective-permute-start | bytes 393224 | tf_op jit(solution)/shard_map/ppermute | solution.py:201
  13.5 1.5 %collective-permute-start.4 = (bf16[64,1024]{1,0:T(8,128)(2,1)S(1)}, bf16[64,1024]{1,0:T(8,128)(2,1)S(1)}, u32[]{:S(2)}, u32[]{:S(2)}) collective-permute-start(bf16[64,1024]{1,0:T(8,128)(2,1)S(1)} %collective-permute-done.3.refs_1_), channel_id=1, source_target_pairs={{0,4},{1,3},{2,6},{3,1},{4,0},{5,7},{6,2},{7,5},{8,12},{9,11},{10,... | collective-permute-start | bytes 393224 | tf_op jit(solution)/shard_map/ppermute | solution.py:201
  17.6 1.5 %collective-permute-start.11 = (bf16[64,1024]{1,0:T(8,128)(2,1)S(1)}, bf16[64,1024]{1,0:T(8,128)(2,1)S(1)}, u32[]{:S(2)}, u32[]{:S(2)}) collective-permute-start(bf16[64,1024]{1,0:T(8,128)(2,1)S(1)} %collective-permute-done.9.refs_4_), channel_id=1, source_target_pairs={{0,4},{1,3},{2,6},{3,1},{4,0},{5,7},{6,2},{7,5},{8,12},{9,11},{10,... | collective-permute-start | bytes 393224 | tf_op jit(solution)/shard_map/ppermute | solution.py:201
  19.7 2.4 %collective-permute-start.6 = (bf16[64,1024]{1,0:T(8,128)(2,1)S(1)}, bf16[64,1024]{1,0:T(8,128)(2,1)S(1)}, u32[]{:S(2)}, u32[]{:S(2)}) collective-permute-start(bf16[64,1024]{1,0:T(8,128)(2,1)S(1)} %collective-permute-done.4.refs_3_), channel_id=1, source_target_pairs={{0,24},{1,25},{2,26},{3,27},{4,28},{5,29},{6,30},{7,31},{8,16},{9,... | collective-permute-start | bytes 393224 | tf_op jit(solution)/shard_map/ppermute | solution.py:201
  22.1 1.3 %collective-permute-start.2 = (bf16[64,1024]{1,0:T(8,128)(2,1)S(1)}, bf16[64,1024]{1,0:T(8,128)(2,1)S(1)}, u32[]{:S(2)}, u32[]{:S(2)}) collective-permute-start(bf16[64,1024]{1,0:T(8,128)(2,1)S(1)} %collective-permute-done.1.refs_6_), channel_id=1, source_target_pairs={{0,2},{1,5},{2,0},{3,7},{4,6},{5,1},{6,4},{7,3},{8,10},{9,13},{10,... | collective-permute-start | bytes 393224 | tf_op jit(solution)/shard_map/ppermute | solution.py:201
  24.5 3.0 %collective-permute-done.6.refs_2_ = bf16[64,1024]{1,0:T(8,128)(2,1)S(1)} collective-permute-done((bf16[64,1024]{1,0:T(8,128)(2,1)S(1)}, bf16[64,1024]{1,0:T(8,128)(2,1)S(1)}, u32[]{:S(2)}, u32[]{:S(2)}) %collective-permute-start.6) | collective-permute-done | bytes 131104 | tf_op jit(solution)/shard_map/ppermute | solution.py:201
  27.5 1.6 %copy-done = bf16[1024,1024]{1,0:T(8,128)(2,1)S(1)} copy-done((bf16[1024,1024]{1,0:T(8,128)(2,1)S(1)}, bf16[1024,1024]{1,0:T(8,128)(2,1)}, u32[]{:S(2)}) %copy-start) | copy-done | bytes 2097176
  30.0 3.1 %early_scores.1 = (f32[768,1024]{1,0:T(8,128)S(1)}, f32[16,64]{1,0:T(8,128)S(1)}, f32[1,64]{1,0:T(1,128)S(1)}, f32[1,1024]{1,0:T(1,128)S(1)}) custom-call(s32[16]{0:T(128)S(1)} %broadcast_xor_fusion.owner_ref, s32[1,1,4,2]{3,2,1,0:T(4,128)S(1)} %copy.7.list_ref, s32[1,1]{1,0:T(1,128)S(6)} %copy.8.count_ref, bf16[64,1024]{1,0:T(8,128)(2,1)S(1)} %bitcast.14, ...), custom_call_target="tpu_custom_call" | custom-call | flops 1610612736 | bytes 6824192 | tf_op jit(solution)/shard_map/early_scores/pallas_call | solution.py:170
  33.1 1.7 %late_scores.1 = (f32[256,1024]{1,0:T(8,128)S(1)}, f32[16,8,128]{2,1,0:T(8,128)S(1)}) custom-call(s32[16]{0:T(128)S(1)} %broadcast_xor_fusion.owner_ref, s32[1,1,4,2]{3,2,1,0:T(4,128)S(1)} %copy.7.list_ref, s32[1,1]{1,0:T(1,128)S(6)} %copy.8.count_ref, bf16[64,1024]{1,0:T(8,128)(2,1)S(1)} %collective-permute-done.2.refs_0_, ...), custom_call_target="tpu_custom_call" | custom-call | flops 536870912 | bytes 3743744 | tf_op jit(solution)/shard_map/late_scores/pallas_call | solution.py:170
  34.8 13.7 %all_to_all.15.value_ref = f32[16,8,128]{2,1,0:T(8,128)S(1)} all-to-all(f32[16,8,128]{2,1,0:T(8,128)S(1)} %get-tuple-element.30), channel_id=1, replica_groups=mesh['grp'=1,'pool'=16,'samp'=2] {'pool'}, dimensions={0} | all-to-all | bytes 131072 | tf_op jit(solution)/shard_map/all_to_all | solution.py:268
  48.5 1.9 %columns.3 = (f32[1,1024]{1,0:T(1,128)S(1)}, f32[1,64]{1,0:T(1,128)}) custom-call(s32[16]{0:T(128)S(1)} %broadcast_xor_fusion.owner_ref, f32[16,8,128]{2,1,0:T(8,128)S(1)} %all_to_all.15.value_ref, f32[1,64]{1,0:T(1,128)S(1)} %get-tuple-element.31.norm_ref, f32[768,1024]{1,0:T(8,128)S(1)} %get-tuple-element.32.refs_0_, f32[256,1024]{1,0:T(8,128)S(1)} %get-tuple-element.33.refs_1_), custom_call_target="tpu_custom_call" | custom-call | flops 8388608 | bytes 4264448 | tf_op jit(solution)/shard_map/columns/pallas_call | solution.py:170
  50.4 1.2 %collective-permute-done.15 = f32[1,1024]{1,0:T(1,128)S(1)} collective-permute-done((f32[1,1024]{1,0:T(1,128)S(1)}, f32[1,1024]{1,0:T(1,128)S(1)}, u32[]{:S(2)}, u32[]{:S(2)}) %collective-permute-start.15) | collective-permute-done | bytes 4128 | tf_op jit(solution)/shard_map/ppermute | solution.py:279
  51.6 1.6 %rows.2 = f32[16,8,128]{2,1,0:T(8,128)S(1)} custom-call(s32[16]{0:T(128)S(1)} %broadcast_xor_fusion.owner_ref, f32[1,1024]{1,0:T(1,128)S(1)} %add_subtract_fusion.1.shift_ref, f32[768,1024]{1,0:T(8,128)S(1)} %get-tuple-element.32.refs_0_, f32[256,1024]{1,0:T(8,128)S(1)} %get-tuple-element.33.refs_1_), custom_call_target="tpu_custom_call" | custom-call | flops 8388608 | bytes 4263936 | tf_op jit(solution)/shard_map/rows/pallas_call | solution.py:170
  53.3 10.1 %all_to_all.16.value_ref = f32[16,8,128]{2,1,0:T(8,128)S(1)} all-to-all(f32[16,8,128]{2,1,0:T(8,128)S(1)} %rows.2), channel_id=1, replica_groups=mesh['grp'=1,'pool'=16,'samp'=2] {'pool'}, dimensions={0} | all-to-all | bytes 131072 | tf_op jit(solution)/shard_map/all_to_all | solution.py:268
  63.4 1.9 %columns.4 = (f32[1,1024]{1,0:T(1,128)S(1)}, f32[1,64]{1,0:T(1,128)}) custom-call(s32[16]{0:T(128)S(1)} %broadcast_xor_fusion.owner_ref, f32[16,8,128]{2,1,0:T(8,128)S(1)} %all_to_all.16.value_ref, f32[1,64]{1,0:T(1,128)S(1)} %get-tuple-element.31.norm_ref, f32[768,1024]{1,0:T(8,128)S(1)} %get-tuple-element.32.refs_0_, f32[256,1024]{1,0:T(8,128)S(1)} %get-tuple-element.33.refs_1_), custom_call_target="tpu_custom_call" | custom-call | flops 8388608 | bytes 4264448 | tf_op jit(solution)/shard_map/columns/pallas_call | solution.py:170
  65.3 1.2 %collective-permute-done.16 = f32[1,1024]{1,0:T(1,128)S(1)} collective-permute-done((f32[1,1024]{1,0:T(1,128)S(1)}, f32[1,1024]{1,0:T(1,128)S(1)}, u32[]{:S(2)}, u32[]{:S(2)}) %collective-permute-start.16) | collective-permute-done | bytes 4128 | tf_op jit(solution)/shard_map/ppermute | solution.py:279
  66.5 1.6 %rows.3 = f32[16,8,128]{2,1,0:T(8,128)S(1)} custom-call(s32[16]{0:T(128)S(1)} %broadcast_xor_fusion.owner_ref, f32[1,1024]{1,0:T(1,128)S(1)} %add_subtract_fusion.shift_ref, f32[768,1024]{1,0:T(8,128)S(1)} %get-tuple-element.32.refs_0_, f32[256,1024]{1,0:T(8,128)S(1)} %get-tuple-element.33.refs_1_), custom_call_target="tpu_custom_call" | custom-call | flops 8388608 | bytes 4263936 | tf_op jit(solution)/shard_map/rows/pallas_call | solution.py:170
  68.1 10.1 %all_to_all.17.value_ref = f32[16,8,128]{2,1,0:T(8,128)S(1)} all-to-all(f32[16,8,128]{2,1,0:T(8,128)S(1)} %rows.3), channel_id=1, replica_groups=mesh['grp'=1,'pool'=16,'samp'=2] {'pool'}, dimensions={0} | all-to-all | bytes 131072 | tf_op jit(solution)/shard_map/all_to_all | solution.py:268
  78.3 1.9 %columns.5 = (f32[1,1024]{1,0:T(1,128)S(1)}, f32[1,64]{1,0:T(1,128)}) custom-call(s32[16]{0:T(128)S(1)} %broadcast_xor_fusion.owner_ref, f32[16,8,128]{2,1,0:T(8,128)S(1)} %all_to_all.17.value_ref, f32[1,64]{1,0:T(1,128)S(1)} %get-tuple-element.31.norm_ref, f32[768,1024]{1,0:T(8,128)S(1)} %get-tuple-element.32.refs_0_, f32[256,1024]{1,0:T(8,128)S(1)} %get-tuple-element.33.refs_1_), custom_call_target="tpu_custom_call" | custom-call | flops 8388608 | bytes 4264448 | tf_op jit(solution)/shard_map/columns/pallas_call | solution.py:170
  (32 shorter events, 6.4 us)
Async XLA Ops:
  0.6 9.7 %collective-permute-start = (bf16[64,1024]{1,0:T(8,128)(2,1)}, bf16[64,1024]{1,0:T(8,128)(2,1)S(1)}, u32[]{:S(2)}, u32[]{:S(2)}) collective-permute-start(bf16[64,1024]{1,0:T(8,128)(2,1)} %bitcast.10), channel_id=1, source_target_pairs={{0,24},{1,25},{2,26},{3,27},{4,28},{5,29},{6,30},{7,31},{8,16},{9,... | collective-permute-start | bytes 393224 | tf_op jit(solution)/shard_map/ppermute | solution.py:201
  5.7 7.7 %collective-permute-start.3 = (bf16[64,1024]{1,0:T(8,128)(2,1)}, bf16[64,1024]{1,0:T(8,128)(2,1)S(1)}, u32[]{:S(2)}, u32[]{:S(2)}) collective-permute-start(bf16[64,1024]{1,0:T(8,128)(2,1)} %bitcast.11), channel_id=1, source_target_pairs={{0,2},{1,5},{2,0},{3,7},{4,6},{5,1},{6,4},{7,3},{8,10},{9,13},{10,... | collective-permute-start | bytes 393224 | tf_op jit(solution)/shard_map/ppermute | solution.py:201
  7.2 9.3 %collective-permute-start.9 = (bf16[64,1024]{1,0:T(8,128)(2,1)}, bf16[64,1024]{1,0:T(8,128)(2,1)S(1)}, u32[]{:S(2)}, u32[]{:S(2)}) collective-permute-start(bf16[64,1024]{1,0:T(8,128)(2,1)} %bitcast.12), channel_id=1, source_target_pairs={{0,8},{1,9},{2,10},{3,11},{4,12},{5,13},{6,14},{7,15},{8,0},{9,1},... | collective-permute-start | bytes 393224 | tf_op jit(solution)/shard_map/ppermute | solution.py:201
  7.2 9.9 %collective-permute-start.8 = (bf16[64,1024]{1,0:T(8,128)(2,1)}, bf16[64,1024]{1,0:T(8,128)(2,1)S(1)}, u32[]{:S(2)}, u32[]{:S(2)}) collective-permute-start(bf16[64,1024]{1,0:T(8,128)(2,1)} %bitcast.13), channel_id=1, source_target_pairs={{0,4},{1,3},{2,6},{3,1},{4,0},{5,7},{6,2},{7,5},{8,12},{9,11},{10,... | collective-permute-start | bytes 393224 | tf_op jit(solution)/shard_map/ppermute | solution.py:201
  10.3 7.3 %collective-permute-start.1 = (bf16[64,1024]{1,0:T(8,128)(2,1)S(1)}, bf16[64,1024]{1,0:T(8,128)(2,1)S(1)}, u32[]{:S(2)}, u32[]{:S(2)}) collective-permute-start(bf16[64,1024]{1,0:T(8,128)(2,1)S(1)} %collective-permute-done.refs_5_), channel_id=1, source_target_pairs={{0,8},{1,9},{2,10},{3,11},{4,12},{5,13},{6,14},{7,15},{8,0},{9,1},... | collective-permute-start | bytes 393224 | tf_op jit(solution)/shard_map/ppermute | solution.py:201
  12.0 7.2 %collective-permute-start.12 = (bf16[64,1024]{1,0:T(8,128)(2,1)S(1)}, bf16[64,1024]{1,0:T(8,128)(2,1)S(1)}, u32[]{:S(2)}, u32[]{:S(2)}) collective-permute-start(bf16[64,1024]{1,0:T(8,128)(2,1)S(1)} %collective-permute-done.refs_5_), channel_id=1, source_target_pairs={{0,2},{1,5},{2,0},{3,7},{4,6},{5,1},{6,4},{7,3},{8,10},{9,13},{10,... | collective-permute-start | bytes 393224 | tf_op jit(solution)/shard_map/ppermute | solution.py:201
  13.5 6.2 %collective-permute-start.4 = (bf16[64,1024]{1,0:T(8,128)(2,1)S(1)}, bf16[64,1024]{1,0:T(8,128)(2,1)S(1)}, u32[]{:S(2)}, u32[]{:S(2)}) collective-permute-start(bf16[64,1024]{1,0:T(8,128)(2,1)S(1)} %collective-permute-done.3.refs_1_), channel_id=1, source_target_pairs={{0,4},{1,3},{2,6},{3,1},{4,0},{5,7},{6,2},{7,5},{8,12},{9,11},{10,... | collective-permute-start | bytes 393224 | tf_op jit(solution)/shard_map/ppermute | solution.py:201
  16.5 5.6 %collective-permute-start.13 = (bf16[64,1024]{1,0:T(8,128)(2,1)S(1)}, bf16[64,1024]{1,0:T(8,128)(2,1)S(1)}, u32[]{:S(2)}, u32[]{:S(2)}) collective-permute-start(bf16[64,1024]{1,0:T(8,128)(2,1)S(1)} %collective-permute-done.refs_5_), channel_id=1, source_target_pairs={{0,4},{1,3},{2,6},{3,1},{4,0},{5,7},{6,2},{7,5},{8,12},{9,11},{10,... | collective-permute-start | bytes 393224 | tf_op jit(solution)/shard_map/ppermute | solution.py:201
  17.1 6.3 %collective-permute-start.10 = (bf16[64,1024]{1,0:T(8,128)(2,1)S(1)}, bf16[64,1024]{1,0:T(8,128)(2,1)S(1)}, u32[]{:S(2)}, u32[]{:S(2)}) collective-permute-start(bf16[64,1024]{1,0:T(8,128)(2,1)S(1)} %collective-permute-done.9.refs_4_), channel_id=1, source_target_pairs={{0,2},{1,5},{2,0},{3,7},{4,6},{5,1},{6,4},{7,3},{8,10},{9,13},{10,... | collective-permute-start | bytes 393224 | tf_op jit(solution)/shard_map/ppermute | solution.py:201
  17.6 9.8 %collective-permute-start.11 = (bf16[64,1024]{1,0:T(8,128)(2,1)S(1)}, bf16[64,1024]{1,0:T(8,128)(2,1)S(1)}, u32[]{:S(2)}, u32[]{:S(2)}) collective-permute-start(bf16[64,1024]{1,0:T(8,128)(2,1)S(1)} %collective-permute-done.9.refs_4_), channel_id=1, source_target_pairs={{0,4},{1,3},{2,6},{3,1},{4,0},{5,7},{6,2},{7,5},{8,12},{9,11},{10,... | collective-permute-start | bytes 393224 | tf_op jit(solution)/shard_map/ppermute | solution.py:201
  19.2 8.3 %collective-permute-start.14 = (bf16[64,1024]{1,0:T(8,128)(2,1)S(1)}, bf16[64,1024]{1,0:T(8,128)(2,1)S(1)}, u32[]{:S(2)}, u32[]{:S(2)}) collective-permute-start(bf16[64,1024]{1,0:T(8,128)(2,1)S(1)} %collective-permute-done.1.refs_6_), channel_id=1, source_target_pairs={{0,4},{1,3},{2,6},{3,1},{4,0},{5,7},{6,2},{7,5},{8,12},{9,11},{10,... | collective-permute-start | bytes 393224 | tf_op jit(solution)/shard_map/ppermute | solution.py:201
  19.7 7.8 %collective-permute-start.6 = (bf16[64,1024]{1,0:T(8,128)(2,1)S(1)}, bf16[64,1024]{1,0:T(8,128)(2,1)S(1)}, u32[]{:S(2)}, u32[]{:S(2)}) collective-permute-start(bf16[64,1024]{1,0:T(8,128)(2,1)S(1)} %collective-permute-done.4.refs_3_), channel_id=1, source_target_pairs={{0,24},{1,25},{2,26},{3,27},{4,28},{5,29},{6,30},{7,31},{8,16},{9,... | collective-permute-start | bytes 393224 | tf_op jit(solution)/shard_map/ppermute | solution.py:201
  22.1 11.0 %collective-permute-start.2 = (bf16[64,1024]{1,0:T(8,128)(2,1)S(1)}, bf16[64,1024]{1,0:T(8,128)(2,1)S(1)}, u32[]{:S(2)}, u32[]{:S(2)}) collective-permute-start(bf16[64,1024]{1,0:T(8,128)(2,1)S(1)} %collective-permute-done.1.refs_6_), channel_id=1, source_target_pairs={{0,2},{1,5},{2,0},{3,7},{4,6},{5,1},{6,4},{7,3},{8,10},{9,13},{10,... | collective-permute-start | bytes 393224 | tf_op jit(solution)/shard_map/ppermute | solution.py:201
  23.4 9.7 %collective-permute-start.5 = (bf16[64,1024]{1,0:T(8,128)(2,1)S(1)}, bf16[64,1024]{1,0:T(8,128)(2,1)S(1)}, u32[]{:S(2)}, u32[]{:S(2)}) collective-permute-start(bf16[64,1024]{1,0:T(8,128)(2,1)S(1)} %collective-permute-done.4.refs_3_), channel_id=1, source_target_pairs={{0,8},{1,9},{2,10},{3,11},{4,12},{5,13},{6,14},{7,15},{8,0},{9,1},... | collective-permute-start | bytes 393224 | tf_op jit(solution)/shard_map/ppermute | solution.py:201
  27.4 5.6 %collective-permute-start.7 = (bf16[64,1024]{1,0:T(8,128)(2,1)S(1)}, bf16[64,1024]{1,0:T(8,128)(2,1)S(1)}, u32[]{:S(2)}, u32[]{:S(2)}) collective-permute-start(bf16[64,1024]{1,0:T(8,128)(2,1)S(1)} %collective-permute-done.6.refs_2_), channel_id=1, source_target_pairs={{0,8},{1,9},{2,10},{3,11},{4,12},{5,13},{6,14},{7,15},{8,0},{9,1},... | collective-permute-start | bytes 393224 | tf_op jit(solution)/shard_map/ppermute | solution.py:201
  27.5 1.6 %copy-start = (bf16[1024,1024]{1,0:T(8,128)(2,1)S(1)}, bf16[1024,1024]{1,0:T(8,128)(2,1)}, u32[]{:S(2)}) copy-start(bf16[1024,1024]{1,0:T(8,128)(2,1)} %refs_4_.1) | copy-start | bytes 6291460
  29.0 0.9 %copy-start.1 = (bf16[1,64,1024]{2,1,0:T(8,128)(2,1)S(1)}, bf16[1,64,1024]{2,1,0:T(8,128)(2,1)}, u32[]{:S(2)}) copy-start(bf16[1,64,1024]{2,1,0:T(8,128)(2,1)} %param.4) | copy-start | bytes 393220
  50.4 1.2 %collective-permute-start.15 = (f32[1,1024]{1,0:T(1,128)S(1)}, f32[1,1024]{1,0:T(1,128)S(1)}, u32[]{:S(2)}, u32[]{:S(2)}) collective-permute-start(f32[1,1024]{1,0:T(1,128)S(1)} %get-tuple-element.34), channel_id=1, source_target_pairs={{0,1},{1,0},{2,3},{3,2},{4,5},{5,4},{6,7},{7,6},{8,9},{9,8},{10,11... | collective-permute-start | bytes 12296 | tf_op jit(solution)/shard_map/ppermute | solution.py:279
  65.3 1.2 %collective-permute-start.16 = (f32[1,1024]{1,0:T(1,128)S(1)}, f32[1,1024]{1,0:T(1,128)S(1)}, u32[]{:S(2)}, u32[]{:S(2)}) collective-permute-start(f32[1,1024]{1,0:T(1,128)S(1)} %get-tuple-element.35), channel_id=1, source_target_pairs={{0,1},{1,0},{2,3},{3,2},{4,5},{5,4},{6,7},{7,6},{8,9},{9,8},{10,11... | collective-permute-start | bytes 12296 | tf_op jit(solution)/shard_map/ppermute | solution.py:279
  80.2 1.2 %collective-permute-start.17 = (f32[1,1024]{1,0:T(1,128)S(1)}, f32[1,1024]{1,0:T(1,128)S(1)}, u32[]{:S(2)}, u32[]{:S(2)}) collective-permute-start(f32[1,1024]{1,0:T(1,128)S(1)} %get-tuple-element.37), channel_id=1, source_target_pairs={{0,1},{1,0},{2,3},{3,2},{4,5},{5,4},{6,7},{7,6},{8,9},{9,8},{10,11... | collective-permute-start | bytes 12296 | tf_op jit(solution)/shard_map/ppermute | solution.py:279

commit v5 on v4

v5 whole, which is shorter than its diff:
```python
import functools
import math

import jax
import jax.numpy as jnp
from jax import lax
from jax.experimental import pallas as pl
from jax.experimental.pallas import tpu as pltpu
from jax.sharding import PartitionSpec as P

TILE = 512
CAP = 4
ITERS = 3


EPS = 0.02
NEG = -1e30
LN2 = math.log(2.0)
LANES = 128
SUBLANES = 8


def log2(value):
    return jnp.log(value) * (1.0 / LN2)


def log2_sum(values):
    peak = functools.reduce(jnp.maximum, values)
    total = functools.reduce(jnp.add, [jnp.exp2(v - peak) for v in values])
    return peak + log2(total)


def columns_of(width):
    return [slice(low, low + LANES) for low in range(0, width, LANES)]


def row_norms(ref):
    rows, width = ref.shape
    norms = []
    for low in range(0, rows, LANES):
        high = min(low + LANES, rows)
        folded = None
        for cut in columns_of(width):
            part = ref[low:high, cut].astype(jnp.float32)
            folded = part * part if folded is None else folded + part * part
        norms.append(jnp.sum(folded.T, axis=0, keepdims=True) * (1.0 / width))
    return norms[0] if len(norms) == 1 else jnp.concatenate(norms, axis=1)


def fill_scores(first, size, scale, code_ref, piece_refs, pool_ref, joined, out):
    own_rows = piece_refs[0].shape[0]
    for k, ref in enumerate(piece_refs):
        joined[k * own_rows : (k + 1) * own_rows, :] = ref[...]
    dots = lax.dot_general(
        joined[...],
        pool_ref[...],
        (((1,), (1,)), ((), ())),
        preferred_element_type=jnp.float32,
    )
    for k in range(len(piece_refs)):
        rows = slice(k * own_rows, (k + 1) * own_rows)
        for u in range(pool_ref.shape[0] // TILE):
            offset = jnp.where((code_ref[first + k] & (size << u)) != 0, 0.0, NEG)
            cut = slice(u * TILE, (u + 1) * TILE)
            out[rows, cut] = dots[rows, cut] * scale + offset


def diagonal(size):
    rows = lax.broadcasted_iota(jnp.int32, (size, size), 0)
    return rows == lax.broadcasted_iota(jnp.int32, (size, size), 1)


def row_pass(first, code_ref, shift, score_ref, held_ref):
    size, own_rows = held_ref.shape
    eye = diagonal(own_rows)
    for k in range(score_ref.shape[0] // own_rows):
        block = score_ref[k * own_rows : (k + 1) * own_rows, :] + shift
        peak = jnp.max(block, axis=1, keepdims=True)
        total = jnp.sum(jnp.exp2(block - peak), axis=1, keepdims=True)
        sums = jnp.sum(jnp.where(eye, peak + log2(total), 0.0), axis=0, keepdims=True)
        held_ref[pl.ds(code_ref[first + k] & (size - 1), 1), :] = sums


def copy_out(held_ref, out_ref):
    across = LANES // held_ref.shape[1]
    for line in range(out_ref.shape[1]):
        sources = [held_ref[line * across + k : line * across + k + 1, :] for k in range(across)]
        wide = jnp.concatenate(sources, axis=1)
        out_ref[:, line, :] = jnp.broadcast_to(wide, (out_ref.shape[0], LANES))


def prepare_kernel(own_ref, pool_ref, own_out, pool_out, own_norm_ref, pool_norm_ref):
    own_out[...] = own_ref[...]
    pool_out[...] = pool_ref[...]
    own_norm_ref[...] = row_norms(own_ref)
    pool_norm_ref[...] = row_norms(pool_ref)


def early_kernel(count, scale, unit, code_ref, *refs):
    pieces, (pool_ref, norm_ref) = refs[:count], refs[count : count + 2]
    score_ref, held_ref, joined = refs[count + 2 :]
    size = held_ref.shape[0]
    fill_scores(0, size, scale, code_ref, pieces, pool_ref, joined, score_ref)
    held_ref[...] = jnp.zeros_like(held_ref)
    row_pass(0, code_ref, norm_ref[...] * (-1.0 / unit), score_ref, held_ref)


def late_kernel(first, count, scale, unit, code_ref, *refs):
    pieces, (pool_ref, norm_ref, before_ref) = refs[:count], refs[count : count + 3]
    score_ref, out_ref, joined, held_ref = refs[count + 3 :]
    size = held_ref.shape[0]
    fill_scores(first, size, scale, code_ref, pieces, pool_ref, joined, score_ref)
    held_ref[...] = before_ref[...]
    row_pass(first, code_ref, norm_ref[...] * (-1.0 / unit), score_ref, held_ref)
    copy_out(held_ref, out_ref)


def row_kernel(code_ref, shift_ref, *refs):
    out_ref, held_ref = refs[-2:]
    shift = shift_ref[...]
    first = 0
    for ref in refs[:-2]:
        row_pass(first, code_ref, shift, ref, held_ref)
        first += ref.shape[0] // held_ref.shape[1]
    copy_out(held_ref, out_ref)


def column_kernel(log_a, unit, code_ref, value_ref, norm_ref, *refs):
    scores, (out_ref, own_ref, held_ref) = refs[:-3], refs[-3:]
    shift = log_a - log2_sum([value_ref[k] for k in range(value_ref.shape[0])])
    size, own_rows = held_ref.shape
    pool_rows = out_ref.shape[1]
    across = LANES // own_rows
    for source in range(size):
        line, place = source // across, source % across
        held_ref[source : source + 1, :] = shift[
            line : line + 1, place * own_rows : (place + 1) * own_rows
        ]
    own_ref[...] = held_ref[pl.ds(code_ref[0] & (size - 1), 1), :] * unit + norm_ref[...]
    eye = diagonal(own_rows)
    folded = (own_rows // SUBLANES, SUBLANES, pool_rows)
    blocks = [
        (ref, slice(low, low + own_rows)) for ref in scores for low in range(0, ref.shape[0], own_rows)
    ]
    columns = []
    peak = None
    for k, (ref, rows) in enumerate(blocks):
        row = held_ref[pl.ds(code_ref[k] & (size - 1), 1), :]
        columns.append(jnp.sum(jnp.where(eye, row, 0.0), axis=1, keepdims=True))
        high = jnp.max((ref[rows, :] + columns[k]).reshape(folded), axis=0)
        peak = high if peak is None else jnp.maximum(peak, high)
    peak = jnp.max(peak, axis=0, keepdims=True)
    total = jnp.zeros((SUBLANES, pool_rows), jnp.float32)
    for k, (ref, rows) in enumerate(blocks):
        total += jnp.sum(jnp.exp2(ref[rows, :] + (columns[k] - peak)).reshape(folded), axis=0)
    out_ref[...] = peak + log2(jnp.sum(total, axis=0, keepdims=True))


def call(kernel, shapes, scratch, scalars, arrays, flops, name, dtypes=(jnp.float32,) * 4):
    smem = pl.BlockSpec(memory_space=pltpu.SMEM)
    vmem = pl.BlockSpec(memory_space=pltpu.VMEM)
    moved = sum(a.size * a.dtype.itemsize for a in arrays) + 4 * sum(map(math.prod, shapes))
    return pl.pallas_call(
        kernel,
        out_shape=[jax.ShapeDtypeStruct(s, d) for s, d in zip(shapes, dtypes)],
        in_specs=[smem] * len(scalars) + [vmem] * len(arrays),
        out_specs=[vmem] * len(shapes),
        scratch_shapes=scratch,
        compiler_params=pltpu.CompilerParams(vmem_limit_bytes=3 * moved + (4 << 20)),
        cost_estimate=pl.CostEstimate(flops=flops, bytes_accessed=moved, transcendentals=0),
        name=name,
    )(*scalars, *arrays)


def body(samples, pool, tile_list, tile_count):
    own_rows, width = samples.shape[1:]
    size = lax.axis_size("pool")
    cores = lax.axis_size("samp")
    half_rows = own_rows * size
    pool_rows = pool.shape[0]
    lines = half_rows // LANES
    unit = EPS * LN2
    scale = 2.0 / (width * unit)
    log_a = -math.log2(half_rows * cores)
    log_b = -math.log2(pool_rows * size)
    own = samples.reshape(own_rows, width)

    def swap(value, masks):
        pairs = [
            (i * cores + c, (i ^ masks[c % 2]) * cores + c)
            for i in range(size)
            for c in range(cores)
        ]
        return lax.ppermute(value, ("pool", "samp"), pairs)

    def side_a(value):
        return swap(value, (1, 2))

    def side_b(value):
        return swap(value, (2, 1))

    def far(value, mask):
        return swap(value, (mask, mask))

    own_copy, pool_copy, own_norm, pool_norm = call(
        prepare_kernel,
        [own.shape, pool.shape, (1, own_rows), (1, pool_rows)],
        [],
        [],
        [own, pool],
        4 * pool_rows * width,
        "prepare",
        (own.dtype, pool.dtype, jnp.float32, jnp.float32),
    )
    mask_a = 1 + lax.axis_index("samp").astype(jnp.int32) % 2
    mask_b = 3 - mask_a
    masks = [0, mask_a, mask_b, 3, 4, 12, 8, 4 + mask_a, 4 + mask_b, 12 + mask_a, 12 + mask_b]
    masks += [8 + mask_b, 8 + mask_a, 7, 15, 11]
    step = 16
    while step < size:
        masks += [m + step for m in masks]
        step *= 2
    owner = lax.axis_index("pool").astype(jnp.int32) ^ jnp.stack([jnp.int32(m) for m in masks])
    tile = owner * own_rows // TILE
    code = owner
    for u in range(pool_rows // TILE):
        for k in range(CAP):
            hit = (tile == tile_list[0, 0, k, 0]) & (tile_list[0, 0, k, 1] == u)
            code |= jnp.where(hit & (k < tile_count[0, 0]), size << u, 0)

    far12, far4 = far(own, 12), far(own, 4)
    a, b = side_a(own), side_b(own)
    corner = side_b(a)
    tied = lax.optimization_barrier((far12, code, own_copy, pool_copy, own_norm, pool_norm))
    far12, code, own_copy, pool_copy, own_norm, pool_norm = tied
    far8 = far(far12, 4)
    a4, b4 = side_a(far4), side_b(far4)
    a12, b12 = side_a(far12), side_b(far12)
    a8, b8 = side_a(far8), side_b(far8)
    corner12, corner4 = far(corner, 12), far(corner, 4)
    corner8 = far(corner12, 4)
    early = [own_copy, a, b, corner, far4, far12, far8, a4, b4, a12, b12, b8]
    late = [a8, corner4, corner12, corner8]
    step = 16
    while step < size:
        late += [far(piece, step) for piece in early + late]
        step *= 2
    count = len(early)
    score0, held = call(
        functools.partial(early_kernel, count, scale, unit),
        [(count * own_rows, pool_rows), (size, own_rows)],
        [pltpu.VMEM((count * own_rows, width), samples.dtype)],
        [code],
        early + [pool_copy, pool_norm],
        2 * count * own_rows * pool_rows * width,
        "early_scores",
    )
    *late, score0, held = lax.optimization_barrier((*late, score0, held))
    rest = len(late)
    score1, value = call(
        functools.partial(late_kernel, count, rest, scale, unit),
        [(rest * own_rows, pool_rows), (size, lines, LANES)],
        [
            pltpu.VMEM((rest * own_rows, width), samples.dtype),
            pltpu.VMEM((size, own_rows), jnp.float32),
        ],
        [code],
        late + [pool_copy, pool_norm, held],
        2 * rest * own_rows * pool_rows * width,
        "late_scores",
    )
    scores = [score0, score1]
    flops = 8 * half_rows * pool_rows
    held = [pltpu.VMEM((size, own_rows), jnp.float32)]
    for iteration in range(ITERS):
        if iteration > 0:
            shapes = [(size, lines, LANES)]
            (value,) = call(row_kernel, shapes, held, [code], [shift] + scores, flops, "rows")
        value = lax.all_to_all(value, "pool", 0, 0, tiled=True)
        value, sample_potential = call(
            functools.partial(column_kernel, log_a, unit),
            [(1, pool_rows), (1, own_rows)],
            held,
            [code],
            [value, own_norm] + scores,
            flops,
            "columns",
        )
        pairs = [(i, i ^ 1) for i in range(cores)]
        shift = log_b - log2_sum([value, lax.ppermute(value, "samp", pairs)])
    return sample_potential, (shift * unit + pool_norm).reshape(pool_rows)


def solution(mesh):
    placed = (
        P(("grp", "samp"), "pool", None),
        P(("grp", "pool"), None),
        P(("grp", "samp"), "pool", None, None),
        P(("grp", "samp"), "pool"),
    )
    return jax.shard_map(
        body,
        mesh=mesh,
        in_specs=placed,
        out_specs=(P(("grp", "samp"), "pool"), P(("grp", "pool"))),
        check_vma=False,
    )
```

time: 82.3 us -> 87.9 us (1.068)
  between operations: 1.36 us -> 6.48 us
  blocking collectives: 34 us -> 30.4 us
  starting transfers between devices: 20.7 us -> 17.2 us
  waiting for transfers between devices: 8.07 us -> 10.8 us
  other arithmetic: 0.69 us -> 3.29 us
  Pallas kernels: 13.8 us -> 15.1 us
  local copies, waits for them, and re-layouts: 3.35 us -> 4.24 us
    all_to_all x3, blocking collectives: 34 us -> 30.4 us  [body(): value = lax.all_to_all(value, 'pool', 0, 0, tiled=True)]
    ppermute x15, starting transfers between devices: 20.7 us -> 17.2 us  [swap(): return lax.ppermute(value, ('pool', 'samp'), pairs)]
    ppermute x15, waiting for transfers between devices: 4.58 us -> 7.29 us  [swap(): return lax.ppermute(value, ('pool', 'samp'), pairs)]
    or x0 -> x1, other arithmetic: none -> 2.6 us  [body(): code |= jnp.where(hit & (k < tile_count[0, 0]), size << u, 0)]
    slice x0 -> x1, local copies, waits for them, and re-layouts: none -> 1.65 us  [body(): hit = (tile == tile_list[0, 0, k, 0]) & (tile_list[0, 0, k, 1] == u)]
    pallas_call x7 -> x8, Pallas kernels: 13.8 us -> 15.1 us  [call(): pl.pallas_call(kernel, out_shape=[jax.ShapeDtypeStruct(s, d) for s, d in...]
    unnamed x5 -> x4, local copies, waits for them, and re-layouts: 3.25 us -> 2.49 us
  transfers between devices with their start and end apart: 18 -> 18, of which waited for: 5 -> 8; matrix products, arithmetic and copies ran while one was open for 1% -> 5% of each run, Pallas kernels for 4% -> 4%
where the time goes in v5:
time: 87.9 us; the launch traced here: 87.5 us
  blocking collectives  30.4 us (35%)
  starting transfers between devices  17.2 us (20%)
  Pallas kernels  15.1 us (17%)
  waiting for transfers between devices  10.8 us (12%)
  between operations  6.48 us (7%)
  local copies, waits for them, and re-layouts  4.24 us (5%)
  other arithmetic  3.29 us (4%)
    all_to_all x3, blocking collectives, body(): value = lax.all_to_all(value, 'pool', 0, 0, tiled=True)  30.4 us
    ppermute x15, starting transfers between devices, swap(): return lax.ppermute(value, ('pool', 'samp'), pairs)  17.2 us
    pallas_call x8, Pallas kernels, call(): pl.pallas_call(kernel, out_shape=[jax.ShapeDtypeStruct(s, d) for s, d in...  15.1 us
    ppermute x15, waiting for transfers between devices, swap(): return lax.ppermute(value, ('pool', 'samp'), pairs)  7.29 us
    ppermute x3, waiting for transfers between devices, body(): shift = log_b - log2_sum([value, lax.ppermute(value, 'samp', pairs)])  3.49 us
    or x1, other arithmetic, body(): code |= jnp.where(hit & (k < tile_count[0, 0]), size << u, 0)  2.6 us
    unnamed x4, local copies, waits for them, and re-layouts  2.49 us
  transfers between devices with their start and end apart: 18, of which 8 were waited for; matrix products, arithmetic and copies ran while one was open for 5% of the time, Pallas kernels for 4%

profile of v5, /device:TPU:0, one launch (start us, length us, event | category | flops | bytes accessed | tf_op | source)
XLA Modules:
  0.0 87.5 jit_solution(12466118793440654049)
XLA Ops:
  0.6 5.1 %collective-permute-start = (bf16[64,1024]{1,0:T(8,128)(2,1)}, bf16[64,1024]{1,0:T(8,128)(2,1)S(1)}, u32[]{:S(2)}, u32[]{:S(2)}) collective-permute-start(bf16[64,1024]{1,0:T(8,128)(2,1)} %bitcast.26), channel_id=1, source_target_pairs={{0,24},{1,25},{2,26},{3,27},{4,28},{5,29},{6,30},{7,31},{8,16},{9,... | collective-permute-start | bytes 393224 | tf_op jit(solution)/shard_map/ppermute | solution.py:194
  5.7 1.5 %collective-permute-start.3 = (bf16[64,1024]{1,0:T(8,128)(2,1)}, bf16[64,1024]{1,0:T(8,128)(2,1)S(1)}, u32[]{:S(2)}, u32[]{:S(2)}) collective-permute-start(bf16[64,1024]{1,0:T(8,128)(2,1)} %bitcast.27), channel_id=1, source_target_pairs={{0,2},{1,5},{2,0},{3,7},{4,6},{5,1},{6,4},{7,3},{8,10},{9,13},{10,... | collective-permute-start | bytes 393224 | tf_op jit(solution)/shard_map/ppermute | solution.py:194
  7.2 1.5 %collective-permute-start.8 = (bf16[64,1024]{1,0:T(8,128)(2,1)}, bf16[64,1024]{1,0:T(8,128)(2,1)S(1)}, u32[]{:S(2)}, u32[]{:S(2)}) collective-permute-start(bf16[64,1024]{1,0:T(8,128)(2,1)} %bitcast.29), channel_id=1, source_target_pairs={{0,4},{1,3},{2,6},{3,1},{4,0},{5,7},{6,2},{7,5},{8,12},{9,11},{10,... | collective-permute-start | bytes 393224 | tf_op jit(solution)/shard_map/ppermute | solution.py:194
  8.8 1.6 %fusion.3 = (s32[1,1,1,1]{2,3,1,0:T(1,128)}, s32[1,1,1,1]{2,3,1,0:T(1,128)}, s32[1,1,1,1]{2,3,1,0:T(1,128)}, s32[1,1,1,1]{2,3,1,0:T(1,128)}, s32[1,1,1,1]{2,3,1,...) fusion(s32[1,1,4,2]{2,3,1,0:T(2,128)} %param.6), kind=kLoop, calls=%fused_computation.22 | loop fusion | bytes 64 | tf_op jit(solution)/shard_map/slice | solution.py:228
  16.2 1.6 %copy-done = bf16[1024,1024]{1,0:T(8,128)(2,1)S(1)} copy-done((bf16[1024,1024]{1,0:T(8,128)(2,1)S(1)}, bf16[1024,1024]{1,0:T(8,128)(2,1)}, u32[]{:S(2)}) %copy-start) | copy-done | bytes 2097176
  19.3 2.6 %or_or_fusion.code_ref = s32[16]{0:T(128)S(1)} fusion(pred[]{:T(512)} %bitcast.11, pred[]{:T(512)} %bitcast.10, pred[]{:T(512)} %bitcast.14, pred[]{:T(512)} %bitcast.13, pred[]{:T(512)} %bitcast.17, pred[]{:T(512)} %bitcast.16, pred[]{:T(512)} %bitcast.20, pred[]{:T(512)} %bitcast.19, pred[]{:T(512)} %bitcast.21, pred[]{:T(512)} %bitcast.22, pred[]{:T(512)} %bitcast.23, ...), kind=kLoop, calls=%fused_computation.21 | loop fusion | flops 848 | bytes 160 | tf_op jit(solution)/shard_map/or | solution.py:229
  22.5 2.0 %collective-permute-start.1 = (bf16[64,1024]{1,0:T(8,128)(2,1)S(1)}, bf16[64,1024]{1,0:T(8,128)(2,1)S(1)}, u32[]{:S(2)}, u32[]{:S(2)}) collective-permute-start(bf16[64,1024]{1,0:T(8,128)(2,1)S(1)} %collective-permute-done.refs_5_), channel_id=1, source_target_pairs={{0,8},{1,9},{2,10},{3,11},{4,12},{5,13},{6,14},{7,15},{8,0},{9,1},... | collective-permute-start | bytes 393224 | tf_op jit(solution)/shard_map/ppermute | solution.py:194
  25.1 1.5 %collective-permute-start.13 = (bf16[64,1024]{1,0:T(8,128)(2,1)S(1)}, bf16[64,1024]{1,0:T(8,128)(2,1)S(1)}, u32[]{:S(2)}, u32[]{:S(2)}) collective-permute-start(bf16[64,1024]{1,0:T(8,128)(2,1)S(1)} %collective-permute-done.refs_5_), channel_id=1, source_target_pairs={{0,4},{1,3},{2,6},{3,1},{4,0},{5,7},{6,2},{7,5},{8,12},{9,11},{10,... | collective-permute-start | bytes 393224 | tf_op jit(solution)/shard_map/ppermute | solution.py:194
  26.6 1.5 %collective-permute-start.10 = (bf16[64,1024]{1,0:T(8,128)(2,1)S(1)}, bf16[64,1024]{1,0:T(8,128)(2,1)S(1)}, u32[]{:S(2)}, u32[]{:S(2)}) collective-permute-start(bf16[64,1024]{1,0:T(8,128)(2,1)S(1)} %collective-permute-done.9.refs_4_), channel_id=1, source_target_pairs={{0,2},{1,5},{2,0},{3,7},{4,6},{5,1},{6,4},{7,3},{8,10},{9,13},{10,... | collective-permute-start | bytes 393224 | tf_op jit(solution)/shard_map/ppermute | solution.py:194
  29.3 1.6 %collective-permute-done.12.refs_9_ = bf16[64,1024]{1,0:T(8,128)(2,1)S(1)} collective-permute-done((bf16[64,1024]{1,0:T(8,128)(2,1)S(1)}, bf16[64,1024]{1,0:T(8,128)(2,1)S(1)}, u32[]{:S(2)}, u32[]{:S(2)}) %collective-permute-start.12) | collective-permute-done | bytes 131104 | tf_op jit(solution)/shard_map/ppermute | solution.py:194
  31.7 1.3 %collective-permute-start.2 = (bf16[64,1024]{1,0:T(8,128)(2,1)S(1)}, bf16[64,1024]{1,0:T(8,128)(2,1)S(1)}, u32[]{:S(2)}, u32[]{:S(2)}) collective-permute-start(bf16[64,1024]{1,0:T(8,128)(2,1)S(1)} %collective-permute-done.1.refs_6_), channel_id=1, source_target_pairs={{0,2},{1,5},{2,0},{3,7},{4,6},{5,1},{6,4},{7,3},{8,10},{9,13},{10,... | collective-permute-start | bytes 393224 | tf_op jit(solution)/shard_map/ppermute | solution.py:194
  33.7 2.6 %collective-permute-done.6.refs_2_ = bf16[64,1024]{1,0:T(8,128)(2,1)S(1)} collective-permute-done((bf16[64,1024]{1,0:T(8,128)(2,1)S(1)}, bf16[64,1024]{1,0:T(8,128)(2,1)S(1)}, u32[]{:S(2)}, u32[]{:S(2)}) %collective-permute-start.6) | collective-permute-done | bytes 131104 | tf_op jit(solution)/shard_map/ppermute | solution.py:194
  36.4 3.0 %early_scores.1 = (f32[768,1024]{1,0:T(8,128)S(1)}, f32[16,64]{1,0:T(8,128)S(1)}) custom-call(s32[16]{0:T(128)S(1)} %or_or_fusion.code_ref, bf16[64,1024]{1,0:T(8,128)(2,1)S(1)} %get-tuple-element.32.refs_0_, bf16[64,1024]{1,0:T(8,128)(2,1)S(1)} %collective-permute-done.3.refs_1_, bf16[64,1024]{1,0:T(8,128)(2,1)S(1)} %collective-permute-done.8.refs_2_, ...), custom_call_target="tpu_custom_call" | custom-call | flops 1610612736 | bytes 6823936 | tf_op jit(solution)/shard_map/early_scores/pallas_call | solution.py:163
  39.4 2.0 %collective-permute-done.7.refs_3_ = bf16[64,1024]{1,0:T(8,128)(2,1)S(1)} collective-permute-done((bf16[64,1024]{1,0:T(8,128)(2,1)S(1)}, bf16[64,1024]{1,0:T(8,128)(2,1)S(1)}, u32[]{:S(2)}, u32[]{:S(2)}) %collective-permute-start.7) | collective-permute-done | bytes 131104 | tf_op jit(solution)/shard_map/ppermute | solution.py:194
  41.3 1.6 %late_scores.1 = (f32[256,1024]{1,0:T(8,128)S(1)}, f32[16,8,128]{2,1,0:T(8,128)S(1)}) custom-call(s32[16]{0:T(128)S(1)} %or_or_fusion.code_ref, bf16[64,1024]{1,0:T(8,128)(2,1)S(1)} %collective-permute-done.2.refs_0_, bf16[64,1024]{1,0:T(8,128)(2,1)S(1)} %collective-permute-done.5.refs_1_, bf16[64,1024]{1,0:T(8,128)(2,1)S(1)} %collective-permute-done.6.refs_2_, ...), custom_call_target="tpu_custom_call" | custom-call | flops 536870912 | bytes 3743744 | tf_op jit(solution)/shard_map/late_scores/pallas_call | solution.py:163
  43.0 10.1 %all_to_all.15.value_ref = f32[16,8,128]{2,1,0:T(8,128)S(1)} all-to-all(f32[16,8,128]{2,1,0:T(8,128)S(1)} %get-tuple-element.42), channel_id=1, replica_groups=mesh['grp'=1,'pool'=16,'samp'=2] {'pool'}, dimensions={0} | all-to-all | bytes 131072 | tf_op jit(solution)/shard_map/all_to_all | solution.py:279
  53.1 2.2 %columns.3 = (f32[1,1024]{1,0:T(1,128)S(1)}, f32[1,64]{1,0:T(1,128)}) custom-call(s32[16]{0:T(128)S(1)} %or_or_fusion.code_ref, f32[16,8,128]{2,1,0:T(8,128)S(1)} %all_to_all.15.value_ref, f32[1,64]{1,0:T(1,128)S(1)} %get-tuple-element.43.norm_ref, f32[768,1024]{1,0:T(8,128)S(1)} %get-tuple-element.44.refs_0_, f32[256,1024]{1,0:T(8,128)S(1)} %get-tuple-element.45.refs_1_), custom_call_target="tpu_custom_call" | custom-call | flops 8388608 | bytes 4264448 | tf_op jit(solution)/shard_map/columns/pallas_call | solution.py:163
  55.3 1.2 %collective-permute-done.15 = f32[1,1024]{1,0:T(1,128)S(1)} collective-permute-done((f32[1,1024]{1,0:T(1,128)S(1)}, f32[1,1024]{1,0:T(1,128)S(1)}, u32[]{:S(2)}, u32[]{:S(2)}) %collective-permute-start.15) | collective-permute-done | bytes 4128 | tf_op jit(solution)/shard_map/ppermute | solution.py:290
  56.5 1.7 %rows.2 = f32[16,8,128]{2,1,0:T(8,128)S(1)} custom-call(s32[16]{0:T(128)S(1)} %or_or_fusion.code_ref, f32[1,1024]{1,0:T(1,128)S(1)} %add_subtract_fusion.1.shift_ref, f32[768,1024]{1,0:T(8,128)S(1)} %get-tuple-element.44.refs_0_, f32[256,1024]{1,0:T(8,128)S(1)} %get-tuple-element.45.refs_1_), custom_call_target="tpu_custom_call" | custom-call | flops 8388608 | bytes 4263936 | tf_op jit(solution)/shard_map/rows/pallas_call | solution.py:163
  58.2 10.1 %all_to_all.16.value_ref = f32[16,8,128]{2,1,0:T(8,128)S(1)} all-to-all(f32[16,8,128]{2,1,0:T(8,128)S(1)} %rows.2), channel_id=1, replica_groups=mesh['grp'=1,'pool'=16,'samp'=2] {'pool'}, dimensions={0} | all-to-all | bytes 131072 | tf_op jit(solution)/shard_map/all_to_all | solution.py:279
  68.3 2.2 %columns.4 = (f32[1,1024]{1,0:T(1,128)S(1)}, f32[1,64]{1,0:T(1,128)}) custom-call(s32[16]{0:T(128)S(1)} %or_or_fusion.code_ref, f32[16,8,128]{2,1,0:T(8,128)S(1)} %all_to_all.16.value_ref, f32[1,64]{1,0:T(1,128)S(1)} %get-tuple-element.43.norm_ref, f32[768,1024]{1,0:T(8,128)S(1)} %get-tuple-element.44.refs_0_, f32[256,1024]{1,0:T(8,128)S(1)} %get-tuple-element.45.refs_1_), custom_call_target="tpu_custom_call" | custom-call | flops 8388608 | bytes 4264448 | tf_op jit(solution)/shard_map/columns/pallas_call | solution.py:163
  71.7 1.7 %rows.3 = f32[16,8,128]{2,1,0:T(8,128)S(1)} custom-call(s32[16]{0:T(128)S(1)} %or_or_fusion.code_ref, f32[1,1024]{1,0:T(1,128)S(1)} %add_subtract_fusion.shift_ref, f32[768,1024]{1,0:T(8,128)S(1)} %get-tuple-element.44.refs_0_, f32[256,1024]{1,0:T(8,128)S(1)} %get-tuple-element.45.refs_1_), custom_call_target="tpu_custom_call" | custom-call | flops 8388608 | bytes 4263936 | tf_op jit(solution)/shard_map/rows/pallas_call | solution.py:163
  73.3 10.1 %all_to_all.17.value_ref = f32[16,8,128]{2,1,0:T(8,128)S(1)} all-to-all(f32[16,8,128]{2,1,0:T(8,128)S(1)} %rows.3), channel_id=1, replica_groups=mesh['grp'=1,'pool'=16,'samp'=2] {'pool'}, dimensions={0} | all-to-all | bytes 131072 | tf_op jit(solution)/shard_map/all_to_all | solution.py:279
  83.5 2.2 %columns.5 = (f32[1,1024]{1,0:T(1,128)S(1)}, f32[1,64]{1,0:T(1,128)}) custom-call(s32[16]{0:T(128)S(1)} %or_or_fusion.code_ref, f32[16,8,128]{2,1,0:T(8,128)S(1)} %all_to_all.17.value_ref, f32[1,64]{1,0:T(1,128)S(1)} %get-tuple-element.43.norm_ref, f32[768,1024]{1,0:T(8,128)S(1)} %get-tuple-element.44.refs_0_, f32[256,1024]{1,0:T(8,128)S(1)} %get-tuple-element.45.refs_1_), custom_call_target="tpu_custom_call" | custom-call | flops 8388608 | bytes 4264448 | tf_op jit(solution)/shard_map/columns/pallas_call | solution.py:163
  (33 shorter events, 8.4 us)
Async XLA Ops:
  0.6 21.3 %collective-permute-start = (bf16[64,1024]{1,0:T(8,128)(2,1)}, bf16[64,1024]{1,0:T(8,128)(2,1)S(1)}, u32[]{:S(2)}, u32[]{:S(2)}) collective-permute-start(bf16[64,1024]{1,0:T(8,128)(2,1)} %bitcast.26), channel_id=1, source_target_pairs={{0,24},{1,25},{2,26},{3,27},{4,28},{5,29},{6,30},{7,31},{8,16},{9,... | collective-permute-start | bytes 393224 | tf_op jit(solution)/shard_map/ppermute | solution.py:194
  5.7 16.2 %collective-permute-start.3 = (bf16[64,1024]{1,0:T(8,128)(2,1)}, bf16[64,1024]{1,0:T(8,128)(2,1)S(1)}, u32[]{:S(2)}, u32[]{:S(2)}) collective-permute-start(bf16[64,1024]{1,0:T(8,128)(2,1)} %bitcast.27), channel_id=1, source_target_pairs={{0,2},{1,5},{2,0},{3,7},{4,6},{5,1},{6,4},{7,3},{8,10},{9,13},{10,... | collective-permute-start | bytes 393224 | tf_op jit(solution)/shard_map/ppermute | solution.py:194
  7.2 17.9 %collective-permute-start.9 = (bf16[64,1024]{1,0:T(8,128)(2,1)}, bf16[64,1024]{1,0:T(8,128)(2,1)S(1)}, u32[]{:S(2)}, u32[]{:S(2)}) collective-permute-start(bf16[64,1024]{1,0:T(8,128)(2,1)} %bitcast.28), channel_id=1, source_target_pairs={{0,8},{1,9},{2,10},{3,11},{4,12},{5,13},{6,14},{7,15},{8,0},{9,1},... | collective-permute-start | bytes 393224 | tf_op jit(solution)/shard_map/ppermute | solution.py:194
  7.2 19.4 %collective-permute-start.8 = (bf16[64,1024]{1,0:T(8,128)(2,1)}, bf16[64,1024]{1,0:T(8,128)(2,1)S(1)}, u32[]{:S(2)}, u32[]{:S(2)}) collective-permute-start(bf16[64,1024]{1,0:T(8,128)(2,1)} %bitcast.29), channel_id=1, source_target_pairs={{0,4},{1,3},{2,6},{3,1},{4,0},{5,7},{6,2},{7,5},{8,12},{9,11},{10,... | collective-permute-start | bytes 393224 | tf_op jit(solution)/shard_map/ppermute | solution.py:194
  16.2 1.6 %copy-start = (bf16[1024,1024]{1,0:T(8,128)(2,1)S(1)}, bf16[1024,1024]{1,0:T(8,128)(2,1)}, u32[]{:S(2)}) copy-start(bf16[1024,1024]{1,0:T(8,128)(2,1)} %pool_ref.1) | copy-start | bytes 6291460
  17.7 0.9 %copy-start.1 = (bf16[1,64,1024]{2,1,0:T(8,128)(2,1)S(1)}, bf16[1,64,1024]{2,1,0:T(8,128)(2,1)}, u32[]{:S(2)}) copy-start(bf16[1,64,1024]{2,1,0:T(8,128)(2,1)} %param.4) | copy-start | bytes 393220
  22.0 6.4 %collective-permute-start.4 = (bf16[64,1024]{1,0:T(8,128)(2,1)S(1)}, bf16[64,1024]{1,0:T(8,128)(2,1)S(1)}, u32[]{:S(2)}, u32[]{:S(2)}) collective-permute-start(bf16[64,1024]{1,0:T(8,128)(2,1)S(1)} %collective-permute-done.3.refs_1_), channel_id=1, source_target_pairs={{0,4},{1,3},{2,6},{3,1},{4,0},{5,7},{6,2},{7,5},{8,12},{9,11},{10,... | collective-permute-start | bytes 393224 | tf_op jit(solution)/shard_map/ppermute | solution.py:194
  22.5 6.7 %collective-permute-start.1 = (bf16[64,1024]{1,0:T(8,128)(2,1)S(1)}, bf16[64,1024]{1,0:T(8,128)(2,1)S(1)}, u32[]{:S(2)}, u32[]{:S(2)}) collective-permute-start(bf16[64,1024]{1,0:T(8,128)(2,1)S(1)} %collective-permute-done.refs_5_), channel_id=1, source_target_pairs={{0,8},{1,9},{2,10},{3,11},{4,12},{5,13},{6,14},{7,15},{8,0},{9,1},... | collective-permute-start | bytes 393224 | tf_op jit(solution)/shard_map/ppermute | solution.py:194
  24.5 6.4 %collective-permute-start.12 = (bf16[64,1024]{1,0:T(8,128)(2,1)S(1)}, bf16[64,1024]{1,0:T(8,128)(2,1)S(1)}, u32[]{:S(2)}, u32[]{:S(2)}) collective-permute-start(bf16[64,1024]{1,0:T(8,128)(2,1)S(1)} %collective-permute-done.refs_5_), channel_id=1, source_target_pairs={{0,2},{1,5},{2,0},{3,7},{4,6},{5,1},{6,4},{7,3},{8,10},{9,13},{10,... | collective-permute-start | bytes 393224 | tf_op jit(solution)/shard_map/ppermute | solution.py:194
  25.1 6.6 %collective-permute-start.13 = (bf16[64,1024]{1,0:T(8,128)(2,1)S(1)}, bf16[64,1024]{1,0:T(8,128)(2,1)S(1)}, u32[]{:S(2)}, u32[]{:S(2)}) collective-permute-start(bf16[64,1024]{1,0:T(8,128)(2,1)S(1)} %collective-permute-done.refs_5_), channel_id=1, source_target_pairs={{0,4},{1,3},{2,6},{3,1},{4,0},{5,7},{6,2},{7,5},{8,12},{9,11},{10,... | collective-permute-start | bytes 393224 | tf_op jit(solution)/shard_map/ppermute | solution.py:194
  26.6 7.1 %collective-permute-start.10 = (bf16[64,1024]{1,0:T(8,128)(2,1)S(1)}, bf16[64,1024]{1,0:T(8,128)(2,1)S(1)}, u32[]{:S(2)}, u32[]{:S(2)}) collective-permute-start(bf16[64,1024]{1,0:T(8,128)(2,1)S(1)} %collective-permute-done.9.refs_4_), channel_id=1, source_target_pairs={{0,2},{1,5},{2,0},{3,7},{4,6},{5,1},{6,4},{7,3},{8,10},{9,13},{10,... | collective-permute-start | bytes 393224 | tf_op jit(solution)/shard_map/ppermute | solution.py:194
  28.4 8.0 %collective-permute-start.6 = (bf16[64,1024]{1,0:T(8,128)(2,1)S(1)}, bf16[64,1024]{1,0:T(8,128)(2,1)S(1)}, u32[]{:S(2)}, u32[]{:S(2)}) collective-permute-start(bf16[64,1024]{1,0:T(8,128)(2,1)S(1)} %collective-permute-done.4.refs_3_), channel_id=1, source_target_pairs={{0,24},{1,25},{2,26},{3,27},{4,28},{5,29},{6,30},{7,31},{8,16},{9,... | collective-permute-start | bytes 393224 | tf_op jit(solution)/shard_map/ppermute | solution.py:194
  29.3 7.1 %collective-permute-start.11 = (bf16[64,1024]{1,0:T(8,128)(2,1)S(1)}, bf16[64,1024]{1,0:T(8,128)(2,1)S(1)}, u32[]{:S(2)}, u32[]{:S(2)}) collective-permute-start(bf16[64,1024]{1,0:T(8,128)(2,1)S(1)} %collective-permute-done.9.refs_4_), channel_id=1, source_target_pairs={{0,4},{1,3},{2,6},{3,1},{4,0},{5,7},{6,2},{7,5},{8,12},{9,11},{10,... | collective-permute-start | bytes 393224 | tf_op jit(solution)/shard_map/ppermute | solution.py:194
  30.9 5.5 %collective-permute-start.14 = (bf16[64,1024]{1,0:T(8,128)(2,1)S(1)}, bf16[64,1024]{1,0:T(8,128)(2,1)S(1)}, u32[]{:S(2)}, u32[]{:S(2)}) collective-permute-start(bf16[64,1024]{1,0:T(8,128)(2,1)S(1)} %collective-permute-done.1.refs_6_), channel_id=1, source_target_pairs={{0,4},{1,3},{2,6},{3,1},{4,0},{5,7},{6,2},{7,5},{8,12},{9,11},{10,... | collective-permute-start | bytes 393224 | tf_op jit(solution)/shard_map/ppermute | solution.py:194
  31.7 7.7 %collective-permute-start.2 = (bf16[64,1024]{1,0:T(8,128)(2,1)S(1)}, bf16[64,1024]{1,0:T(8,128)(2,1)S(1)}, u32[]{:S(2)}, u32[]{:S(2)}) collective-permute-start(bf16[64,1024]{1,0:T(8,128)(2,1)S(1)} %collective-permute-done.1.refs_6_), channel_id=1, source_target_pairs={{0,2},{1,5},{2,0},{3,7},{4,6},{5,1},{6,4},{7,3},{8,10},{9,13},{10,... | collective-permute-start | bytes 393224 | tf_op jit(solution)/shard_map/ppermute | solution.py:194
  33.7 5.6 %collective-permute-start.5 = (bf16[64,1024]{1,0:T(8,128)(2,1)S(1)}, bf16[64,1024]{1,0:T(8,128)(2,1)S(1)}, u32[]{:S(2)}, u32[]{:S(2)}) collective-permute-start(bf16[64,1024]{1,0:T(8,128)(2,1)S(1)} %collective-permute-done.4.refs_3_), channel_id=1, source_target_pairs={{0,8},{1,9},{2,10},{3,11},{4,12},{5,13},{6,14},{7,15},{8,0},{9,1},... | collective-permute-start | bytes 393224 | tf_op jit(solution)/shard_map/ppermute | solution.py:194
  36.4 5.0 %collective-permute-start.7 = (bf16[64,1024]{1,0:T(8,128)(2,1)S(1)}, bf16[64,1024]{1,0:T(8,128)(2,1)S(1)}, u32[]{:S(2)}, u32[]{:S(2)}) collective-permute-start(bf16[64,1024]{1,0:T(8,128)(2,1)S(1)} %collective-permute-done.6.refs_2_), channel_id=1, source_target_pairs={{0,8},{1,9},{2,10},{3,11},{4,12},{5,13},{6,14},{7,15},{8,0},{9,1},... | collective-permute-start | bytes 393224 | tf_op jit(solution)/shard_map/ppermute | solution.py:194
  55.3 1.2 %collective-permute-start.15 = (f32[1,1024]{1,0:T(1,128)S(1)}, f32[1,1024]{1,0:T(1,128)S(1)}, u32[]{:S(2)}, u32[]{:S(2)}) collective-permute-start(f32[1,1024]{1,0:T(1,128)S(1)} %get-tuple-element.46), channel_id=1, source_target_pairs={{0,1},{1,0},{2,3},{3,2},{4,5},{5,4},{6,7},{7,6},{8,9},{9,8},{10,11... | collective-permute-start | bytes 12296 | tf_op jit(solution)/shard_map/ppermute | solution.py:290
  70.5 1.2 %collective-permute-start.16 = (f32[1,1024]{1,0:T(1,128)S(1)}, f32[1,1024]{1,0:T(1,128)S(1)}, u32[]{:S(2)}, u32[]{:S(2)}) collective-permute-start(f32[1,1024]{1,0:T(1,128)S(1)} %get-tuple-element.47), channel_id=1, source_target_pairs={{0,1},{1,0},{2,3},{3,2},{4,5},{5,4},{6,7},{7,6},{8,9},{9,8},{10,11... | collective-permute-start | bytes 12296 | tf_op jit(solution)/shard_map/ppermute | solution.py:290
  85.7 1.2 %collective-permute-start.17 = (f32[1,1024]{1,0:T(1,128)S(1)}, f32[1,1024]{1,0:T(1,128)S(1)}, u32[]{:S(2)}, u32[]{:S(2)}) collective-permute-start(f32[1,1024]{1,0:T(1,128)S(1)} %get-tuple-element.49), channel_id=1, source_target_pairs={{0,1},{1,0},{2,3},{3,2},{4,5},{5,4},{6,7},{7,6},{8,9},{9,8},{10,11... | collective-permute-start | bytes 12296 | tf_op jit(solution)/shard_map/ppermute | solution.py:290

commit v6 on v5

v6 whole, which is shorter than its diff:
```python
import functools
import math

import jax
import jax.numpy as jnp
from jax import lax
from jax.experimental import pallas as pl
from jax.experimental.pallas import tpu as pltpu
from jax.sharding import PartitionSpec as P

TILE = 512
CAP = 4
ITERS = 3


EPS = 0.02
NEG = -1e30
LN2 = math.log(2.0)
LANES = 128
SUBLANES = 8


def log2(value):
    return jnp.log(value) * (1.0 / LN2)


def log2_sum(values):
    peak = functools.reduce(jnp.maximum, values)
    total = functools.reduce(jnp.add, [jnp.exp2(v - peak) for v in values])
    return peak + log2(total)


def owner_of(id_ref, piece):
    near, far = piece
    side = id_ref[0] & 1
    mask = (0, 1 + side, 2 - side, 3)[near] + far
    return lax.shift_right_logical(id_ref[0], 1) ^ mask


def columns_of(width):
    return [slice(low, low + LANES) for low in range(0, width, LANES)]


def row_norms(block):
    rows, width = block.shape
    folded = None
    for cut in columns_of(width):
        part = block[:, cut].astype(jnp.float32)
        folded = part * part if folded is None else folded + part * part
    return jnp.sum(folded.T, axis=0, keepdims=True) * (1.0 / width)


def fill_scores(pieces, scale, id_ref, piece_refs, pool_ref, mask_ref, joined, out):
    own_rows = piece_refs[0].shape[0]
    for k, ref in enumerate(piece_refs):
        joined[k * own_rows : (k + 1) * own_rows, :] = ref[...]
    dots = lax.dot_general(
        joined[...],
        pool_ref[...],
        (((1,), (1,)), ((), ())),
        preferred_element_type=jnp.float32,
    )
    for k, piece in enumerate(pieces):
        rows = slice(k * own_rows, (k + 1) * own_rows)
        tile = lax.div(owner_of(id_ref, piece) * own_rows, TILE)
        out[rows, :] = dots[rows, :] * scale + mask_ref[pl.ds(tile, 1), :]


def diagonal(size):
    rows = lax.broadcasted_iota(jnp.int32, (size, size), 0)
    return rows == lax.broadcasted_iota(jnp.int32, (size, size), 1)


def row_pass(pieces, id_ref, shift, score_ref, held_ref):
    own_rows = held_ref.shape[1]
    eye = diagonal(own_rows)
    for k, piece in enumerate(pieces):
        block = score_ref[k * own_rows : (k + 1) * own_rows, :] + shift
        peak = jnp.max(block, axis=1, keepdims=True)
        total = jnp.sum(jnp.exp2(block - peak), axis=1, keepdims=True)
        sums = jnp.sum(jnp.where(eye, peak + log2(total), 0.0), axis=0, keepdims=True)
        held_ref[pl.ds(owner_of(id_ref, piece), 1), :] = sums


def copy_out(held_ref, out_ref):
    across = LANES // held_ref.shape[1]
    for line in range(out_ref.shape[1]):
        sources = [held_ref[line * across + k : line * across + k + 1, :] for k in range(across)]
        wide = jnp.concatenate(sources, axis=1)
        out_ref[:, line, :] = jnp.broadcast_to(wide, (out_ref.shape[0], LANES))


def prepare_kernel(list_ref, count_ref, own_ref, pool_ref, *refs):
    own_out, pool_out, own_norm_ref, pool_norm_ref, mask_ref, own_sem, pool_sem = refs
    own_copy = pltpu.make_async_copy(own_ref, own_out, own_sem)
    own_copy.start()
    pool_rows = pool_ref.shape[0]
    step = pool_rows // pool_sem.shape[0]
    copies = []
    for k in range(pool_sem.shape[0]):
        rows = pl.ds(k * step, step)
        copies.append(
            pltpu.make_async_copy(pool_ref.at[rows], pool_out.at[rows], pool_sem.at[k])
        )
        copies[-1].start()
    for t in range(mask_ref.shape[0]):
        for u in range(pool_rows // TILE):
            counted = jnp.int32(0)
            for k in range(CAP):
                hit = (list_ref[0, 0, k, 0] == t) & (list_ref[0, 0, k, 1] == u)
                counted += jnp.where(hit & (k < count_ref[0, 0]), 1, 0)
            offset = jnp.where(counted > 0, 0.0, NEG)
            mask_ref[t : t + 1, u * TILE : (u + 1) * TILE] = jnp.full((1, TILE), offset)
    own_copy.wait()
    own_norm_ref[...] = row_norms(own_out[...])
    for k, copy in enumerate(copies):
        copy.wait()
        for low in range(k * step, (k + 1) * step, LANES):
            rows = slice(low, low + LANES)
            pool_norm_ref[:, rows] = row_norms(pool_out[rows, :])


def early_kernel(pieces, scale, unit, id_ref, *refs):
    count = len(pieces)
    piece_refs, (pool_ref, norm_ref, mask_ref) = refs[:count], refs[count : count + 3]
    score_ref, held_ref, joined = refs[count + 3 :]
    fill_scores(pieces, scale, id_ref, piece_refs, pool_ref, mask_ref, joined, score_ref)
    held_ref[...] = jnp.zeros_like(held_ref)
    row_pass(pieces, id_ref, norm_ref[...] * (-1.0 / unit), score_ref, held_ref)


def late_kernel(pieces, scale, unit, id_ref, *refs):
    count = len(pieces)
    piece_refs, (pool_ref, norm_ref, mask_ref) = refs[:count], refs[count : count + 3]
    before_ref, score_ref, out_ref, joined, held_ref = refs[count + 3 :]
    fill_scores(pieces, scale, id_ref, piece_refs, pool_ref, mask_ref, joined, score_ref)
    held_ref[...] = before_ref[...]
    row_pass(pieces, id_ref, norm_ref[...] * (-1.0 / unit), score_ref, held_ref)
    copy_out(held_ref, out_ref)


def row_kernel(parts, id_ref, shift_ref, *refs):
    out_ref, held_ref = refs[-2:]
    shift = shift_ref[...]
    for ref, pieces in zip(refs[:-2], parts):
        row_pass(pieces, id_ref, shift, ref, held_ref)
    copy_out(held_ref, out_ref)


def column_kernel(parts, log_a, unit, id_ref, value_ref, norm_ref, *refs):
    scores, (out_ref, own_ref, held_ref) = refs[:-3], refs[-3:]
    shift = log_a - log2_sum([value_ref[k] for k in range(value_ref.shape[0])])
    size, own_rows = held_ref.shape
    pool_rows = out_ref.shape[1]
    across = LANES // own_rows
    for source in range(size):
        line, place = source // across, source % across
        held_ref[source : source + 1, :] = shift[
            line : line + 1, place * own_rows : (place + 1) * own_rows
        ]
    own_ref[...] = held_ref[pl.ds(owner_of(id_ref, (0, 0)), 1), :] * unit + norm_ref[...]
    eye = diagonal(own_rows)
    folded = (own_rows // SUBLANES, SUBLANES, pool_rows)
    blocks = [
        (ref, slice(k * own_rows, (k + 1) * own_rows), piece)
        for ref, pieces in zip(scores, parts)
        for k, piece in enumerate(pieces)
    ]
    columns = []
    peak = None
    for k, (ref, rows, piece) in enumerate(blocks):
        row = held_ref[pl.ds(owner_of(id_ref, piece), 1), :]
        columns.append(jnp.sum(jnp.where(eye, row, 0.0), axis=1, keepdims=True))
        high = jnp.max((ref[rows, :] + columns[k]).reshape(folded), axis=0)
        peak = high if peak is None else jnp.maximum(peak, high)
    peak = jnp.max(peak, axis=0, keepdims=True)
    total = jnp.zeros((SUBLANES, pool_rows), jnp.float32)
    for k, (ref, rows, _) in enumerate(blocks):
        total += jnp.sum(jnp.exp2(ref[rows, :] + (columns[k] - peak)).reshape(folded), axis=0)
    out_ref[...] = peak + log2(jnp.sum(total, axis=0, keepdims=True))


def call(kernel, shapes, scratch, scalars, arrays, flops, name):
    smem = pl.BlockSpec(memory_space=pltpu.SMEM)
    vmem = pl.BlockSpec(memory_space=pltpu.VMEM)
    moved = sum(a.size * a.dtype.itemsize for a in arrays) + 4 * sum(map(math.prod, shapes))
    return pl.pallas_call(
        kernel,
        out_shape=[jax.ShapeDtypeStruct(s, jnp.float32) for s in shapes],
        in_specs=[smem] * len(scalars) + [vmem] * len(arrays),
        out_specs=[vmem] * len(shapes),
        scratch_shapes=scratch,
        compiler_params=pltpu.CompilerParams(vmem_limit_bytes=3 * moved + (4 << 20)),
        cost_estimate=pl.CostEstimate(flops=flops, bytes_accessed=moved, transcendentals=0),
        name=name,
    )(*scalars, *arrays)


def prepare(tile_list, tile_count, own, pool, tiles):
    smem = pl.BlockSpec(memory_space=pltpu.SMEM)
    vmem = pl.BlockSpec(memory_space=pltpu.VMEM)
    chunks = 4
    shapes = [
        jax.ShapeDtypeStruct(own.shape, own.dtype),
        jax.ShapeDtypeStruct(pool.shape, pool.dtype),
        jax.ShapeDtypeStruct((1, own.shape[0]), jnp.float32),
        jax.ShapeDtypeStruct((1, pool.shape[0]), jnp.float32),
        jax.ShapeDtypeStruct((tiles, pool.shape[0]), jnp.float32),
    ]
    return pl.pallas_call(
        prepare_kernel,
        out_shape=shapes,
        in_specs=[smem, smem] + [pl.BlockSpec(memory_space=pl.ANY)] * 2,
        out_specs=[vmem] * len(shapes),
        scratch_shapes=[pltpu.SemaphoreType.DMA, pltpu.SemaphoreType.DMA((chunks,))],
        compiler_params=pltpu.CompilerParams(vmem_limit_bytes=16 << 20),
        cost_estimate=pl.CostEstimate(
            flops=2 * pool.size, bytes_accessed=4 * pool.size, transcendentals=0
        ),
        name="prepare",
    )(tile_list, tile_count, own, pool)


def body(samples, pool, tile_list, tile_count):
    own_rows, width = samples.shape[1:]
    size = lax.axis_size("pool")
    cores = lax.axis_size("samp")
    half_rows = own_rows * size
    pool_rows = pool.shape[0]
    lines = half_rows // LANES
    unit = EPS * LN2
    scale = 2.0 / (width * unit)
    log_a = -math.log2(half_rows * cores)
    log_b = -math.log2(pool_rows * size)
    own = samples.reshape(own_rows, width)

    def swap(value, masks):
        pairs = [
            (i * cores + c, (i ^ masks[c % 2]) * cores + c)
            for i in range(size)
            for c in range(cores)
        ]
        return lax.ppermute(value, ("pool", "samp"), pairs)

    def side_a(value):
        return swap(value, (1, 2))

    def side_b(value):
        return swap(value, (2, 1))

    def far(value, mask):
        return swap(value, (mask, mask))

    local = prepare(tile_list, tile_count, own, pool, half_rows // TILE)
    index = lax.axis_index("pool") * 2 + lax.axis_index("samp") % 2
    ids = [index.astype(jnp.int32).reshape(1)]

    far12, far4 = far(own, 12), far(own, 4)
    a, b = side_a(own), side_b(own)
    corner = side_b(a)
    far12, *local = lax.optimization_barrier((far12, *local))
    own_copy, pool_copy, own_norm, pool_norm, mask = local
    far8 = far(far12, 4)
    a4, b4 = side_a(far4), side_b(far4)
    a12, b12 = side_a(far12), side_b(far12)
    a8, b8 = side_a(far8), side_b(far8)
    corner12, corner4 = far(corner, 12), far(corner, 4)
    corner8 = far(corner12, 4)
    early = [own_copy, a, b, corner, far4, far12, far8, a4, b4, a12, b12, b8]
    early_pieces = [(0, 0), (1, 0), (2, 0), (3, 0), (0, 4), (0, 12), (0, 8)]
    early_pieces += [(1, 4), (2, 4), (1, 12), (2, 12), (2, 8)]
    late = [a8, corner4, corner12, corner8]
    late_pieces = [(1, 8), (3, 4), (3, 12), (3, 8)]
    step = 16
    while step < size:
        late += [far(piece, step) for piece in early + late]
        late_pieces += [(near, z + step) for near, z in early_pieces + late_pieces]
        step *= 2

    count = len(early) * own_rows
    score0, held = call(
        functools.partial(early_kernel, early_pieces, scale, unit),
        [(count, pool_rows), (size, own_rows)],
        [pltpu.VMEM((count, width), samples.dtype)],
        ids,
        early + [pool_copy, pool_norm, mask],
        2 * count * pool_rows * width,
        "early_scores",
    )
    *late, score0, held = lax.optimization_barrier((*late, score0, held))
    count = len(late) * own_rows
    score1, value = call(
        functools.partial(late_kernel, late_pieces, scale, unit),
        [(count, pool_rows), (size, lines, LANES)],
        [
            pltpu.VMEM((count, width), samples.dtype),
            pltpu.VMEM((size, own_rows), jnp.float32),
        ],
        ids,
        late + [pool_copy, pool_norm, mask, held],
        2 * count * pool_rows * width,
        "late_scores",
    )
    parts = [early_pieces, late_pieces]
    scores = [score0, score1]
    flops = 8 * half_rows * pool_rows
    held = [pltpu.VMEM((size, own_rows), jnp.float32)]
    for iteration in range(ITERS):
        if iteration > 0:
            kernel = functools.partial(row_kernel, parts)
            shapes = [(size, lines, LANES)]
            (value,) = call(kernel, shapes, held, ids, [shift] + scores, flops, "rows")
        value = lax.all_to_all(value, "pool", 0, 0, tiled=True)
        value, sample_potential = call(
            functools.partial(column_kernel, parts, log_a, unit),
            [(1, pool_rows), (1, own_rows)],
            held,
            ids,
            [value, own_norm] + scores,
            flops,
            "columns",
        )
        pairs = [(i, i ^ 1) for i in range(cores)]
        shift = log_b - log2_sum([value, lax.ppermute(value, "samp", pairs)])
    return sample_potential, (shift * unit + pool_norm).reshape(pool_rows)


def solution(mesh):
    placed = (
        P(("grp", "samp"), "pool", None),
        P(("grp", "pool"), None),
        P(("grp", "samp"), "pool", None, None),
        P(("grp", "samp"), "pool"),
    )
    return jax.shard_map(
        body,
        mesh=mesh,
        in_specs=placed,
        out_specs=(P(("grp", "samp"), "pool"), P(("grp", "pool"))),
        check_vma=False,
    )
```

time: 87.9 us -> 77.1 us (0.88)
  between operations: 6.48 us -> 1.39 us
  other arithmetic: 3.29 us -> 0.69 us
  Pallas kernels: 15.1 us -> 13.5 us
  local copies, waits for them, and re-layouts: 4.24 us -> 3.25 us
    or x1 -> x0, other arithmetic: 2.6 us -> none  [body(): code |= jnp.where(hit & (k < tile_count[0, 0]), size << u, 0)]
    slice x1 -> x0, local copies, waits for them, and re-layouts: 1.65 us -> none  [body(): hit = (tile == tile_list[0, 0, k, 0]) & (tile_list[0, 0, k, 1] == u)]
    pallas_call x8, Pallas kernels: 15.1 us -> 13.5 us  [the longest x7 11.7 us: call(): pl.pallas_call(kernel, out_shape=[jax.ShapeDtypeStruct(s, jnp.float32) fo...]
    unnamed x4 -> x5, local copies, waits for them, and re-layouts: 2.49 us -> 3.25 us
  transfers between devices with their start and end apart: 18 -> 18, of which waited for: 8 -> 8; matrix products, arithmetic and copies ran while one was open for 5% -> 1% of each run, Pallas kernels for 4% -> 7%
where the time goes in v6:
time: 77.1 us; the launch traced here: 76.8 us
  blocking collectives  30.4 us (39%)
  starting transfers between devices  17.2 us (22%)
  Pallas kernels  13.5 us (18%)
  waiting for transfers between devices  10.3 us (13%)
  local copies, waits for them, and re-layouts  3.25 us (4%)
  between operations  1.39 us (2%)
    all_to_all x3, blocking collectives, body(): value = lax.all_to_all(value, 'pool', 0, 0, tiled=True)  30.4 us
    ppermute x15, starting transfers between devices, swap(): return lax.ppermute(value, ('pool', 'samp'), pairs)  17.2 us
    pallas_call x7, Pallas kernels, call(): pl.pallas_call(kernel, out_shape=[jax.ShapeDtypeStruct(s, jnp.float32) fo...  11.7 us
    ppermute x15, waiting for transfers between devices, swap(): return lax.ppermute(value, ('pool', 'samp'), pairs)  6.85 us
    ppermute x3, waiting for transfers between devices, body(): shift = log_b - log2_sum([value, lax.ppermute(value, 'samp', pairs)])  3.49 us
    unnamed x5, local copies, waits for them, and re-layouts  3.25 us
    pallas_call x1, Pallas kernels, prepare(): pl.pallas_call(prepare_kernel, out_shape=shapes, in_specs=[smem, smem] +...  1.81 us
  transfers between devices with their start and end apart: 18, of which 8 were waited for; matrix products, arithmetic and copies ran while one was open for 1% of the time, Pallas kernels for 7%

profile of v6, /device:TPU:0, one launch (start us, length us, event | category | flops | bytes accessed | tf_op | source)
XLA Modules:
  0.0 76.8 jit_solution(2750974318107180850)
XLA Ops:
  0.6 5.1 %collective-permute-start = (bf16[64,1024]{1,0:T(8,128)(2,1)}, bf16[64,1024]{1,0:T(8,128)(2,1)S(1)}, u32[]{:S(2)}, u32[]{:S(2)}) collective-permute-start(bf16[64,1024]{1,0:T(8,128)(2,1)} %bitcast.3), channel_id=1, source_target_pairs={{0,24},{1,25},{2,26},{3,27},{4,28},{5,29},{6,30},{7,31},{8,16},{9,... | collective-permute-start | bytes 393224 | tf_op jit(solution)/shard_map/ppermute | solution.py:243
  5.7 1.5 %collective-permute-start.3 = (bf16[64,1024]{1,0:T(8,128)(2,1)}, bf16[64,1024]{1,0:T(8,128)(2,1)S(1)}, u32[]{:S(2)}, u32[]{:S(2)}) collective-permute-start(bf16[64,1024]{1,0:T(8,128)(2,1)} %bitcast.4), channel_id=1, source_target_pairs={{0,2},{1,5},{2,0},{3,7},{4,6},{5,1},{6,4},{7,3},{8,10},{9,13},{10,... | collective-permute-start | bytes 393224 | tf_op jit(solution)/shard_map/ppermute | solution.py:243
  7.2 1.5 %collective-permute-start.8 = (bf16[64,1024]{1,0:T(8,128)(2,1)}, bf16[64,1024]{1,0:T(8,128)(2,1)S(1)}, u32[]{:S(2)}, u32[]{:S(2)}) collective-permute-start(bf16[64,1024]{1,0:T(8,128)(2,1)} %bitcast.6), channel_id=1, source_target_pairs={{0,4},{1,3},{2,6},{3,1},{4,0},{5,7},{6,2},{7,5},{8,12},{9,11},{10,... | collective-permute-start | bytes 393224 | tf_op jit(solution)/shard_map/ppermute | solution.py:243
  10.2 1.6 %copy-done = bf16[1024,1024]{1,0:T(8,128)(2,1)S(1)} copy-done((bf16[1024,1024]{1,0:T(8,128)(2,1)S(1)}, bf16[1024,1024]{1,0:T(8,128)(2,1)}, u32[]{:S(2)}) %copy-start) | copy-done | bytes 2097176
  12.7 1.8 %prepare.1 = (bf16[64,1024]{1,0:T(8,128)(2,1)S(1)}, bf16[1024,1024]{1,0:T(8,128)(2,1)S(1)}, f32[1,64]{1,0:T(1,128)S(1)}, f32[1,1024]{1,0:T(1,128)S(1)}, f32[2,1024]{1,0:T(2,128)S(1)}) custom-call(s32[1,1,4,2]{3,2,1,0:T(4,128)S(1)} %copy.6.list_ref, s32[1,1]{1,0:T(1,128)S(6)} %copy.7.count_ref, bf16[64,1024]{1,0:T(8,128)(2,1)S(1)} %bitcast.7, ...), custom_call_target="tpu_custom_call" | custom-call | flops 2097152 | bytes 4194304 | tf_op jit(solution)/shard_map/prepare/pallas_call | solution.py:210
  15.1 2.0 %collective-permute-start.1 = (bf16[64,1024]{1,0:T(8,128)(2,1)S(1)}, bf16[64,1024]{1,0:T(8,128)(2,1)S(1)}, u32[]{:S(2)}, u32[]{:S(2)}) collective-permute-start(bf16[64,1024]{1,0:T(8,128)(2,1)S(1)} %collective-permute-done.refs_5_), channel_id=1, source_target_pairs={{0,8},{1,9},{2,10},{3,11},{4,12},{5,13},{6,14},{7,15},{8,0},{9,1},... | collective-permute-start | bytes 393224 | tf_op jit(solution)/shard_map/ppermute | solution.py:243
  17.6 1.5 %collective-permute-start.13 = (bf16[64,1024]{1,0:T(8,128)(2,1)S(1)}, bf16[64,1024]{1,0:T(8,128)(2,1)S(1)}, u32[]{:S(2)}, u32[]{:S(2)}) collective-permute-start(bf16[64,1024]{1,0:T(8,128)(2,1)S(1)} %collective-permute-done.refs_5_), channel_id=1, source_target_pairs={{0,4},{1,3},{2,6},{3,1},{4,0},{5,7},{6,2},{7,5},{8,12},{9,11},{10,... | collective-permute-start | bytes 393224 | tf_op jit(solution)/shard_map/ppermute | solution.py:243
  19.2 1.5 %collective-permute-start.10 = (bf16[64,1024]{1,0:T(8,128)(2,1)S(1)}, bf16[64,1024]{1,0:T(8,128)(2,1)S(1)}, u32[]{:S(2)}, u32[]{:S(2)}) collective-permute-start(bf16[64,1024]{1,0:T(8,128)(2,1)S(1)} %collective-permute-done.9.refs_4_), channel_id=1, source_target_pairs={{0,2},{1,5},{2,0},{3,7},{4,6},{5,1},{6,4},{7,3},{8,10},{9,13},{10,... | collective-permute-start | bytes 393224 | tf_op jit(solution)/shard_map/ppermute | solution.py:243
  21.8 1.6 %collective-permute-done.12.refs_9_ = bf16[64,1024]{1,0:T(8,128)(2,1)S(1)} collective-permute-done((bf16[64,1024]{1,0:T(8,128)(2,1)S(1)}, bf16[64,1024]{1,0:T(8,128)(2,1)S(1)}, u32[]{:S(2)}, u32[]{:S(2)}) %collective-permute-start.12) | collective-permute-done | bytes 131104 | tf_op jit(solution)/shard_map/ppermute | solution.py:243
  24.2 1.3 %collective-permute-start.2 = (bf16[64,1024]{1,0:T(8,128)(2,1)S(1)}, bf16[64,1024]{1,0:T(8,128)(2,1)S(1)}, u32[]{:S(2)}, u32[]{:S(2)}) collective-permute-start(bf16[64,1024]{1,0:T(8,128)(2,1)S(1)} %collective-permute-done.1.refs_6_), channel_id=1, source_target_pairs={{0,2},{1,5},{2,0},{3,7},{4,6},{5,1},{6,4},{7,3},{8,10},{9,13},{10,... | collective-permute-start | bytes 393224 | tf_op jit(solution)/shard_map/ppermute | solution.py:243
  26.3 2.6 %collective-permute-done.6.refs_2_ = bf16[64,1024]{1,0:T(8,128)(2,1)S(1)} collective-permute-done((bf16[64,1024]{1,0:T(8,128)(2,1)S(1)}, bf16[64,1024]{1,0:T(8,128)(2,1)S(1)}, u32[]{:S(2)}, u32[]{:S(2)}) %collective-permute-start.6) | collective-permute-done | bytes 131104 | tf_op jit(solution)/shard_map/ppermute | solution.py:243
  28.9 3.4 %early_scores.1 = (f32[768,1024]{1,0:T(8,128)S(1)}, f32[16,64]{1,0:T(8,128)S(1)}) custom-call(s32[1]{0:T(128)} %bitcast.id_ref, bf16[64,1024]{1,0:T(8,128)(2,1)S(1)} %get-tuple-element.33.refs_0_, bf16[64,1024]{1,0:T(8,128)(2,1)S(1)} %collective-permute-done.3.refs_1_, bf16[64,1024]{1,0:T(8,128)(2,1)S(1)} %collective-permute-done.8.refs_2_, ...), custom_call_target="tpu_custom_call" | custom-call | flops 1610612736 | bytes 6832128 | tf_op jit(solution)/shard_map/early_scores/pallas_call | solution.py:187
  32.4 1.5 %collective-permute-done.7.refs_3_ = bf16[64,1024]{1,0:T(8,128)(2,1)S(1)} collective-permute-done((bf16[64,1024]{1,0:T(8,128)(2,1)S(1)}, bf16[64,1024]{1,0:T(8,128)(2,1)S(1)}, u32[]{:S(2)}, u32[]{:S(2)}) %collective-permute-start.7) | collective-permute-done | bytes 131104 | tf_op jit(solution)/shard_map/ppermute | solution.py:243
  35.0 10.1 %all_to_all.15.value_ref = f32[16,8,128]{2,1,0:T(8,128)S(1)} all-to-all(f32[16,8,128]{2,1,0:T(8,128)S(1)} %get-tuple-element.44), channel_id=1, replica_groups=mesh['grp'=1,'pool'=16,'samp'=2] {'pool'}, dimensions={0} | all-to-all | bytes 131072 | tf_op jit(solution)/shard_map/all_to_all | solution.py:313
  45.1 1.6 %columns.3 = (f32[1,1024]{1,0:T(1,128)S(1)}, f32[1,64]{1,0:T(1,128)}) custom-call(s32[1]{0:T(128)} %bitcast.id_ref, f32[16,8,128]{2,1,0:T(8,128)S(1)} %all_to_all.15.value_ref, f32[1,64]{1,0:T(1,128)S(1)} %get-tuple-element.45.norm_ref, f32[768,1024]{1,0:T(8,128)S(1)} %get-tuple-element.46.refs_0_, f32[256,1024]{1,0:T(8,128)S(1)} %get-tuple-element.47.refs_1_), custom_call_target="tpu_custom_call" | custom-call | flops 8388608 | bytes 4264448 | tf_op jit(solution)/shard_map/columns/pallas_call | solution.py:187
  46.8 1.2 %collective-permute-done.15 = f32[1,1024]{1,0:T(1,128)S(1)} collective-permute-done((f32[1,1024]{1,0:T(1,128)S(1)}, f32[1,1024]{1,0:T(1,128)S(1)}, u32[]{:S(2)}, u32[]{:S(2)}) %collective-permute-start.15) | collective-permute-done | bytes 4128 | tf_op jit(solution)/shard_map/ppermute | solution.py:324
  48.0 1.1 %rows.2 = f32[16,8,128]{2,1,0:T(8,128)S(1)} custom-call(s32[1]{0:T(128)} %bitcast.id_ref, f32[1,1024]{1,0:T(1,128)S(1)} %add_subtract_fusion.1.shift_ref, f32[768,1024]{1,0:T(8,128)S(1)} %get-tuple-element.46.refs_0_, f32[256,1024]{1,0:T(8,128)S(1)} %get-tuple-element.47.refs_1_), custom_call_target="tpu_custom_call" | custom-call | flops 8388608 | bytes 4263936 | tf_op jit(solution)/shard_map/rows/pallas_call | solution.py:187
  49.1 10.1 %all_to_all.16.value_ref = f32[16,8,128]{2,1,0:T(8,128)S(1)} all-to-all(f32[16,8,128]{2,1,0:T(8,128)S(1)} %rows.2), channel_id=1, replica_groups=mesh['grp'=1,'pool'=16,'samp'=2] {'pool'}, dimensions={0} | all-to-all | bytes 131072 | tf_op jit(solution)/shard_map/all_to_all | solution.py:313
  59.2 1.6 %columns.4 = (f32[1,1024]{1,0:T(1,128)S(1)}, f32[1,64]{1,0:T(1,128)}) custom-call(s32[1]{0:T(128)} %bitcast.id_ref, f32[16,8,128]{2,1,0:T(8,128)S(1)} %all_to_all.16.value_ref, f32[1,64]{1,0:T(1,128)S(1)} %get-tuple-element.45.norm_ref, f32[768,1024]{1,0:T(8,128)S(1)} %get-tuple-element.46.refs_0_, f32[256,1024]{1,0:T(8,128)S(1)} %get-tuple-element.47.refs_1_), custom_call_target="tpu_custom_call" | custom-call | flops 8388608 | bytes 4264448 | tf_op jit(solution)/shard_map/columns/pallas_call | solution.py:187
  60.9 1.2 %collective-permute-done.16 = f32[1,1024]{1,0:T(1,128)S(1)} collective-permute-done((f32[1,1024]{1,0:T(1,128)S(1)}, f32[1,1024]{1,0:T(1,128)S(1)}, u32[]{:S(2)}, u32[]{:S(2)}) %collective-permute-start.16) | collective-permute-done | bytes 4128 | tf_op jit(solution)/shard_map/ppermute | solution.py:324
  62.1 1.1 %rows.3 = f32[16,8,128]{2,1,0:T(8,128)S(1)} custom-call(s32[1]{0:T(128)} %bitcast.id_ref, f32[1,1024]{1,0:T(1,128)S(1)} %add_subtract_fusion.shift_ref, f32[768,1024]{1,0:T(8,128)S(1)} %get-tuple-element.46.refs_0_, f32[256,1024]{1,0:T(8,128)S(1)} %get-tuple-element.47.refs_1_), custom_call_target="tpu_custom_call" | custom-call | flops 8388608 | bytes 4263936 | tf_op jit(solution)/shard_map/rows/pallas_call | solution.py:187
  63.2 10.1 %all_to_all.17.value_ref = f32[16,8,128]{2,1,0:T(8,128)S(1)} all-to-all(f32[16,8,128]{2,1,0:T(8,128)S(1)} %rows.3), channel_id=1, replica_groups=mesh['grp'=1,'pool'=16,'samp'=2] {'pool'}, dimensions={0} | all-to-all | bytes 131072 | tf_op jit(solution)/shard_map/all_to_all | solution.py:313
  73.3 1.6 %columns.5 = (f32[1,1024]{1,0:T(1,128)S(1)}, f32[1,64]{1,0:T(1,128)}) custom-call(s32[1]{0:T(128)} %bitcast.id_ref, f32[16,8,128]{2,1,0:T(8,128)S(1)} %all_to_all.17.value_ref, f32[1,64]{1,0:T(1,128)S(1)} %get-tuple-element.45.norm_ref, f32[768,1024]{1,0:T(8,128)S(1)} %get-tuple-element.46.refs_0_, f32[256,1024]{1,0:T(8,128)S(1)} %get-tuple-element.47.refs_1_), custom_call_target="tpu_custom_call" | custom-call | flops 8388608 | bytes 4264448 | tf_op jit(solution)/shard_map/columns/pallas_call | solution.py:187
  75.0 1.2 %collective-permute-done.17 = f32[1,1024]{1,0:T(1,128)S(1)} collective-permute-done((f32[1,1024]{1,0:T(1,128)S(1)}, f32[1,1024]{1,0:T(1,128)S(1)}, u32[]{:S(2)}, u32[]{:S(2)}) %collective-permute-start.17) | collective-permute-done | bytes 4128 | tf_op jit(solution)/shard_map/ppermute | solution.py:324
  (31 shorter events, 7.3 us)
Async XLA Ops:
  0.6 13.9 %collective-permute-start = (bf16[64,1024]{1,0:T(8,128)(2,1)}, bf16[64,1024]{1,0:T(8,128)(2,1)S(1)}, u32[]{:S(2)}, u32[]{:S(2)}) collective-permute-start(bf16[64,1024]{1,0:T(8,128)(2,1)} %bitcast.3), channel_id=1, source_target_pairs={{0,24},{1,25},{2,26},{3,27},{4,28},{5,29},{6,30},{7,31},{8,16},{9,... | collective-permute-start | bytes 393224 | tf_op jit(solution)/shard_map/ppermute | solution.py:243
  5.7 8.8 %collective-permute-start.3 = (bf16[64,1024]{1,0:T(8,128)(2,1)}, bf16[64,1024]{1,0:T(8,128)(2,1)S(1)}, u32[]{:S(2)}, u32[]{:S(2)}) collective-permute-start(bf16[64,1024]{1,0:T(8,128)(2,1)} %bitcast.4), channel_id=1, source_target_pairs={{0,2},{1,5},{2,0},{3,7},{4,6},{5,1},{6,4},{7,3},{8,10},{9,13},{10,... | collective-permute-start | bytes 393224 | tf_op jit(solution)/shard_map/ppermute | solution.py:243
  7.2 10.4 %collective-permute-start.9 = (bf16[64,1024]{1,0:T(8,128)(2,1)}, bf16[64,1024]{1,0:T(8,128)(2,1)S(1)}, u32[]{:S(2)}, u32[]{:S(2)}) collective-permute-start(bf16[64,1024]{1,0:T(8,128)(2,1)} %bitcast.5), channel_id=1, source_target_pairs={{0,8},{1,9},{2,10},{3,11},{4,12},{5,13},{6,14},{7,15},{8,0},{9,1},... | collective-permute-start | bytes 393224 | tf_op jit(solution)/shard_map/ppermute | solution.py:243
  7.2 11.9 %collective-permute-start.8 = (bf16[64,1024]{1,0:T(8,128)(2,1)}, bf16[64,1024]{1,0:T(8,128)(2,1)S(1)}, u32[]{:S(2)}, u32[]{:S(2)}) collective-permute-start(bf16[64,1024]{1,0:T(8,128)(2,1)} %bitcast.6), channel_id=1, source_target_pairs={{0,4},{1,3},{2,6},{3,1},{4,0},{5,7},{6,2},{7,5},{8,12},{9,11},{10,... | collective-permute-start | bytes 393224 | tf_op jit(solution)/shard_map/ppermute | solution.py:243
  10.2 1.6 %copy-start = (bf16[1024,1024]{1,0:T(8,128)(2,1)S(1)}, bf16[1024,1024]{1,0:T(8,128)(2,1)}, u32[]{:S(2)}) copy-start(bf16[1024,1024]{1,0:T(8,128)(2,1)} %pool_ref.1) | copy-start | bytes 6291460
  11.8 0.9 %copy-start.1 = (bf16[1,64,1024]{2,1,0:T(8,128)(2,1)S(1)}, bf16[1,64,1024]{2,1,0:T(8,128)(2,1)}, u32[]{:S(2)}) copy-start(bf16[1,64,1024]{2,1,0:T(8,128)(2,1)} %param.4) | copy-start | bytes 393220
  14.5 6.4 %collective-permute-start.4 = (bf16[64,1024]{1,0:T(8,128)(2,1)S(1)}, bf16[64,1024]{1,0:T(8,128)(2,1)S(1)}, u32[]{:S(2)}, u32[]{:S(2)}) collective-permute-start(bf16[64,1024]{1,0:T(8,128)(2,1)S(1)} %collective-permute-done.3.refs_1_), channel_id=1, source_target_pairs={{0,4},{1,3},{2,6},{3,1},{4,0},{5,7},{6,2},{7,5},{8,12},{9,11},{10,... | collective-permute-start | bytes 393224 | tf_op jit(solution)/shard_map/ppermute | solution.py:243
  15.1 6.7 %collective-permute-start.1 = (bf16[64,1024]{1,0:T(8,128)(2,1)S(1)}, bf16[64,1024]{1,0:T(8,128)(2,1)S(1)}, u32[]{:S(2)}, u32[]{:S(2)}) collective-permute-start(bf16[64,1024]{1,0:T(8,128)(2,1)S(1)} %collective-permute-done.refs_5_), channel_id=1, source_target_pairs={{0,8},{1,9},{2,10},{3,11},{4,12},{5,13},{6,14},{7,15},{8,0},{9,1},... | collective-permute-start | bytes 393224 | tf_op jit(solution)/shard_map/ppermute | solution.py:243
  17.1 6.4 %collective-permute-start.12 = (bf16[64,1024]{1,0:T(8,128)(2,1)S(1)}, bf16[64,1024]{1,0:T(8,128)(2,1)S(1)}, u32[]{:S(2)}, u32[]{:S(2)}) collective-permute-start(bf16[64,1024]{1,0:T(8,128)(2,1)S(1)} %collective-permute-done.refs_5_), channel_id=1, source_target_pairs={{0,2},{1,5},{2,0},{3,7},{4,6},{5,1},{6,4},{7,3},{8,10},{9,13},{10,... | collective-permute-start | bytes 393224 | tf_op jit(solution)/shard_map/ppermute | solution.py:243
  17.6 6.6 %collective-permute-start.13 = (bf16[64,1024]{1,0:T(8,128)(2,1)S(1)}, bf16[64,1024]{1,0:T(8,128)(2,1)S(1)}, u32[]{:S(2)}, u32[]{:S(2)}) collective-permute-start(bf16[64,1024]{1,0:T(8,128)(2,1)S(1)} %collective-permute-done.refs_5_), channel_id=1, source_target_pairs={{0,4},{1,3},{2,6},{3,1},{4,0},{5,7},{6,2},{7,5},{8,12},{9,11},{10,... | collective-permute-start | bytes 393224 | tf_op jit(solution)/shard_map/ppermute | solution.py:243
  19.2 7.1 %collective-permute-start.10 = (bf16[64,1024]{1,0:T(8,128)(2,1)S(1)}, bf16[64,1024]{1,0:T(8,128)(2,1)S(1)}, u32[]{:S(2)}, u32[]{:S(2)}) collective-permute-start(bf16[64,1024]{1,0:T(8,128)(2,1)S(1)} %collective-permute-done.9.refs_4_), channel_id=1, source_target_pairs={{0,2},{1,5},{2,0},{3,7},{4,6},{5,1},{6,4},{7,3},{8,10},{9,13},{10,... | collective-permute-start | bytes 393224 | tf_op jit(solution)/shard_map/ppermute | solution.py:243
  20.9 8.0 %collective-permute-start.6 = (bf16[64,1024]{1,0:T(8,128)(2,1)S(1)}, bf16[64,1024]{1,0:T(8,128)(2,1)S(1)}, u32[]{:S(2)}, u32[]{:S(2)}) collective-permute-start(bf16[64,1024]{1,0:T(8,128)(2,1)S(1)} %collective-permute-done.4.refs_3_), channel_id=1, source_target_pairs={{0,24},{1,25},{2,26},{3,27},{4,28},{5,29},{6,30},{7,31},{8,16},{9,... | collective-permute-start | bytes 393224 | tf_op jit(solution)/shard_map/ppermute | solution.py:243
  21.8 7.1 %collective-permute-start.11 = (bf16[64,1024]{1,0:T(8,128)(2,1)S(1)}, bf16[64,1024]{1,0:T(8,128)(2,1)}, u32[]{:S(2)}, u32[]{:S(2)}) collective-permute-start(bf16[64,1024]{1,0:T(8,128)(2,1)S(1)} %collective-permute-done.9.refs_4_), channel_id=1, source_target_pairs={{0,4},{1,3},{2,6},{3,1},{4,0},{5,7},{6,2},{7,5},{8,12},{9,11},{10,... | collective-permute-start | bytes 393224 | tf_op jit(solution)/shard_map/ppermute | solution.py:243
  23.5 5.5 %collective-permute-start.14 = (bf16[64,1024]{1,0:T(8,128)(2,1)S(1)}, bf16[64,1024]{1,0:T(8,128)(2,1)}, u32[]{:S(2)}, u32[]{:S(2)}) collective-permute-start(bf16[64,1024]{1,0:T(8,128)(2,1)S(1)} %collective-permute-done.1.refs_6_), channel_id=1, source_target_pairs={{0,4},{1,3},{2,6},{3,1},{4,0},{5,7},{6,2},{7,5},{8,12},{9,11},{10,... | collective-permute-start | bytes 393224 | tf_op jit(solution)/shard_map/ppermute | solution.py:243
  24.2 8.1 %collective-permute-start.2 = (bf16[64,1024]{1,0:T(8,128)(2,1)S(1)}, bf16[64,1024]{1,0:T(8,128)(2,1)S(1)}, u32[]{:S(2)}, u32[]{:S(2)}) collective-permute-start(bf16[64,1024]{1,0:T(8,128)(2,1)S(1)} %collective-permute-done.1.refs_6_), channel_id=1, source_target_pairs={{0,2},{1,5},{2,0},{3,7},{4,6},{5,1},{6,4},{7,3},{8,10},{9,13},{10,... | collective-permute-start | bytes 393224 | tf_op jit(solution)/shard_map/ppermute | solution.py:243
  26.3 6.1 %collective-permute-start.5 = (bf16[64,1024]{1,0:T(8,128)(2,1)S(1)}, bf16[64,1024]{1,0:T(8,128)(2,1)S(1)}, u32[]{:S(2)}, u32[]{:S(2)}) collective-permute-start(bf16[64,1024]{1,0:T(8,128)(2,1)S(1)} %collective-permute-done.4.refs_3_), channel_id=1, source_target_pairs={{0,8},{1,9},{2,10},{3,11},{4,12},{5,13},{6,14},{7,15},{8,0},{9,1},... | collective-permute-start | bytes 393224 | tf_op jit(solution)/shard_map/ppermute | solution.py:243
  28.9 5.0 %collective-permute-start.7 = (bf16[64,1024]{1,0:T(8,128)(2,1)S(1)}, bf16[64,1024]{1,0:T(8,128)(2,1)S(1)}, u32[]{:S(2)}, u32[]{:S(2)}) collective-permute-start(bf16[64,1024]{1,0:T(8,128)(2,1)S(1)} %collective-permute-done.6.refs_2_), channel_id=1, source_target_pairs={{0,8},{1,9},{2,10},{3,11},{4,12},{5,13},{6,14},{7,15},{8,0},{9,1},... | collective-permute-start | bytes 393224 | tf_op jit(solution)/shard_map/ppermute | solution.py:243
  46.8 1.2 %collective-permute-start.15 = (f32[1,1024]{1,0:T(1,128)S(1)}, f32[1,1024]{1,0:T(1,128)S(1)}, u32[]{:S(2)}, u32[]{:S(2)}) collective-permute-start(f32[1,1024]{1,0:T(1,128)S(1)} %get-tuple-element.48), channel_id=1, source_target_pairs={{0,1},{1,0},{2,3},{3,2},{4,5},{5,4},{6,7},{7,6},{8,9},{9,8},{10,11... | collective-permute-start | bytes 12296 | tf_op jit(solution)/shard_map/ppermute | solution.py:324
  60.9 1.2 %collective-permute-start.16 = (f32[1,1024]{1,0:T(1,128)S(1)}, f32[1,1024]{1,0:T(1,128)S(1)}, u32[]{:S(2)}, u32[]{:S(2)}) collective-permute-start(f32[1,1024]{1,0:T(1,128)S(1)} %get-tuple-element.49), channel_id=1, source_target_pairs={{0,1},{1,0},{2,3},{3,2},{4,5},{5,4},{6,7},{7,6},{8,9},{9,8},{10,11... | collective-permute-start | bytes 12296 | tf_op jit(solution)/shard_map/ppermute | solution.py:324
  75.0 1.2 %collective-permute-start.17 = (f32[1,1024]{1,0:T(1,128)S(1)}, f32[1,1024]{1,0:T(1,128)S(1)}, u32[]{:S(2)}, u32[]{:S(2)}) collective-permute-start(f32[1,1024]{1,0:T(1,128)S(1)} %get-tuple-element.51), channel_id=1, source_target_pairs={{0,1},{1,0},{2,3},{3,2},{4,5},{5,4},{6,7},{7,6},{8,9},{9,8},{10,11... | collective-permute-start | bytes 12296 | tf_op jit(solution)/shard_map/ppermute | solution.py:324

commit v7 on v6

--- a/solution.py
+++ b/solution.py
@@ -90,8 +90,13 @@
         out_ref[:, line, :] = jnp.broadcast_to(wide, (out_ref.shape[0], LANES))
 
 
-def prepare_kernel(list_ref, count_ref, own_ref, pool_ref, *refs):
-    own_out, pool_out, own_norm_ref, pool_norm_ref, mask_ref, own_sem, pool_sem = refs
+def prepare_kernel(list_hbm, count_hbm, own_ref, pool_ref, *refs):
+    own_out, pool_out, own_norm_ref, pool_norm_ref, mask_ref = refs[:5]
+    list_ref, count_ref, list_sem, count_sem, own_sem, pool_sem = refs[5:]
+    list_copy = pltpu.make_async_copy(list_hbm, list_ref, list_sem)
+    count_copy = pltpu.make_async_copy(count_hbm, count_ref, count_sem)
+    list_copy.start()
+    count_copy.start()
     own_copy = pltpu.make_async_copy(own_ref, own_out, own_sem)
     own_copy.start()
     pool_rows = pool_ref.shape[0]
@@ -103,11 +108,13 @@
             pltpu.make_async_copy(pool_ref.at[rows], pool_out.at[rows], pool_sem.at[k])
         )
         copies[-1].start()
+    list_copy.wait()
+    count_copy.wait()
     for t in range(mask_ref.shape[0]):
         for u in range(pool_rows // TILE):
             counted = jnp.int32(0)
             for k in range(CAP):
-                hit = (list_ref[0, 0, k, 0] == t) & (list_ref[0, 0, k, 1] == u)
+                hit = (list_ref[0, 0, 0, k] == t) & (list_ref[0, 0, 1, k] == u)
                 counted += jnp.where(hit & (k < count_ref[0, 0]), 1, 0)
             offset = jnp.where(counted > 0, 0.0, NEG)
             mask_ref[t : t + 1, u * TILE : (u + 1) * TILE] = jnp.full((1, TILE), offset)
@@ -158,7 +165,8 @@
         held_ref[source : source + 1, :] = shift[
             line : line + 1, place * own_rows : (place + 1) * own_rows
         ]
-    own_ref[...] = held_ref[pl.ds(owner_of(id_ref, (0, 0)), 1), :] * unit + norm_ref[...]
+    own = held_ref[pl.ds(owner_of(id_ref, (0, 0)), 1), :] * unit + norm_ref[...]
+    own_ref[...] = jnp.broadcast_to(jnp.concatenate([own] * across, axis=1), own_ref.shape)
     eye = diagonal(own_rows)
     folded = (own_rows // SUBLANES, SUBLANES, pool_rows)
     blocks = [
@@ -197,7 +205,6 @@
 
 
 def prepare(tile_list, tile_count, own, pool, tiles):
-    smem = pl.BlockSpec(memory_space=pltpu.SMEM)
     vmem = pl.BlockSpec(memory_space=pltpu.VMEM)
     chunks = 4
     shapes = [
@@ -210,9 +217,16 @@
     return pl.pallas_call(
         prepare_kernel,
         out_shape=shapes,
-        in_specs=[smem, smem] + [pl.BlockSpec(memory_space=pl.ANY)] * 2,
+        in_specs=[pl.BlockSpec(memory_space=pltpu.HBM)] * 4,
         out_specs=[vmem] * len(shapes),
-        scratch_shapes=[pltpu.SemaphoreType.DMA, pltpu.SemaphoreType.DMA((chunks,))],
+        scratch_shapes=[
+            pltpu.SMEM(tile_list.shape, jnp.int32),
+            pltpu.SMEM(tile_count.shape, jnp.int32),
+            pltpu.SemaphoreType.DMA,
+            pltpu.SemaphoreType.DMA,
+            pltpu.SemaphoreType.DMA,
+            pltpu.SemaphoreType.DMA((chunks,)),
+        ],
         compiler_params=pltpu.CompilerParams(vmem_limit_bytes=16 << 20),
         cost_estimate=pl.CostEstimate(
             flops=2 * pool.size, bytes_accessed=4 * pool.size, transcendentals=0
@@ -251,13 +265,14 @@
     def far(value, mask):
         return swap(value, (mask, mask))
 
-    local = prepare(tile_list, tile_count, own, pool, half_rows // TILE)
     index = lax.axis_index("pool") * 2 + lax.axis_index("samp") % 2
     ids = [index.astype(jnp.int32).reshape(1)]
 
     far12, far4 = far(own, 12), far(own, 4)
     a, b = side_a(own), side_b(own)
-    corner = side_b(a)
+    corner = swap(own, (3, 3))
+    pairs = tile_list.swapaxes(2, 3)
+    local = prepare(pairs, tile_count, own, pool, half_rows // TILE)
     far12, *local = lax.optimization_barrier((far12, *local))
     own_copy, pool_copy, own_norm, pool_norm, mask = local
     far8 = far(far12, 4)
@@ -313,7 +328,7 @@
         value = lax.all_to_all(value, "pool", 0, 0, tiled=True)
         value, sample_potential = call(
             functools.partial(column_kernel, parts, log_a, unit),
-            [(1, pool_rows), (1, own_rows)],
+            [(1, pool_rows), (SUBLANES, LANES)],
             held,
             ids,
             [value, own_norm] + scores,
@@ -322,7 +337,7 @@
         )
         pairs = [(i, i ^ 1) for i in range(cores)]
         shift = log_b - log2_sum([value, lax.ppermute(value, "samp", pairs)])
-    return sample_potential, (shift * unit + pool_norm).reshape(pool_rows)
+    return sample_potential[:1, :own_rows], (shift * unit + pool_norm).reshape(pool_rows)
 
 
 def solution(mesh):

time: 77.1 us -> 75.5 us (0.979)
  waiting for transfers between devices: 10.3 us -> 7.42 us
  starting transfers between devices: 17.2 us -> 19.3 us
  Pallas kernels: 13.5 us -> 11.7 us
    ppermute x15, waiting for transfers between devices: 6.85 us -> 4.47 us  [swap(): return lax.ppermute(value, ('pool', 'samp'), pairs)]
    ppermute x15, starting transfers between devices: 17.2 us -> 19.1 us  [swap(): return lax.ppermute(value, ('pool', 'samp'), pairs)]
    pallas_call x7, Pallas kernels: 11.7 us -> 10.2 us  [call(): pl.pallas_call(kernel, out_shape=[jax.ShapeDtypeStruct(s, jnp.float32) fo...]
    unnamed x5 -> x6, local copies, waits for them, and re-layouts: 3.25 us -> 3.17 us
where the time goes in v7:
time: 75.5 us; the launch traced here: 75.2 us
  blocking collectives  31 us (41%)
  starting transfers between devices  19.3 us (26%)
  Pallas kernels  11.7 us (15%)
  waiting for transfers between devices  7.42 us (10%)
  local copies, waits for them, and re-layouts  3.68 us (5%)
  between operations  1.41 us (2%)
    all_to_all x3, blocking collectives, body(): value = lax.all_to_all(value, 'pool', 0, 0, tiled=True)  31 us
    ppermute x15, starting transfers between devices, swap(): return lax.ppermute(value, ('pool', 'samp'), pairs)  19.1 us
    pallas_call x7, Pallas kernels, call(): pl.pallas_call(kernel, out_shape=[jax.ShapeDtypeStruct(s, jnp.float32) fo...  10.2 us
    ppermute x15, waiting for transfers between devices, swap(): return lax.ppermute(value, ('pool', 'samp'), pairs)  4.47 us
    unnamed x6, local copies, waits for them, and re-layouts  3.17 us
    ppermute x3, waiting for transfers between devices, body(): shift = log_b - log2_sum([value, lax.ppermute(value, 'samp', pairs)])  2.94 us
    pallas_call x1, Pallas kernels, prepare(): pl.pallas_call(prepare_kernel, out_shape=shapes, in_specs=[pl.BlockSpec(m...  1.51 us
  transfers between devices with their start and end apart: 18, of which 8 were waited for; matrix products, arithmetic and copies ran while one was open for 1% of the time, Pallas kernels for 7%

profile of v7, /device:TPU:0, one launch (start us, length us, event | category | flops | bytes accessed | tf_op | source)
XLA Modules:
  0.0 75.2 jit_solution(5978023342980106089)
XLA Ops:
  0.6 5.1 %collective-permute-start = (bf16[64,1024]{1,0:T(8,128)(2,1)}, bf16[64,1024]{1,0:T(8,128)(2,1)S(1)}, u32[]{:S(2)}, u32[]{:S(2)}) collective-permute-start(bf16[64,1024]{1,0:T(8,128)(2,1)} %bitcast.4), channel_id=1, source_target_pairs={{0,24},{1,25},{2,26},{3,27},{4,28},{5,29},{6,30},{7,31},{8,16},{9,... | collective-permute-start | bytes 393224 | tf_op jit(solution)/shard_map/ppermute | solution.py:257
  5.7 2.4 %collective-permute-start.3 = (bf16[64,1024]{1,0:T(8,128)(2,1)}, bf16[64,1024]{1,0:T(8,128)(2,1)S(1)}, u32[]{:S(2)}, u32[]{:S(2)}) collective-permute-start(bf16[64,1024]{1,0:T(8,128)(2,1)} %bitcast.6), channel_id=1, source_target_pairs={{0,6},{1,7},{2,4},{3,5},{4,2},{5,3},{6,0},{7,1},{8,14},{9,15},{10,... | collective-permute-start | bytes 393224 | tf_op jit(solution)/shard_map/ppermute | solution.py:257
  9.9 1.6 %copy-done = bf16[1024,1024]{1,0:T(8,128)(2,1)S(1)} copy-done((bf16[1024,1024]{1,0:T(8,128)(2,1)S(1)}, bf16[1024,1024]{1,0:T(8,128)(2,1)}, u32[]{:S(2)}) %copy-start) | copy-done | bytes 2097176
  13.1 1.5 %prepare.1 = (bf16[64,1024]{1,0:T(8,128)(2,1)S(1)}, bf16[1024,1024]{1,0:T(8,128)(2,1)S(1)}, f32[1,64]{1,0:T(1,128)S(1)}, f32[1,1024]{1,0:T(1,128)S(1)}, f32[2,1024]{1,0:T(2,128)S(1)}) custom-call(s32[1,1,2,4]{3,2,1,0:T(2,128)S(1)} %bitcast.10, s32[1,1]{1,0:T(1,128)S(6)} %copy.6.count_hbm, bf16[64,1024]{1,0:T(8,128)(2,1)S(1)} %bitcast.9, ...), custom_call_target="tpu_custom_call" | custom-call | flops 2097152 | bytes 4194304 | tf_op jit(solution)/shard_map/prepare/pallas_call | solution.py:217
  14.6 2.1 %collective-permute-start.1 = (bf16[64,1024]{1,0:T(8,128)(2,1)S(1)}, bf16[64,1024]{1,0:T(8,128)(2,1)S(1)}, u32[]{:S(2)}, u32[]{:S(2)}) collective-permute-start(bf16[64,1024]{1,0:T(8,128)(2,1)S(1)} %collective-permute-done.refs_5_), channel_id=1, source_target_pairs={{0,8},{1,9},{2,10},{3,11},{4,12},{5,13},{6,14},{7,15},{8,0},{9,1},... | collective-permute-start | bytes 393224 | tf_op jit(solution)/shard_map/ppermute | solution.py:257
  16.7 1.5 %collective-permute-start.12 = (bf16[64,1024]{1,0:T(8,128)(2,1)S(1)}, bf16[64,1024]{1,0:T(8,128)(2,1)S(1)}, u32[]{:S(2)}, u32[]{:S(2)}) collective-permute-start(bf16[64,1024]{1,0:T(8,128)(2,1)S(1)} %collective-permute-done.refs_5_), channel_id=1, source_target_pairs={{0,2},{1,5},{2,0},{3,7},{4,6},{5,1},{6,4},{7,3},{8,10},{9,13},{10,... | collective-permute-start | bytes 393224 | tf_op jit(solution)/shard_map/ppermute | solution.py:257
  18.2 1.5 %collective-permute-start.13 = (bf16[64,1024]{1,0:T(8,128)(2,1)S(1)}, bf16[64,1024]{1,0:T(8,128)(2,1)S(1)}, u32[]{:S(2)}, u32[]{:S(2)}) collective-permute-start(bf16[64,1024]{1,0:T(8,128)(2,1)S(1)} %collective-permute-done.refs_5_), channel_id=1, source_target_pairs={{0,4},{1,3},{2,6},{3,1},{4,0},{5,7},{6,2},{7,5},{8,12},{9,11},{10,... | collective-permute-start | bytes 393224 | tf_op jit(solution)/shard_map/ppermute | solution.py:257
  20.5 1.4 %collective-permute-start.11 = (bf16[64,1024]{1,0:T(8,128)(2,1)S(1)}, bf16[64,1024]{1,0:T(8,128)(2,1)}, u32[]{:S(2)}, u32[]{:S(2)}) collective-permute-start(bf16[64,1024]{1,0:T(8,128)(2,1)S(1)} %collective-permute-done.9.refs_4_), channel_id=1, source_target_pairs={{0,4},{1,3},{2,6},{3,1},{4,0},{5,7},{6,2},{7,5},{8,12},{9,11},{10,... | collective-permute-start | bytes 393224 | tf_op jit(solution)/shard_map/ppermute | solution.py:257
  21.9 1.2 %collective-permute-done.12.refs_9_ = bf16[64,1024]{1,0:T(8,128)(2,1)S(1)} collective-permute-done((bf16[64,1024]{1,0:T(8,128)(2,1)S(1)}, bf16[64,1024]{1,0:T(8,128)(2,1)S(1)}, u32[]{:S(2)}, u32[]{:S(2)}) %collective-permute-start.12) | collective-permute-done | bytes 131104 | tf_op jit(solution)/shard_map/ppermute | solution.py:257
  23.1 1.5 %collective-permute-start.14 = (bf16[64,1024]{1,0:T(8,128)(2,1)S(1)}, bf16[64,1024]{1,0:T(8,128)(2,1)}, u32[]{:S(2)}, u32[]{:S(2)}) collective-permute-start(bf16[64,1024]{1,0:T(8,128)(2,1)S(1)} %collective-permute-done.1.refs_6_), channel_id=1, source_target_pairs={{0,4},{1,3},{2,6},{3,1},{4,0},{5,7},{6,2},{7,5},{8,12},{9,11},{10,... | collective-permute-start | bytes 393224 | tf_op jit(solution)/shard_map/ppermute | solution.py:257
  25.8 1.4 %collective-permute-start.2 = (bf16[64,1024]{1,0:T(8,128)(2,1)S(1)}, bf16[64,1024]{1,0:T(8,128)(2,1)S(1)}, u32[]{:S(2)}, u32[]{:S(2)}) collective-permute-start(bf16[64,1024]{1,0:T(8,128)(2,1)S(1)} %collective-permute-done.1.refs_6_), channel_id=1, source_target_pairs={{0,2},{1,5},{2,0},{3,7},{4,6},{5,1},{6,4},{7,3},{8,10},{9,13},{10,... | collective-permute-start | bytes 393224 | tf_op jit(solution)/shard_map/ppermute | solution.py:257
  28.3 3.4 %early_scores.1 = (f32[768,1024]{1,0:T(8,128)S(1)}, f32[16,64]{1,0:T(8,128)S(1)}) custom-call(s32[1]{0:T(128)} %bitcast.id_ref, bf16[64,1024]{1,0:T(8,128)(2,1)S(1)} %get-tuple-element.33.refs_0_, bf16[64,1024]{1,0:T(8,128)(2,1)S(1)} %collective-permute-done.7.refs_1_, bf16[64,1024]{1,0:T(8,128)(2,1)S(1)} %collective-permute-done.8.refs_2_, ...), custom_call_target="tpu_custom_call" | custom-call | flops 1610612736 | bytes 6832128 | tf_op jit(solution)/shard_map/early_scores/pallas_call | solution.py:195
  31.8 1.2 %collective-permute-done.6.refs_3_ = bf16[64,1024]{1,0:T(8,128)(2,1)S(1)} collective-permute-done((bf16[64,1024]{1,0:T(8,128)(2,1)S(1)}, bf16[64,1024]{1,0:T(8,128)(2,1)S(1)}, u32[]{:S(2)}, u32[]{:S(2)}) %collective-permute-start.6) | collective-permute-done | bytes 131104 | tf_op jit(solution)/shard_map/ppermute | solution.py:257
  32.9 1.1 %late_scores.1 = (f32[256,1024]{1,0:T(8,128)S(1)}, f32[16,8,128]{2,1,0:T(8,128)S(1)}) custom-call(s32[1]{0:T(128)} %bitcast.id_ref, bf16[64,1024]{1,0:T(8,128)(2,1)S(1)} %collective-permute-done.2.refs_0_, bf16[64,1024]{1,0:T(8,128)(2,1)S(1)} %collective-permute-done.4.refs_1_, bf16[64,1024]{1,0:T(8,128)(2,1)S(1)} %collective-permute-done.5.refs_2_, ...), custom_call_target="tpu_custom_call" | custom-call | flops 536870912 | bytes 3751936 | tf_op jit(solution)/shard_map/late_scores/pallas_call | solution.py:195
  34.1 10.7 %all_to_all.15.value_ref = f32[16,8,128]{2,1,0:T(8,128)S(1)} all-to-all(f32[16,8,128]{2,1,0:T(8,128)S(1)} %get-tuple-element.44), channel_id=1, replica_groups=mesh['grp'=1,'pool'=16,'samp'=2] {'pool'}, dimensions={0} | all-to-all | bytes 131072 | tf_op jit(solution)/shard_map/all_to_all | solution.py:328
  44.8 1.2 %columns.3 = (f32[1,1024]{1,0:T(1,128)S(1)}, f32[8,128]{1,0:T(8,128)}) custom-call(s32[1]{0:T(128)} %bitcast.id_ref, f32[16,8,128]{2,1,0:T(8,128)S(1)} %all_to_all.15.value_ref, f32[1,64]{1,0:T(1,128)S(1)} %get-tuple-element.45.norm_ref, f32[768,1024]{1,0:T(8,128)S(1)} %get-tuple-element.46.refs_0_, f32[256,1024]{1,0:T(8,128)S(1)} %get-tuple-element.47.refs_1_), custom_call_target="tpu_custom_call" | custom-call | flops 8388608 | bytes 4268288 | tf_op jit(solution)/shard_map/columns/pallas_call | solution.py:195
  46.0 1.2 %collective-permute-done.15 = f32[1,1024]{1,0:T(1,128)S(1)} collective-permute-done((f32[1,1024]{1,0:T(1,128)S(1)}, f32[1,1024]{1,0:T(1,128)S(1)}, u32[]{:S(2)}, u32[]{:S(2)}) %collective-permute-start.15) | collective-permute-done | bytes 4128 | tf_op jit(solution)/shard_map/ppermute | solution.py:339
  47.2 1.1 %rows.2 = f32[16,8,128]{2,1,0:T(8,128)S(1)} custom-call(s32[1]{0:T(128)} %bitcast.id_ref, f32[1,1024]{1,0:T(1,128)S(1)} %add_subtract_fusion.1.shift_ref, f32[768,1024]{1,0:T(8,128)S(1)} %get-tuple-element.46.refs_0_, f32[256,1024]{1,0:T(8,128)S(1)} %get-tuple-element.47.refs_1_), custom_call_target="tpu_custom_call" | custom-call | flops 8388608 | bytes 4263936 | tf_op jit(solution)/shard_map/rows/pallas_call | solution.py:195
  48.4 10.1 %all_to_all.16.value_ref = f32[16,8,128]{2,1,0:T(8,128)S(1)} all-to-all(f32[16,8,128]{2,1,0:T(8,128)S(1)} %rows.2), channel_id=1, replica_groups=mesh['grp'=1,'pool'=16,'samp'=2] {'pool'}, dimensions={0} | all-to-all | bytes 131072 | tf_op jit(solution)/shard_map/all_to_all | solution.py:328
  58.5 1.2 %columns.4 = (f32[1,1024]{1,0:T(1,128)S(1)}, f32[8,128]{1,0:T(8,128)}) custom-call(s32[1]{0:T(128)} %bitcast.id_ref, f32[16,8,128]{2,1,0:T(8,128)S(1)} %all_to_all.16.value_ref, f32[1,64]{1,0:T(1,128)S(1)} %get-tuple-element.45.norm_ref, f32[768,1024]{1,0:T(8,128)S(1)} %get-tuple-element.46.refs_0_, f32[256,1024]{1,0:T(8,128)S(1)} %get-tuple-element.47.refs_1_), custom_call_target="tpu_custom_call" | custom-call | flops 8388608 | bytes 4268288 | tf_op jit(solution)/shard_map/columns/pallas_call | solution.py:195
  59.7 1.2 %collective-permute-done.16 = f32[1,1024]{1,0:T(1,128)S(1)} collective-permute-done((f32[1,1024]{1,0:T(1,128)S(1)}, f32[1,1024]{1,0:T(1,128)S(1)}, u32[]{:S(2)}, u32[]{:S(2)}) %collective-permute-start.16) | collective-permute-done | bytes 4128 | tf_op jit(solution)/shard_map/ppermute | solution.py:339
  60.9 1.1 %rows.3 = f32[16,8,128]{2,1,0:T(8,128)S(1)} custom-call(s32[1]{0:T(128)} %bitcast.id_ref, f32[1,1024]{1,0:T(1,128)S(1)} %add_subtract_fusion.shift_ref, f32[768,1024]{1,0:T(8,128)S(1)} %get-tuple-element.46.refs_0_, f32[256,1024]{1,0:T(8,128)S(1)} %get-tuple-element.47.refs_1_), custom_call_target="tpu_custom_call" | custom-call | flops 8388608 | bytes 4263936 | tf_op jit(solution)/shard_map/rows/pallas_call | solution.py:195
  62.0 10.1 %all_to_all.17.value_ref = f32[16,8,128]{2,1,0:T(8,128)S(1)} all-to-all(f32[16,8,128]{2,1,0:T(8,128)S(1)} %rows.3), channel_id=1, replica_groups=mesh['grp'=1,'pool'=16,'samp'=2] {'pool'}, dimensions={0} | all-to-all | bytes 131072 | tf_op jit(solution)/shard_map/all_to_all | solution.py:328
  72.2 1.1 %columns.5 = (f32[1,1024]{1,0:T(1,128)S(1)}, f32[8,128]{1,0:T(8,128)S(1)}) custom-call(s32[1]{0:T(128)} %bitcast.id_ref, f32[16,8,128]{2,1,0:T(8,128)S(1)} %all_to_all.17.value_ref, f32[1,64]{1,0:T(1,128)S(1)} %get-tuple-element.45.norm_ref, f32[768,1024]{1,0:T(8,128)S(1)} %get-tuple-element.46.refs_0_, f32[256,1024]{1,0:T(8,128)S(1)} %get-tuple-element.47.refs_1_), custom_call_target="tpu_custom_call" | custom-call | flops 8388608 | bytes 4268288 | tf_op jit(solution)/shard_map/columns/pallas_call | solution.py:195
  (33 shorter events, 7.8 us)
Async XLA Ops:
  0.6 14.0 %collective-permute-start = (bf16[64,1024]{1,0:T(8,128)(2,1)}, bf16[64,1024]{1,0:T(8,128)(2,1)S(1)}, u32[]{:S(2)}, u32[]{:S(2)}) collective-permute-start(bf16[64,1024]{1,0:T(8,128)(2,1)} %bitcast.4), channel_id=1, source_target_pairs={{0,24},{1,25},{2,26},{3,27},{4,28},{5,29},{6,30},{7,31},{8,16},{9,... | collective-permute-start | bytes 393224 | tf_op jit(solution)/shard_map/ppermute | solution.py:257
  5.7 10.9 %collective-permute-start.9 = (bf16[64,1024]{1,0:T(8,128)(2,1)}, bf16[64,1024]{1,0:T(8,128)(2,1)S(1)}, u32[]{:S(2)}, u32[]{:S(2)}) collective-permute-start(bf16[64,1024]{1,0:T(8,128)(2,1)} %bitcast.5), channel_id=1, source_target_pairs={{0,8},{1,9},{2,10},{3,11},{4,12},{5,13},{6,14},{7,15},{8,0},{9,1},... | collective-permute-start | bytes 393224 | tf_op jit(solution)/shard_map/ppermute | solution.py:257
  5.7 12.4 %collective-permute-start.3 = (bf16[64,1024]{1,0:T(8,128)(2,1)}, bf16[64,1024]{1,0:T(8,128)(2,1)S(1)}, u32[]{:S(2)}, u32[]{:S(2)}) collective-permute-start(bf16[64,1024]{1,0:T(8,128)(2,1)} %bitcast.6), channel_id=1, source_target_pairs={{0,6},{1,7},{2,4},{3,5},{4,2},{5,3},{6,0},{7,1},{8,14},{9,15},{10,... | collective-permute-start | bytes 393224 | tf_op jit(solution)/shard_map/ppermute | solution.py:257
  8.2 11.5 %collective-permute-start.7 = (bf16[64,1024]{1,0:T(8,128)(2,1)}, bf16[64,1024]{1,0:T(8,128)(2,1)S(1)}, u32[]{:S(2)}, u32[]{:S(2)}) collective-permute-start(bf16[64,1024]{1,0:T(8,128)(2,1)} %bitcast.7), channel_id=1, source_target_pairs={{0,2},{1,5},{2,0},{3,7},{4,6},{5,1},{6,4},{7,3},{8,10},{9,13},{10,... | collective-permute-start | bytes 393224 | tf_op jit(solution)/shard_map/ppermute | solution.py:257
  8.7 11.5 %collective-permute-start.8 = (bf16[64,1024]{1,0:T(8,128)(2,1)}, bf16[64,1024]{1,0:T(8,128)(2,1)S(1)}, u32[]{:S(2)}, u32[]{:S(2)}) collective-permute-start(bf16[64,1024]{1,0:T(8,128)(2,1)} %bitcast.8), channel_id=1, source_target_pairs={{0,4},{1,3},{2,6},{3,1},{4,0},{5,7},{6,2},{7,5},{8,12},{9,11},{10,... | collective-permute-start | bytes 393224 | tf_op jit(solution)/shard_map/ppermute | solution.py:257
  9.9 1.6 %copy-start = (bf16[1024,1024]{1,0:T(8,128)(2,1)S(1)}, bf16[1024,1024]{1,0:T(8,128)(2,1)}, u32[]{:S(2)}) copy-start(bf16[1024,1024]{1,0:T(8,128)(2,1)} %pool_ref.1) | copy-start | bytes 6291460
  11.5 0.9 %copy-start.1 = (bf16[1,64,1024]{2,1,0:T(8,128)(2,1)S(1)}, bf16[1,64,1024]{2,1,0:T(8,128)(2,1)}, u32[]{:S(2)}) copy-start(bf16[1,64,1024]{2,1,0:T(8,128)(2,1)} %param.4) | copy-start | bytes 393220
  12.4 0.7 copy-start.2
  14.6 5.9 %collective-permute-start.1 = (bf16[64,1024]{1,0:T(8,128)(2,1)S(1)}, bf16[64,1024]{1,0:T(8,128)(2,1)S(1)}, u32[]{:S(2)}, u32[]{:S(2)}) collective-permute-start(bf16[64,1024]{1,0:T(8,128)(2,1)S(1)} %collective-permute-done.refs_5_), channel_id=1, source_target_pairs={{0,8},{1,9},{2,10},{3,11},{4,12},{5,13},{6,14},{7,15},{8,0},{9,1},... | collective-permute-start | bytes 393224 | tf_op jit(solution)/shard_map/ppermute | solution.py:257
  16.7 6.4 %collective-permute-start.12 = (bf16[64,1024]{1,0:T(8,128)(2,1)S(1)}, bf16[64,1024]{1,0:T(8,128)(2,1)S(1)}, u32[]{:S(2)}, u32[]{:S(2)}) collective-permute-start(bf16[64,1024]{1,0:T(8,128)(2,1)S(1)} %collective-permute-done.refs_5_), channel_id=1, source_target_pairs={{0,2},{1,5},{2,0},{3,7},{4,6},{5,1},{6,4},{7,3},{8,10},{9,13},{10,... | collective-permute-start | bytes 393224 | tf_op jit(solution)/shard_map/ppermute | solution.py:257
  18.2 6.4 %collective-permute-start.13 = (bf16[64,1024]{1,0:T(8,128)(2,1)S(1)}, bf16[64,1024]{1,0:T(8,128)(2,1)S(1)}, u32[]{:S(2)}, u32[]{:S(2)}) collective-permute-start(bf16[64,1024]{1,0:T(8,128)(2,1)S(1)} %collective-permute-done.refs_5_), channel_id=1, source_target_pairs={{0,4},{1,3},{2,6},{3,1},{4,0},{5,7},{6,2},{7,5},{8,12},{9,11},{10,... | collective-permute-start | bytes 393224 | tf_op jit(solution)/shard_map/ppermute | solution.py:257
  19.7 6.1 %collective-permute-start.10 = (bf16[64,1024]{1,0:T(8,128)(2,1)S(1)}, bf16[64,1024]{1,0:T(8,128)(2,1)S(1)}, u32[]{:S(2)}, u32[]{:S(2)}) collective-permute-start(bf16[64,1024]{1,0:T(8,128)(2,1)S(1)} %collective-permute-done.9.refs_4_), channel_id=1, source_target_pairs={{0,2},{1,5},{2,0},{3,7},{4,6},{5,1},{6,4},{7,3},{8,10},{9,13},{10,... | collective-permute-start | bytes 393224 | tf_op jit(solution)/shard_map/ppermute | solution.py:257
  20.2 7.7 %collective-permute-start.5 = (bf16[64,1024]{1,0:T(8,128)(2,1)S(1)}, bf16[64,1024]{1,0:T(8,128)(2,1)S(1)}, u32[]{:S(2)}, u32[]{:S(2)}) collective-permute-start(bf16[64,1024]{1,0:T(8,128)(2,1)S(1)} %collective-permute-done.3.refs_3_), channel_id=1, source_target_pairs={{0,24},{1,25},{2,26},{3,27},{4,28},{5,29},{6,30},{7,31},{8,16},{9,... | collective-permute-start | bytes 393224 | tf_op jit(solution)/shard_map/ppermute | solution.py:257
  20.5 7.6 %collective-permute-start.11 = (bf16[64,1024]{1,0:T(8,128)(2,1)S(1)}, bf16[64,1024]{1,0:T(8,128)(2,1)}, u32[]{:S(2)}, u32[]{:S(2)}) collective-permute-start(bf16[64,1024]{1,0:T(8,128)(2,1)S(1)} %collective-permute-done.9.refs_4_), channel_id=1, source_target_pairs={{0,4},{1,3},{2,6},{3,1},{4,0},{5,7},{6,2},{7,5},{8,12},{9,11},{10,... | collective-permute-start | bytes 393224 | tf_op jit(solution)/shard_map/ppermute | solution.py:257
  23.1 5.3 %collective-permute-start.14 = (bf16[64,1024]{1,0:T(8,128)(2,1)S(1)}, bf16[64,1024]{1,0:T(8,128)(2,1)}, u32[]{:S(2)}, u32[]{:S(2)}) collective-permute-start(bf16[64,1024]{1,0:T(8,128)(2,1)S(1)} %collective-permute-done.1.refs_6_), channel_id=1, source_target_pairs={{0,4},{1,3},{2,6},{3,1},{4,0},{5,7},{6,2},{7,5},{8,12},{9,11},{10,... | collective-permute-start | bytes 393224 | tf_op jit(solution)/shard_map/ppermute | solution.py:257
  24.6 7.1 %collective-permute-start.4 = (bf16[64,1024]{1,0:T(8,128)(2,1)S(1)}, bf16[64,1024]{1,0:T(8,128)(2,1)S(1)}, u32[]{:S(2)}, u32[]{:S(2)}) collective-permute-start(bf16[64,1024]{1,0:T(8,128)(2,1)S(1)} %collective-permute-done.3.refs_3_), channel_id=1, source_target_pairs={{0,8},{1,9},{2,10},{3,11},{4,12},{5,13},{6,14},{7,15},{8,0},{9,1},... | collective-permute-start | bytes 393224 | tf_op jit(solution)/shard_map/ppermute | solution.py:257
  25.8 5.9 %collective-permute-start.2 = (bf16[64,1024]{1,0:T(8,128)(2,1)S(1)}, bf16[64,1024]{1,0:T(8,128)(2,1)S(1)}, u32[]{:S(2)}, u32[]{:S(2)}) collective-permute-start(bf16[64,1024]{1,0:T(8,128)(2,1)S(1)} %collective-permute-done.1.refs_6_), channel_id=1, source_target_pairs={{0,2},{1,5},{2,0},{3,7},{4,6},{5,1},{6,4},{7,3},{8,10},{9,13},{10,... | collective-permute-start | bytes 393224 | tf_op jit(solution)/shard_map/ppermute | solution.py:257
  28.0 5.0 %collective-permute-start.6 = (bf16[64,1024]{1,0:T(8,128)(2,1)S(1)}, bf16[64,1024]{1,0:T(8,128)(2,1)S(1)}, u32[]{:S(2)}, u32[]{:S(2)}) collective-permute-start(bf16[64,1024]{1,0:T(8,128)(2,1)S(1)} %collective-permute-done.5.refs_2_), channel_id=1, source_target_pairs={{0,8},{1,9},{2,10},{3,11},{4,12},{5,13},{6,14},{7,15},{8,0},{9,1},... | collective-permute-start | bytes 393224 | tf_op jit(solution)/shard_map/ppermute | solution.py:257
  46.0 1.2 %collective-permute-start.15 = (f32[1,1024]{1,0:T(1,128)S(1)}, f32[1,1024]{1,0:T(1,128)S(1)}, u32[]{:S(2)}, u32[]{:S(2)}) collective-permute-start(f32[1,1024]{1,0:T(1,128)S(1)} %get-tuple-element.48), channel_id=1, source_target_pairs={{0,1},{1,0},{2,3},{3,2},{4,5},{5,4},{6,7},{7,6},{8,9},{9,8},{10,11... | collective-permute-start | bytes 12296 | tf_op jit(solution)/shard_map/ppermute | solution.py:339
  59.6 1.2 %collective-permute-start.16 = (f32[1,1024]{1,0:T(1,128)S(1)}, f32[1,1024]{1,0:T(1,128)S(1)}, u32[]{:S(2)}, u32[]{:S(2)}) collective-permute-start(f32[1,1024]{1,0:T(1,128)S(1)} %get-tuple-element.49), channel_id=1, source_target_pairs={{0,1},{1,0},{2,3},{3,2},{4,5},{5,4},{6,7},{7,6},{8,9},{9,8},{10,11... | collective-permute-start | bytes 12296 | tf_op jit(solution)/shard_map/ppermute | solution.py:339
  73.3 1.2 %collective-permute-start.17 = (f32[1,1024]{1,0:T(1,128)S(1)}, f32[1,1024]{1,0:T(1,128)S(1)}, u32[]{:S(2)}, u32[]{:S(2)}) collective-permute-start(f32[1,1024]{1,0:T(1,128)S(1)} %get-tuple-element.51), channel_id=1, source_target_pairs={{0,1},{1,0},{2,3},{3,2},{4,5},{5,4},{6,7},{7,6},{8,9},{9,8},{10,11... | collective-permute-start | bytes 12296 | tf_op jit(solution)/shard_map/ppermute | solution.py:339

commit v8 on v7

--- a/solution.py
+++ b/solution.py
@@ -51,9 +51,11 @@
 
 
 def fill_scores(pieces, scale, id_ref, piece_refs, pool_ref, mask_ref, joined, out):
-    own_rows = piece_refs[0].shape[0]
-    for k, ref in enumerate(piece_refs):
-        joined[k * own_rows : (k + 1) * own_rows, :] = ref[...]
+    own_rows = joined.shape[0] // len(pieces)
+    low = 0
+    for ref in piece_refs:
+        joined[low : low + ref.shape[0], :] = ref[...]
+        low += ref.shape[0]
     dots = lax.dot_general(
         joined[...],
         pool_ref[...],
@@ -128,18 +130,15 @@
 
 
 def early_kernel(pieces, scale, unit, id_ref, *refs):
-    count = len(pieces)
-    piece_refs, (pool_ref, norm_ref, mask_ref) = refs[:count], refs[count : count + 3]
-    score_ref, held_ref, joined = refs[count + 3 :]
+    *piece_refs, pool_ref, norm_ref, mask_ref, score_ref, held_ref, joined = refs
     fill_scores(pieces, scale, id_ref, piece_refs, pool_ref, mask_ref, joined, score_ref)
     held_ref[...] = jnp.zeros_like(held_ref)
     row_pass(pieces, id_ref, norm_ref[...] * (-1.0 / unit), score_ref, held_ref)
 
 
 def late_kernel(pieces, scale, unit, id_ref, *refs):
-    count = len(pieces)
-    piece_refs, (pool_ref, norm_ref, mask_ref) = refs[:count], refs[count : count + 3]
-    before_ref, score_ref, out_ref, joined, held_ref = refs[count + 3 :]
+    *piece_refs, pool_ref, norm_ref, mask_ref, before_ref = refs[:-4]
+    score_ref, out_ref, joined, held_ref = refs[-4:]
     fill_scores(pieces, scale, id_ref, piece_refs, pool_ref, mask_ref, joined, score_ref)
     held_ref[...] = before_ref[...]
     row_pass(pieces, id_ref, norm_ref[...] * (-1.0 / unit), score_ref, held_ref)
@@ -273,26 +272,26 @@
     corner = swap(own, (3, 3))
     pairs = tile_list.swapaxes(2, 3)
     local = prepare(pairs, tile_count, own, pool, half_rows // TILE)
-    far12, *local = lax.optimization_barrier((far12, *local))
+    far12, ids[0], *local = lax.optimization_barrier((far12, ids[0], *local))
     own_copy, pool_copy, own_norm, pool_norm, mask = local
     far8 = far(far12, 4)
-    a4, b4 = side_a(far4), side_b(far4)
-    a12, b12 = side_a(far12), side_b(far12)
+    pair = jnp.concatenate([far4, far12], axis=0)
+    a_pair, b_pair = side_a(pair), side_b(pair)
     a8, b8 = side_a(far8), side_b(far8)
     corner12, corner4 = far(corner, 12), far(corner, 4)
     corner8 = far(corner12, 4)
-    early = [own_copy, a, b, corner, far4, far12, far8, a4, b4, a12, b12, b8]
+    early = [own_copy, a, b, corner, far4, far12, far8, a_pair, b_pair, b8]
     early_pieces = [(0, 0), (1, 0), (2, 0), (3, 0), (0, 4), (0, 12), (0, 8)]
-    early_pieces += [(1, 4), (2, 4), (1, 12), (2, 12), (2, 8)]
+    early_pieces += [(1, 4), (1, 12), (2, 4), (2, 12), (2, 8)]
     late = [a8, corner4, corner12, corner8]
     late_pieces = [(1, 8), (3, 4), (3, 12), (3, 8)]
     step = 16
     while step < size:
-        late += [far(piece, step) for piece in early + late]
-        late_pieces += [(near, z + step) for near, z in early_pieces + late_pieces]
+        late = late + [far(piece, step) for piece in early + late]
+        late_pieces = late_pieces + [(near, z + step) for near, z in early_pieces + late_pieces]
         step *= 2
 
-    count = len(early) * own_rows
+    count = len(early_pieces) * own_rows
     score0, held = call(
         functools.partial(early_kernel, early_pieces, scale, unit),
         [(count, pool_rows), (size, own_rows)],
@@ -303,7 +302,7 @@
         "early_scores",
     )
     *late, score0, held = lax.optimization_barrier((*late, score0, held))
-    count = len(late) * own_rows
+    count = len(late_pieces) * own_rows
     score1, value = call(
         functools.partial(late_kernel, late_pieces, scale, unit),
         [(count, pool_rows), (size, lines, LANES)],

time: 75.5 us -> 74.4 us (0.985)
  Pallas kernels: 11.7 us -> 10.8 us
    pallas_call x7, Pallas kernels: 10.2 us -> 9.24 us  [call(): pl.pallas_call(kernel, out_shape=[jax.ShapeDtypeStruct(s, jnp.float32) fo...]
    ppermute x15 -> x13, waiting for transfers between devices: 4.47 us -> 5.05 us  [swap(): return lax.ppermute(value, ('pool', 'samp'), pairs)]
    ppermute x15 -> x13, starting transfers between devices: 19.1 us -> 18.7 us  [swap(): return lax.ppermute(value, ('pool', 'samp'), pairs)]
    unnamed x6 -> x7, local copies, waits for them, and re-layouts: 3.17 us -> 3.18 us
  transfers between devices with their start and end apart: 18 -> 16, of which waited for: 8 -> 9; matrix products, arithmetic and copies ran while one was open for 1% -> 1% of each run, Pallas kernels for 7% -> 5%
where the time goes in v8:
time: 74.4 us; the launch traced here: 74.1 us
  blocking collectives  30.6 us (41%)
  starting transfers between devices  18.9 us (25%)
  Pallas kernels  10.8 us (15%)
  waiting for transfers between devices  7.99 us (11%)
  local copies, waits for them, and re-layouts  3.7 us (5%)
  between operations  1.43 us (2%)
    all_to_all x3, blocking collectives, body(): value = lax.all_to_all(value, 'pool', 0, 0, tiled=True)  30.6 us
    ppermute x13, starting transfers between devices, swap(): return lax.ppermute(value, ('pool', 'samp'), pairs)  18.7 us
    pallas_call x7, Pallas kernels, call(): pl.pallas_call(kernel, out_shape=[jax.ShapeDtypeStruct(s, jnp.float32) fo...  9.24 us
    ppermute x13, waiting for transfers between devices, swap(): return lax.ppermute(value, ('pool', 'samp'), pairs)  5.05 us
    unnamed x7, local copies, waits for them, and re-layouts  3.18 us
    ppermute x3, waiting for transfers between devices, body(): shift = log_b - log2_sum([value, lax.ppermute(value, 'samp', pairs)])  2.94 us
    pallas_call x1, Pallas kernels, prepare(): pl.pallas_call(prepare_kernel, out_shape=shapes, in_specs=[pl.BlockSpec(m...  1.51 us
  transfers between devices with their start and end apart: 16, of which 9 were waited for; matrix products, arithmetic and copies ran while one was open for 1% of the time, Pallas kernels for 5%

profile of v8, /device:TPU:0, one launch (start us, length us, event | category | flops | bytes accessed | tf_op | source)
XLA Modules:
  0.0 74.1 jit_solution(2191047910506513942)
XLA Ops:
  0.6 5.1 %collective-permute-start = (bf16[64,1024]{1,0:T(8,128)(2,1)}, bf16[64,1024]{1,0:T(8,128)(2,1)S(1)}, u32[]{:S(2)}, u32[]{:S(2)}) collective-permute-start(bf16[64,1024]{1,0:T(8,128)(2,1)} %bitcast.4), channel_id=1, source_target_pairs={{0,24},{1,25},{2,26},{3,27},{4,28},{5,29},{6,30},{7,31},{8,16},{9,... | collective-permute-start | bytes 393224 | tf_op jit(solution)/shard_map/ppermute | solution.py:256
  5.7 2.4 %collective-permute-start.3 = (bf16[64,1024]{1,0:T(8,128)(2,1)}, bf16[64,1024]{1,0:T(8,128)(2,1)S(1)}, u32[]{:S(2)}, u32[]{:S(2)}) collective-permute-start(bf16[64,1024]{1,0:T(8,128)(2,1)} %bitcast.6), channel_id=1, source_target_pairs={{0,6},{1,7},{2,4},{3,5},{4,2},{5,3},{6,0},{7,1},{8,14},{9,15},{10,... | collective-permute-start | bytes 393224 | tf_op jit(solution)/shard_map/ppermute | solution.py:256
  9.4 1.6 %copy-done = bf16[1024,1024]{1,0:T(8,128)(2,1)S(1)} copy-done((bf16[1024,1024]{1,0:T(8,128)(2,1)S(1)}, bf16[1024,1024]{1,0:T(8,128)(2,1)}, u32[]{:S(2)}) %copy-start) | copy-done | bytes 2097176
  12.6 1.5 %prepare.1 = (bf16[64,1024]{1,0:T(8,128)(2,1)S(1)}, bf16[1024,1024]{1,0:T(8,128)(2,1)S(1)}, f32[1,64]{1,0:T(1,128)S(1)}, f32[1,1024]{1,0:T(1,128)S(1)}, f32[2,1024]{1,0:T(2,128)S(1)}) custom-call(s32[1,1,2,4]{3,2,1,0:T(2,128)S(1)} %bitcast.10, s32[1,1]{1,0:T(1,128)S(6)} %copy.7.count_hbm, bf16[64,1024]{1,0:T(8,128)(2,1)S(1)} %bitcast.8, ...), custom_call_target="tpu_custom_call" | custom-call | flops 2097152 | bytes 4194304 | tf_op jit(solution)/shard_map/prepare/pallas_call | solution.py:216
  14.1 1.6 %collective-permute-start.10 = (bf16[128,1024]{1,0:T(8,128)(2,1)S(1)}, bf16[128,1024]{1,0:T(8,128)(2,1)S(1)}, u32[]{:S(2)}, u32[]{:S(2)}) collective-permute-start(bf16[128,1024]{1,0:T(8,128)(2,1)S(1)} %constant_dynamic-update-slice_fusion), channel_id=1, source_target_pairs={{0,2},{1,5},{2,0},{3,7},{4,6},{5,1},{6,4},{7,3},{8,10},{9,13},{10,... | collective-permute-start | bytes 786440 | tf_op jit(solution)/shard_map/ppermute | solution.py:256
  16.2 2.0 %collective-permute-start.1 = (bf16[64,1024]{1,0:T(8,128)(2,1)S(1)}, bf16[64,1024]{1,0:T(8,128)(2,1)S(1)}, u32[]{:S(2)}, u32[]{:S(2)}) collective-permute-start(bf16[64,1024]{1,0:T(8,128)(2,1)S(1)} %collective-permute-done.refs_5_), channel_id=1, source_target_pairs={{0,8},{1,9},{2,10},{3,11},{4,12},{5,13},{6,14},{7,15},{8,0},{9,1},... | collective-permute-start | bytes 393224 | tf_op jit(solution)/shard_map/ppermute | solution.py:256
  18.2 1.5 %collective-permute-start.8 = (bf16[64,1024]{1,0:T(8,128)(2,1)S(1)}, bf16[64,1024]{1,0:T(8,128)(2,1)S(1)}, u32[]{:S(2)}, u32[]{:S(2)}) collective-permute-start(bf16[64,1024]{1,0:T(8,128)(2,1)S(1)} %bitcast.9), channel_id=1, source_target_pairs={{0,4},{1,3},{2,6},{3,1},{4,0},{5,7},{6,2},{7,5},{8,12},{9,11},{10,... | collective-permute-start | bytes 393224 | tf_op jit(solution)/shard_map/ppermute | solution.py:256
  20.0 1.2 %collective-permute-done.1.refs_6_ = bf16[64,1024]{1,0:T(8,128)(2,1)S(1)} collective-permute-done((bf16[64,1024]{1,0:T(8,128)(2,1)S(1)}, bf16[64,1024]{1,0:T(8,128)(2,1)S(1)}, u32[]{:S(2)}, u32[]{:S(2)}) %collective-permute-start.1) | collective-permute-done | bytes 131104 | tf_op jit(solution)/shard_map/ppermute | solution.py:256
  21.2 2.0 %collective-permute-start.12 = (bf16[64,1024]{1,0:T(8,128)(2,1)S(1)}, bf16[64,1024]{1,0:T(8,128)(2,1)S(1)}, u32[]{:S(2)}, u32[]{:S(2)}) collective-permute-start(bf16[64,1024]{1,0:T(8,128)(2,1)S(1)} %collective-permute-done.1.refs_6_), channel_id=1, source_target_pairs={{0,4},{1,3},{2,6},{3,1},{4,0},{5,7},{6,2},{7,5},{8,12},{9,11},{10,... | collective-permute-start | bytes 393224 | tf_op jit(solution)/shard_map/ppermute | solution.py:256
  23.5 2.0 %collective-permute-start.4 = (bf16[64,1024]{1,0:T(8,128)(2,1)S(1)}, bf16[64,1024]{1,0:T(8,128)(2,1)S(1)}, u32[]{:S(2)}, u32[]{:S(2)}) collective-permute-start(bf16[64,1024]{1,0:T(8,128)(2,1)S(1)} %collective-permute-done.3.refs_3_), channel_id=1, source_target_pairs={{0,8},{1,9},{2,10},{3,11},{4,12},{5,13},{6,14},{7,15},{8,0},{9,1},... | collective-permute-start | bytes 393224 | tf_op jit(solution)/shard_map/ppermute | solution.py:256
  25.5 1.0 %collective-permute-done.5.refs_2_ = bf16[64,1024]{1,0:T(8,128)(2,1)S(1)} collective-permute-done((bf16[64,1024]{1,0:T(8,128)(2,1)S(1)}, bf16[64,1024]{1,0:T(8,128)(2,1)S(1)}, u32[]{:S(2)}, u32[]{:S(2)}) %collective-permute-start.5) | collective-permute-done | bytes 131104 | tf_op jit(solution)/shard_map/ppermute | solution.py:256
  27.3 2.4 %early_scores.1 = (f32[768,1024]{1,0:T(8,128)S(1)}, f32[16,64]{1,0:T(8,128)S(1)}) custom-call(s32[1]{0:T(128)} %bitcast.1.id_ref, bf16[64,1024]{1,0:T(8,128)(2,1)S(1)} %get-tuple-element.35.refs_0_, bf16[64,1024]{1,0:T(8,128)(2,1)S(1)} %collective-permute-done.7.refs_1_, bf16[64,1024]{1,0:T(8,128)(2,1)S(1)} %collective-permute-done.8.refs_2_, ...), custom_call_target="tpu_custom_call" | custom-call | flops 1610612736 | bytes 6832128 | tf_op jit(solution)/shard_map/early_scores/pallas_call | solution.py:194
  29.8 1.7 %collective-permute-done.2.refs_0_ = bf16[64,1024]{1,0:T(8,128)(2,1)S(1)} collective-permute-done((bf16[64,1024]{1,0:T(8,128)(2,1)S(1)}, bf16[64,1024]{1,0:T(8,128)(2,1)S(1)}, u32[]{:S(2)}, u32[]{:S(2)}) %collective-permute-start.2) | collective-permute-done | bytes 131104 | tf_op jit(solution)/shard_map/ppermute | solution.py:256
  32.2 1.1 %late_scores.1 = (f32[256,1024]{1,0:T(8,128)S(1)}, f32[16,8,128]{2,1,0:T(8,128)S(1)}) custom-call(s32[1]{0:T(128)} %bitcast.1.id_ref, bf16[64,1024]{1,0:T(8,128)(2,1)S(1)} %collective-permute-done.2.refs_0_, bf16[64,1024]{1,0:T(8,128)(2,1)S(1)} %collective-permute-done.4.refs_1_, bf16[64,1024]{1,0:T(8,128)(2,1)S(1)} %collective-permute-done.5.refs_2_, ...), custom_call_target="tpu_custom_call" | custom-call | flops 536870912 | bytes 3751936 | tf_op jit(solution)/shard_map/late_scores/pallas_call | solution.py:194
  33.4 10.3 %all_to_all.15.value_ref = f32[16,8,128]{2,1,0:T(8,128)S(1)} all-to-all(f32[16,8,128]{2,1,0:T(8,128)S(1)} %get-tuple-element.46), channel_id=1, replica_groups=mesh['grp'=1,'pool'=16,'samp'=2] {'pool'}, dimensions={0} | all-to-all | bytes 131072 | tf_op jit(solution)/shard_map/all_to_all | solution.py:327
  43.7 1.2 %columns.3 = (f32[1,1024]{1,0:T(1,128)S(1)}, f32[8,128]{1,0:T(8,128)}) custom-call(s32[1]{0:T(128)} %bitcast.1.id_ref, f32[16,8,128]{2,1,0:T(8,128)S(1)} %all_to_all.15.value_ref, f32[1,64]{1,0:T(1,128)S(1)} %get-tuple-element.47.norm_ref, f32[768,1024]{1,0:T(8,128)S(1)} %get-tuple-element.48.refs_0_, f32[256,1024]{1,0:T(8,128)S(1)} %get-tuple-element.49.refs_1_), custom_call_target="tpu_custom_call" | custom-call | flops 8388608 | bytes 4268288 | tf_op jit(solution)/shard_map/columns/pallas_call | solution.py:194
  44.9 1.2 %collective-permute-done.13 = f32[1,1024]{1,0:T(1,128)S(1)} collective-permute-done((f32[1,1024]{1,0:T(1,128)S(1)}, f32[1,1024]{1,0:T(1,128)S(1)}, u32[]{:S(2)}, u32[]{:S(2)}) %collective-permute-start.13) | collective-permute-done | bytes 4128 | tf_op jit(solution)/shard_map/ppermute | solution.py:338
  46.1 1.1 %rows.2 = f32[16,8,128]{2,1,0:T(8,128)S(1)} custom-call(s32[1]{0:T(128)} %bitcast.1.id_ref, f32[1,1024]{1,0:T(1,128)S(1)} %add_subtract_fusion.1.shift_ref, f32[768,1024]{1,0:T(8,128)S(1)} %get-tuple-element.48.refs_0_, f32[256,1024]{1,0:T(8,128)S(1)} %get-tuple-element.49.refs_1_), custom_call_target="tpu_custom_call" | custom-call | flops 8388608 | bytes 4263936 | tf_op jit(solution)/shard_map/rows/pallas_call | solution.py:194
  47.3 10.1 %all_to_all.16.value_ref = f32[16,8,128]{2,1,0:T(8,128)S(1)} all-to-all(f32[16,8,128]{2,1,0:T(8,128)S(1)} %rows.2), channel_id=1, replica_groups=mesh['grp'=1,'pool'=16,'samp'=2] {'pool'}, dimensions={0} | all-to-all | bytes 131072 | tf_op jit(solution)/shard_map/all_to_all | solution.py:327
  57.4 1.2 %columns.4 = (f32[1,1024]{1,0:T(1,128)S(1)}, f32[8,128]{1,0:T(8,128)}) custom-call(s32[1]{0:T(128)} %bitcast.1.id_ref, f32[16,8,128]{2,1,0:T(8,128)S(1)} %all_to_all.16.value_ref, f32[1,64]{1,0:T(1,128)S(1)} %get-tuple-element.47.norm_ref, f32[768,1024]{1,0:T(8,128)S(1)} %get-tuple-element.48.refs_0_, f32[256,1024]{1,0:T(8,128)S(1)} %get-tuple-element.49.refs_1_), custom_call_target="tpu_custom_call" | custom-call | flops 8388608 | bytes 4268288 | tf_op jit(solution)/shard_map/columns/pallas_call | solution.py:194
  58.6 1.2 %collective-permute-done.14 = f32[1,1024]{1,0:T(1,128)S(1)} collective-permute-done((f32[1,1024]{1,0:T(1,128)S(1)}, f32[1,1024]{1,0:T(1,128)S(1)}, u32[]{:S(2)}, u32[]{:S(2)}) %collective-permute-start.14) | collective-permute-done | bytes 4128 | tf_op jit(solution)/shard_map/ppermute | solution.py:338
  59.8 1.1 %rows.3 = f32[16,8,128]{2,1,0:T(8,128)S(1)} custom-call(s32[1]{0:T(128)} %bitcast.1.id_ref, f32[1,1024]{1,0:T(1,128)S(1)} %add_subtract_fusion.shift_ref, f32[768,1024]{1,0:T(8,128)S(1)} %get-tuple-element.48.refs_0_, f32[256,1024]{1,0:T(8,128)S(1)} %get-tuple-element.49.refs_1_), custom_call_target="tpu_custom_call" | custom-call | flops 8388608 | bytes 4263936 | tf_op jit(solution)/shard_map/rows/pallas_call | solution.py:194
  60.9 10.1 %all_to_all.17.value_ref = f32[16,8,128]{2,1,0:T(8,128)S(1)} all-to-all(f32[16,8,128]{2,1,0:T(8,128)S(1)} %rows.3), channel_id=1, replica_groups=mesh['grp'=1,'pool'=16,'samp'=2] {'pool'}, dimensions={0} | all-to-all | bytes 131072 | tf_op jit(solution)/shard_map/all_to_all | solution.py:327
  71.1 1.1 %columns.5 = (f32[1,1024]{1,0:T(1,128)S(1)}, f32[8,128]{1,0:T(8,128)S(1)}) custom-call(s32[1]{0:T(128)} %bitcast.1.id_ref, f32[16,8,128]{2,1,0:T(8,128)S(1)} %all_to_all.17.value_ref, f32[1,64]{1,0:T(1,128)S(1)} %get-tuple-element.47.norm_ref, f32[768,1024]{1,0:T(8,128)S(1)} %get-tuple-element.48.refs_0_, f32[256,1024]{1,0:T(8,128)S(1)} %get-tuple-element.49.refs_1_), custom_call_target="tpu_custom_call" | custom-call | flops 8388608 | bytes 4268288 | tf_op jit(solution)/shard_map/columns/pallas_call | solution.py:194
  (31 shorter events, 6.8 us)
Async XLA Ops:
  0.6 13.5 %collective-permute-start = (bf16[64,1024]{1,0:T(8,128)(2,1)}, bf16[64,1024]{1,0:T(8,128)(2,1)S(1)}, u32[]{:S(2)}, u32[]{:S(2)}) collective-permute-start(bf16[64,1024]{1,0:T(8,128)(2,1)} %bitcast.4), channel_id=1, source_target_pairs={{0,24},{1,25},{2,26},{3,27},{4,28},{5,29},{6,30},{7,31},{8,16},{9,... | collective-permute-start | bytes 393224 | tf_op jit(solution)/shard_map/ppermute | solution.py:256
  5.7 8.4 %collective-permute-start.9 = (bf16[64,1024]{1,0:T(8,128)(2,1)}, bf16[64,1024]{1,0:T(8,128)(2,1)S(1)}, u32[]{:S(2)}, u32[]{:S(2)}) collective-permute-start(bf16[64,1024]{1,0:T(8,128)(2,1)} %bitcast.5), channel_id=1, source_target_pairs={{0,8},{1,9},{2,10},{3,11},{4,12},{5,13},{6,14},{7,15},{8,0},{9,1},... | collective-permute-start | bytes 393224 | tf_op jit(solution)/shard_map/ppermute | solution.py:256
  5.7 12.5 %collective-permute-start.3 = (bf16[64,1024]{1,0:T(8,128)(2,1)}, bf16[64,1024]{1,0:T(8,128)(2,1)S(1)}, u32[]{:S(2)}, u32[]{:S(2)}) collective-permute-start(bf16[64,1024]{1,0:T(8,128)(2,1)} %bitcast.6), channel_id=1, source_target_pairs={{0,6},{1,7},{2,4},{3,5},{4,2},{5,3},{6,0},{7,1},{8,14},{9,15},{10,... | collective-permute-start | bytes 393224 | tf_op jit(solution)/shard_map/ppermute | solution.py:256
  8.2 11.6 %collective-permute-start.7 = (bf16[64,1024]{1,0:T(8,128)(2,1)}, bf16[64,1024]{1,0:T(8,128)(2,1)S(1)}, u32[]{:S(2)}, u32[]{:S(2)}) collective-permute-start(bf16[64,1024]{1,0:T(8,128)(2,1)} %bitcast.7), channel_id=1, source_target_pairs={{0,2},{1,5},{2,0},{3,7},{4,6},{5,1},{6,4},{7,3},{8,10},{9,13},{10,... | collective-permute-start | bytes 393224 | tf_op jit(solution)/shard_map/ppermute | solution.py:256
  9.4 1.6 %copy-start = (bf16[1024,1024]{1,0:T(8,128)(2,1)S(1)}, bf16[1024,1024]{1,0:T(8,128)(2,1)}, u32[]{:S(2)}) copy-start(bf16[1024,1024]{1,0:T(8,128)(2,1)} %pool_ref.1) | copy-start | bytes 6291460
  11.0 0.9 %copy-start.1 = (bf16[1,64,1024]{2,1,0:T(8,128)(2,1)S(1)}, bf16[1,64,1024]{2,1,0:T(8,128)(2,1)}, u32[]{:S(2)}) copy-start(bf16[1,64,1024]{2,1,0:T(8,128)(2,1)} %param.4) | copy-start | bytes 393220
  11.9 0.7 copy-start.2
  14.1 13.1 %collective-permute-start.10 = (bf16[128,1024]{1,0:T(8,128)(2,1)S(1)}, bf16[128,1024]{1,0:T(8,128)(2,1)S(1)}, u32[]{:S(2)}, u32[]{:S(2)}) collective-permute-start(bf16[128,1024]{1,0:T(8,128)(2,1)S(1)} %constant_dynamic-update-slice_fusion), channel_id=1, source_target_pairs={{0,2},{1,5},{2,0},{3,7},{4,6},{5,1},{6,4},{7,3},{8,10},{9,13},{10,... | collective-permute-start | bytes 786440 | tf_op jit(solution)/shard_map/ppermute | solution.py:256
  15.7 11.6 %collective-permute-start.11 = (bf16[128,1024]{1,0:T(8,128)(2,1)S(1)}, bf16[128,1024]{1,0:T(8,128)(2,1)S(1)}, u32[]{:S(2)}, u32[]{:S(2)}) collective-permute-start(bf16[128,1024]{1,0:T(8,128)(2,1)S(1)} %constant_dynamic-update-slice_fusion), channel_id=1, source_target_pairs={{0,4},{1,3},{2,6},{3,1},{4,0},{5,7},{6,2},{7,5},{8,12},{9,11},{10,... | collective-permute-start | bytes 786440 | tf_op jit(solution)/shard_map/ppermute | solution.py:256
  16.2 5.0 %collective-permute-start.1 = (bf16[64,1024]{1,0:T(8,128)(2,1)S(1)}, bf16[64,1024]{1,0:T(8,128)(2,1)S(1)}, u32[]{:S(2)}, u32[]{:S(2)}) collective-permute-start(bf16[64,1024]{1,0:T(8,128)(2,1)S(1)} %collective-permute-done.refs_5_), channel_id=1, source_target_pairs={{0,8},{1,9},{2,10},{3,11},{4,12},{5,13},{6,14},{7,15},{8,0},{9,1},... | collective-permute-start | bytes 393224 | tf_op jit(solution)/shard_map/ppermute | solution.py:256
  18.2 5.2 %collective-permute-start.8 = (bf16[64,1024]{1,0:T(8,128)(2,1)S(1)}, bf16[64,1024]{1,0:T(8,128)(2,1)S(1)}, u32[]{:S(2)}, u32[]{:S(2)}) collective-permute-start(bf16[64,1024]{1,0:T(8,128)(2,1)S(1)} %bitcast.9), channel_id=1, source_target_pairs={{0,4},{1,3},{2,6},{3,1},{4,0},{5,7},{6,2},{7,5},{8,12},{9,11},{10,... | collective-permute-start | bytes 393224 | tf_op jit(solution)/shard_map/ppermute | solution.py:256
  19.8 6.8 %collective-permute-start.5 = (bf16[64,1024]{1,0:T(8,128)(2,1)S(1)}, bf16[64,1024]{1,0:T(8,128)(2,1)S(1)}, u32[]{:S(2)}, u32[]{:S(2)}) collective-permute-start(bf16[64,1024]{1,0:T(8,128)(2,1)S(1)} %collective-permute-done.3.refs_3_), channel_id=1, source_target_pairs={{0,24},{1,25},{2,26},{3,27},{4,28},{5,29},{6,30},{7,31},{8,16},{9,... | collective-permute-start | bytes 393224 | tf_op jit(solution)/shard_map/ppermute | solution.py:256
  21.2 6.1 %collective-permute-start.12 = (bf16[64,1024]{1,0:T(8,128)(2,1)S(1)}, bf16[64,1024]{1,0:T(8,128)(2,1)S(1)}, u32[]{:S(2)}, u32[]{:S(2)}) collective-permute-start(bf16[64,1024]{1,0:T(8,128)(2,1)S(1)} %collective-permute-done.1.refs_6_), channel_id=1, source_target_pairs={{0,4},{1,3},{2,6},{3,1},{4,0},{5,7},{6,2},{7,5},{8,12},{9,11},{10,... | collective-permute-start | bytes 393224 | tf_op jit(solution)/shard_map/ppermute | solution.py:256
  23.5 6.3 %collective-permute-start.4 = (bf16[64,1024]{1,0:T(8,128)(2,1)S(1)}, bf16[64,1024]{1,0:T(8,128)(2,1)S(1)}, u32[]{:S(2)}, u32[]{:S(2)}) collective-permute-start(bf16[64,1024]{1,0:T(8,128)(2,1)S(1)} %collective-permute-done.3.refs_3_), channel_id=1, source_target_pairs={{0,8},{1,9},{2,10},{3,11},{4,12},{5,13},{6,14},{7,15},{8,0},{9,1},... | collective-permute-start | bytes 393224 | tf_op jit(solution)/shard_map/ppermute | solution.py:256
  26.5 5.0 %collective-permute-start.2 = (bf16[64,1024]{1,0:T(8,128)(2,1)S(1)}, bf16[64,1024]{1,0:T(8,128)(2,1)S(1)}, u32[]{:S(2)}, u32[]{:S(2)}) collective-permute-start(bf16[64,1024]{1,0:T(8,128)(2,1)S(1)} %collective-permute-done.1.refs_6_), channel_id=1, source_target_pairs={{0,2},{1,5},{2,0},{3,7},{4,6},{5,1},{6,4},{7,3},{8,10},{9,13},{10,... | collective-permute-start | bytes 393224 | tf_op jit(solution)/shard_map/ppermute | solution.py:256
  27.3 5.0 %collective-permute-start.6 = (bf16[64,1024]{1,0:T(8,128)(2,1)S(1)}, bf16[64,1024]{1,0:T(8,128)(2,1)S(1)}, u32[]{:S(2)}, u32[]{:S(2)}) collective-permute-start(bf16[64,1024]{1,0:T(8,128)(2,1)S(1)} %collective-permute-done.5.refs_2_), channel_id=1, source_target_pairs={{0,8},{1,9},{2,10},{3,11},{4,12},{5,13},{6,14},{7,15},{8,0},{9,1},... | collective-permute-start | bytes 393224 | tf_op jit(solution)/shard_map/ppermute | solution.py:256
  44.9 1.2 %collective-permute-start.13 = (f32[1,1024]{1,0:T(1,128)S(1)}, f32[1,1024]{1,0:T(1,128)S(1)}, u32[]{:S(2)}, u32[]{:S(2)}) collective-permute-start(f32[1,1024]{1,0:T(1,128)S(1)} %get-tuple-element.50), channel_id=1, source_target_pairs={{0,1},{1,0},{2,3},{3,2},{4,5},{5,4},{6,7},{7,6},{8,9},{9,8},{10,11... | collective-permute-start | bytes 12296 | tf_op jit(solution)/shard_map/ppermute | solution.py:338
  58.5 1.2 %collective-permute-start.14 = (f32[1,1024]{1,0:T(1,128)S(1)}, f32[1,1024]{1,0:T(1,128)S(1)}, u32[]{:S(2)}, u32[]{:S(2)}) collective-permute-start(f32[1,1024]{1,0:T(1,128)S(1)} %get-tuple-element.51), channel_id=1, source_target_pairs={{0,1},{1,0},{2,3},{3,2},{4,5},{5,4},{6,7},{7,6},{8,9},{9,8},{10,11... | collective-permute-start | bytes 12296 | tf_op jit(solution)/shard_map/ppermute | solution.py:338
  72.2 1.2 %collective-permute-start.15 = (f32[1,1024]{1,0:T(1,128)S(1)}, f32[1,1024]{1,0:T(1,128)S(1)}, u32[]{:S(2)}, u32[]{:S(2)}) collective-permute-start(f32[1,1024]{1,0:T(1,128)S(1)} %get-tuple-element.53), channel_id=1, source_target_pairs={{0,1},{1,0},{2,3},{3,2},{4,5},{5,4},{6,7},{7,6},{8,9},{9,8},{10,11... | collective-permute-start | bytes 12296 | tf_op jit(solution)/shard_map/ppermute | solution.py:338

commit v9 on v8

--- a/solution.py
+++ b/solution.py
@@ -92,15 +92,13 @@
         out_ref[:, line, :] = jnp.broadcast_to(wide, (out_ref.shape[0], LANES))
 
 
-def prepare_kernel(list_hbm, count_hbm, own_ref, pool_ref, *refs):
-    own_out, pool_out, own_norm_ref, pool_norm_ref, mask_ref = refs[:5]
-    list_ref, count_ref, list_sem, count_sem, own_sem, pool_sem = refs[5:]
+def prepare_kernel(list_hbm, count_hbm, pool_ref, *refs):
+    pool_out, pool_norm_ref, mask_ref = refs[:3]
+    list_ref, count_ref, list_sem, count_sem, pool_sem = refs[3:]
     list_copy = pltpu.make_async_copy(list_hbm, list_ref, list_sem)
     count_copy = pltpu.make_async_copy(count_hbm, count_ref, count_sem)
     list_copy.start()
     count_copy.start()
-    own_copy = pltpu.make_async_copy(own_ref, own_out, own_sem)
-    own_copy.start()
     pool_rows = pool_ref.shape[0]
     step = pool_rows // pool_sem.shape[0]
     copies = []
@@ -120,8 +118,6 @@
                 counted += jnp.where(hit & (k < count_ref[0, 0]), 1, 0)
             offset = jnp.where(counted > 0, 0.0, NEG)
             mask_ref[t : t + 1, u * TILE : (u + 1) * TILE] = jnp.full((1, TILE), offset)
-    own_copy.wait()
-    own_norm_ref[...] = row_norms(own_out[...])
     for k, copy in enumerate(copies):
         copy.wait()
         for low in range(k * step, (k + 1) * step, LANES):
@@ -130,7 +126,10 @@
 
 
 def early_kernel(pieces, scale, unit, id_ref, *refs):
-    *piece_refs, pool_ref, norm_ref, mask_ref, score_ref, held_ref, joined = refs
+    *piece_refs, pool_ref, norm_ref, mask_ref = refs[:-4]
+    score_ref, held_ref, own_norm_ref, joined = refs[-4:]
+    own_norm_ref[...] = jnp.zeros_like(own_norm_ref)
+    own_norm_ref[:1, : held_ref.shape[1]] = row_norms(piece_refs[0][...])
     fill_scores(pieces, scale, id_ref, piece_refs, pool_ref, mask_ref, joined, score_ref)
     held_ref[...] = jnp.zeros_like(held_ref)
     row_pass(pieces, id_ref, norm_ref[...] * (-1.0 / unit), score_ref, held_ref)
@@ -164,7 +163,8 @@
         held_ref[source : source + 1, :] = shift[
             line : line + 1, place * own_rows : (place + 1) * own_rows
         ]
-    own = held_ref[pl.ds(owner_of(id_ref, (0, 0)), 1), :] * unit + norm_ref[...]
+    own = held_ref[pl.ds(owner_of(id_ref, (0, 0)), 1), :] * unit
+    own += norm_ref[:1, :own_rows]
     own_ref[...] = jnp.broadcast_to(jnp.concatenate([own] * across, axis=1), own_ref.shape)
     eye = diagonal(own_rows)
     folded = (own_rows // SUBLANES, SUBLANES, pool_rows)
@@ -203,25 +203,22 @@
     )(*scalars, *arrays)
 
 
-def prepare(tile_list, tile_count, own, pool, tiles):
+def prepare(tile_list, tile_count, pool, tiles):
     vmem = pl.BlockSpec(memory_space=pltpu.VMEM)
     chunks = 4
     shapes = [
-        jax.ShapeDtypeStruct(own.shape, own.dtype),
         jax.ShapeDtypeStruct(pool.shape, pool.dtype),
-        jax.ShapeDtypeStruct((1, own.shape[0]), jnp.float32),
         jax.ShapeDtypeStruct((1, pool.shape[0]), jnp.float32),
         jax.ShapeDtypeStruct((tiles, pool.shape[0]), jnp.float32),
     ]
     return pl.pallas_call(
         prepare_kernel,
         out_shape=shapes,
-        in_specs=[pl.BlockSpec(memory_space=pltpu.HBM)] * 4,
+        in_specs=[pl.BlockSpec(memory_space=pltpu.HBM)] * 3,
         out_specs=[vmem] * len(shapes),
         scratch_shapes=[
             pltpu.SMEM(tile_list.shape, jnp.int32),
             pltpu.SMEM(tile_count.shape, jnp.int32),
-            pltpu.SemaphoreType.DMA,
             pltpu.SemaphoreType.DMA,
             pltpu.SemaphoreType.DMA,
             pltpu.SemaphoreType.DMA((chunks,)),
@@ -231,7 +228,7 @@
             flops=2 * pool.size, bytes_accessed=4 * pool.size, transcendentals=0
         ),
         name="prepare",
-    )(tile_list, tile_count, own, pool)
+    )(tile_list, tile_count, pool)
 
 
 def body(samples, pool, tile_list, tile_count):
@@ -264,23 +261,23 @@
     def far(value, mask):
         return swap(value, (mask, mask))
 
-    index = lax.axis_index("pool") * 2 + lax.axis_index("samp") % 2
+    index = lax.axis_index("pool") * 2 | (lax.axis_index("samp") & 1)
     ids = [index.astype(jnp.int32).reshape(1)]
 
     far12, far4 = far(own, 12), far(own, 4)
     a, b = side_a(own), side_b(own)
     corner = swap(own, (3, 3))
     pairs = tile_list.swapaxes(2, 3)
-    local = prepare(pairs, tile_count, own, pool, half_rows // TILE)
+    local = prepare(pairs, tile_count, pool, half_rows // TILE)
     far12, ids[0], *local = lax.optimization_barrier((far12, ids[0], *local))
-    own_copy, pool_copy, own_norm, pool_norm, mask = local
+    pool_copy, pool_norm, mask = local
     far8 = far(far12, 4)
     pair = jnp.concatenate([far4, far12], axis=0)
     a_pair, b_pair = side_a(pair), side_b(pair)
     a8, b8 = side_a(far8), side_b(far8)
     corner12, corner4 = far(corner, 12), far(corner, 4)
     corner8 = far(corner12, 4)
-    early = [own_copy, a, b, corner, far4, far12, far8, a_pair, b_pair, b8]
+    early = [own, a, b, corner, far4, far12, far8, a_pair, b_pair, b8]
     early_pieces = [(0, 0), (1, 0), (2, 0), (3, 0), (0, 4), (0, 12), (0, 8)]
     early_pieces += [(1, 4), (1, 12), (2, 4), (2, 12), (2, 8)]
     late = [a8, corner4, corner12, corner8]
@@ -292,16 +289,16 @@
         step *= 2
 
     count = len(early_pieces) * own_rows
-    score0, held = call(
+    score0, held, own_norm = call(
         functools.partial(early_kernel, early_pieces, scale, unit),
-        [(count, pool_rows), (size, own_rows)],
+        [(count, pool_rows), (size, own_rows), (SUBLANES, LANES)],
         [pltpu.VMEM((count, width), samples.dtype)],
         ids,
         early + [pool_copy, pool_norm, mask],
         2 * count * pool_rows * width,
         "early_scores",
     )
-    *late, score0, held = lax.optimization_barrier((*late, score0, held))
+    *late, score0, held, own_norm = lax.optimization_barrier((*late, score0, held, own_norm))
     count = len(late_pieces) * own_rows
     score1, value = call(
         functools.partial(late_kernel, late_pieces, scale, unit),

time: 74.4 us -> 73.6 us (0.989)
  local copies, waits for them, and re-layouts: 3.7 us -> 2.8 us
    unnamed x7, local copies, waits for them, and re-layouts: 3.18 us -> 2.28 us
where the time goes in v9:
time: 73.6 us; the launch traced here: 73.4 us
  blocking collectives  30.8 us (42%)
  starting transfers between devices  18.4 us (25%)
  Pallas kernels  10.8 us (15%)
  waiting for transfers between devices  8.38 us (11%)
  local copies, waits for them, and re-layouts  2.8 us (4%)
  between operations  1.43 us (2%)
    all_to_all x3, blocking collectives, body(): value = lax.all_to_all(value, 'pool', 0, 0, tiled=True)  30.8 us
    ppermute x13, starting transfers between devices, swap(): return lax.ppermute(value, ('pool', 'samp'), pairs)  18.2 us
    pallas_call x7, Pallas kernels, call(): pl.pallas_call(kernel, out_shape=[jax.ShapeDtypeStruct(s, jnp.float32) fo...  9.43 us
    ppermute x13, waiting for transfers between devices, swap(): return lax.ppermute(value, ('pool', 'samp'), pairs)  5.44 us
    ppermute x3, waiting for transfers between devices, body(): shift = log_b - log2_sum([value, lax.ppermute(value, 'samp', pairs)])  2.94 us
    unnamed x7, local copies, waits for them, and re-layouts  2.28 us
  transfers between devices with their start and end apart: 16, of which 9 were waited for; matrix products, arithmetic and copies ran while one was open for 1% of the time, Pallas kernels for 5%

profile of v9, /device:TPU:0, one launch (start us, length us, event | category | flops | bytes accessed | tf_op | source)
XLA Modules:
  0.0 73.4 jit_solution(16318955874214979874)
XLA Ops:
  0.6 5.1 %collective-permute-start = (bf16[64,1024]{1,0:T(8,128)(2,1)}, bf16[64,1024]{1,0:T(8,128)(2,1)S(1)}, u32[]{:S(2)}, u32[]{:S(2)}) collective-permute-start(bf16[64,1024]{1,0:T(8,128)(2,1)} %bitcast.5), channel_id=1, source_target_pairs={{0,24},{1,25},{2,26},{3,27},{4,28},{5,29},{6,30},{7,31},{8,16},{9,... | collective-permute-start | bytes 393224 | tf_op jit(solution)/shard_map/ppermute | solution.py:253
  5.7 2.4 %collective-permute-start.3 = (bf16[64,1024]{1,0:T(8,128)(2,1)}, bf16[64,1024]{1,0:T(8,128)(2,1)S(1)}, u32[]{:S(2)}, u32[]{:S(2)}) collective-permute-start(bf16[64,1024]{1,0:T(8,128)(2,1)} %bitcast.7), channel_id=1, source_target_pairs={{0,6},{1,7},{2,4},{3,5},{4,2},{5,3},{6,0},{7,1},{8,14},{9,15},{10,... | collective-permute-start | bytes 393224 | tf_op jit(solution)/shard_map/ppermute | solution.py:253
  9.4 1.6 %copy-done = bf16[1024,1024]{1,0:T(8,128)(2,1)S(1)} copy-done((bf16[1024,1024]{1,0:T(8,128)(2,1)S(1)}, bf16[1024,1024]{1,0:T(8,128)(2,1)}, u32[]{:S(2)}) %copy-start) | copy-done | bytes 2097176
  11.7 1.4 %prepare.1 = (bf16[1024,1024]{1,0:T(8,128)(2,1)S(1)}, f32[1,1024]{1,0:T(1,128)S(1)}, f32[2,1024]{1,0:T(2,128)S(1)}) custom-call(s32[1,1,2,4]{3,2,1,0:T(2,128)S(1)} %bitcast.4, s32[1,1]{1,0:T(1,128)S(6)} %copy.7.count_hbm, bf16[1024,1024]{1,0:T(8,128)(2,1)S(1)} %copy-done), custom_call_target="tpu_custom_call" | custom-call | flops 2097152 | bytes 4194304 | tf_op jit(solution)/shard_map/prepare/pallas_call | solution.py:214
  13.1 1.6 %collective-permute-start.10 = (bf16[128,1024]{1,0:T(8,128)(2,1)S(1)}, bf16[128,1024]{1,0:T(8,128)(2,1)S(1)}, u32[]{:S(2)}, u32[]{:S(2)}) collective-permute-start(bf16[128,1024]{1,0:T(8,128)(2,1)S(1)} %constant_dynamic-update-slice_fusion), channel_id=1, source_target_pairs={{0,2},{1,5},{2,0},{3,7},{4,6},{5,1},{6,4},{7,3},{8,10},{9,13},{10,... | collective-permute-start | bytes 786440 | tf_op jit(solution)/shard_map/ppermute | solution.py:253
  15.5 1.7 %collective-permute-start.1 = (bf16[64,1024]{1,0:T(8,128)(2,1)S(1)}, bf16[64,1024]{1,0:T(8,128)(2,1)S(1)}, u32[]{:S(2)}, u32[]{:S(2)}) collective-permute-start(bf16[64,1024]{1,0:T(8,128)(2,1)S(1)} %collective-permute-done.refs_5_), channel_id=1, source_target_pairs={{0,8},{1,9},{2,10},{3,11},{4,12},{5,13},{6,14},{7,15},{8,0},{9,1},... | collective-permute-start | bytes 393224 | tf_op jit(solution)/shard_map/ppermute | solution.py:253
  17.2 1.5 %collective-permute-start.8 = (bf16[64,1024]{1,0:T(8,128)(2,1)S(1)}, bf16[64,1024]{1,0:T(8,128)(2,1)S(1)}, u32[]{:S(2)}, u32[]{:S(2)}) collective-permute-start(bf16[64,1024]{1,0:T(8,128)(2,1)S(1)} %bitcast.9), channel_id=1, source_target_pairs={{0,4},{1,3},{2,6},{3,1},{4,0},{5,7},{6,2},{7,5},{8,12},{9,11},{10,... | collective-permute-start | bytes 393224 | tf_op jit(solution)/shard_map/ppermute | solution.py:253
  18.9 1.5 %collective-permute-done.1.refs_6_ = bf16[64,1024]{1,0:T(8,128)(2,1)S(1)} collective-permute-done((bf16[64,1024]{1,0:T(8,128)(2,1)S(1)}, bf16[64,1024]{1,0:T(8,128)(2,1)S(1)}, u32[]{:S(2)}, u32[]{:S(2)}) %collective-permute-start.1) | collective-permute-done | bytes 131104 | tf_op jit(solution)/shard_map/ppermute | solution.py:253
  20.4 1.7 %collective-permute-start.12 = (bf16[64,1024]{1,0:T(8,128)(2,1)S(1)}, bf16[64,1024]{1,0:T(8,128)(2,1)S(1)}, u32[]{:S(2)}, u32[]{:S(2)}) collective-permute-start(bf16[64,1024]{1,0:T(8,128)(2,1)S(1)} %collective-permute-done.1.refs_6_), channel_id=1, source_target_pairs={{0,4},{1,3},{2,6},{3,1},{4,0},{5,7},{6,2},{7,5},{8,12},{9,11},{10,... | collective-permute-start | bytes 393224 | tf_op jit(solution)/shard_map/ppermute | solution.py:253
  22.4 2.0 %collective-permute-start.4 = (bf16[64,1024]{1,0:T(8,128)(2,1)S(1)}, bf16[64,1024]{1,0:T(8,128)(2,1)S(1)}, u32[]{:S(2)}, u32[]{:S(2)}) collective-permute-start(bf16[64,1024]{1,0:T(8,128)(2,1)S(1)} %collective-permute-done.3.refs_3_), channel_id=1, source_target_pairs={{0,8},{1,9},{2,10},{3,11},{4,12},{5,13},{6,14},{7,15},{8,0},{9,1},... | collective-permute-start | bytes 393224 | tf_op jit(solution)/shard_map/ppermute | solution.py:253
  24.5 1.0 %collective-permute-done.5.refs_2_ = bf16[64,1024]{1,0:T(8,128)(2,1)S(1)} collective-permute-done((bf16[64,1024]{1,0:T(8,128)(2,1)S(1)}, bf16[64,1024]{1,0:T(8,128)(2,1)S(1)}, u32[]{:S(2)}, u32[]{:S(2)}) %collective-permute-start.5) | collective-permute-done | bytes 131104 | tf_op jit(solution)/shard_map/ppermute | solution.py:253
  26.0 2.5 %early_scores.1 = (f32[768,1024]{1,0:T(8,128)S(1)}, f32[16,64]{1,0:T(8,128)S(1)}, f32[8,128]{1,0:T(8,128)S(1)}) custom-call(s32[1]{0:T(128)} %bitcast.1.id_ref, bf16[64,1024]{1,0:T(8,128)(2,1)S(1)} %bitcast.10, bf16[64,1024]{1,0:T(8,128)(2,1)S(1)} %collective-permute-done.7.refs_1_, bf16[64,1024]{1,0:T(8,128)(2,1)S(1)} %collective-permute-done.8.refs_2_, ...), custom_call_target="tpu_custom_call" | custom-call | flops 1610612736 | bytes 6836224 | tf_op jit(solution)/shard_map/early_scores/pallas_call | solution.py:194
  28.8 1.7 %collective-permute-done.2.refs_0_ = bf16[64,1024]{1,0:T(8,128)(2,1)S(1)} collective-permute-done((bf16[64,1024]{1,0:T(8,128)(2,1)S(1)}, bf16[64,1024]{1,0:T(8,128)(2,1)S(1)}, u32[]{:S(2)}, u32[]{:S(2)}) %collective-permute-start.2) | collective-permute-done | bytes 131104 | tf_op jit(solution)/shard_map/ppermute | solution.py:253
  31.1 1.1 %late_scores.1 = (f32[256,1024]{1,0:T(8,128)S(1)}, f32[16,8,128]{2,1,0:T(8,128)S(1)}) custom-call(s32[1]{0:T(128)} %bitcast.1.id_ref, bf16[64,1024]{1,0:T(8,128)(2,1)S(1)} %collective-permute-done.2.refs_0_, bf16[64,1024]{1,0:T(8,128)(2,1)S(1)} %collective-permute-done.4.refs_1_, bf16[64,1024]{1,0:T(8,128)(2,1)S(1)} %collective-permute-done.5.refs_2_, ...), custom_call_target="tpu_custom_call" | custom-call | flops 536870912 | bytes 3751936 | tf_op jit(solution)/shard_map/late_scores/pallas_call | solution.py:194
  32.2 10.6 %all_to_all.15.value_ref = f32[16,8,128]{2,1,0:T(8,128)S(1)} all-to-all(f32[16,8,128]{2,1,0:T(8,128)S(1)} %get-tuple-element.42), channel_id=1, replica_groups=mesh['grp'=1,'pool'=16,'samp'=2] {'pool'}, dimensions={0} | all-to-all | bytes 131072 | tf_op jit(solution)/shard_map/all_to_all | solution.py:324
  42.8 1.2 %columns.3 = (f32[1,1024]{1,0:T(1,128)S(1)}, f32[8,128]{1,0:T(8,128)}) custom-call(s32[1]{0:T(128)} %bitcast.1.id_ref, f32[16,8,128]{2,1,0:T(8,128)S(1)} %all_to_all.15.value_ref, f32[8,128]{1,0:T(8,128)S(1)} %get-tuple-element.43.norm_ref, f32[768,1024]{1,0:T(8,128)S(1)} %get-tuple-element.44.refs_0_, f32[256,1024]{1,0:T(8,128)S(1)} %get-tuple-element.45.refs_1_), custom_call_target="tpu_custom_call" | custom-call | flops 8388608 | bytes 4272128 | tf_op jit(solution)/shard_map/columns/pallas_call | solution.py:194
  44.1 1.2 %collective-permute-done.13 = f32[1,1024]{1,0:T(1,128)S(1)} collective-permute-done((f32[1,1024]{1,0:T(1,128)S(1)}, f32[1,1024]{1,0:T(1,128)S(1)}, u32[]{:S(2)}, u32[]{:S(2)}) %collective-permute-start.13) | collective-permute-done | bytes 4128 | tf_op jit(solution)/shard_map/ppermute | solution.py:335
  45.3 1.1 %rows.2 = f32[16,8,128]{2,1,0:T(8,128)S(1)} custom-call(s32[1]{0:T(128)} %bitcast.1.id_ref, f32[1,1024]{1,0:T(1,128)S(1)} %add_subtract_fusion.1.shift_ref, f32[768,1024]{1,0:T(8,128)S(1)} %get-tuple-element.44.refs_0_, f32[256,1024]{1,0:T(8,128)S(1)} %get-tuple-element.45.refs_1_), custom_call_target="tpu_custom_call" | custom-call | flops 8388608 | bytes 4263936 | tf_op jit(solution)/shard_map/rows/pallas_call | solution.py:194
  46.4 10.1 %all_to_all.16.value_ref = f32[16,8,128]{2,1,0:T(8,128)S(1)} all-to-all(f32[16,8,128]{2,1,0:T(8,128)S(1)} %rows.2), channel_id=1, replica_groups=mesh['grp'=1,'pool'=16,'samp'=2] {'pool'}, dimensions={0} | all-to-all | bytes 131072 | tf_op jit(solution)/shard_map/all_to_all | solution.py:324
  56.6 1.2 %columns.4 = (f32[1,1024]{1,0:T(1,128)S(1)}, f32[8,128]{1,0:T(8,128)}) custom-call(s32[1]{0:T(128)} %bitcast.1.id_ref, f32[16,8,128]{2,1,0:T(8,128)S(1)} %all_to_all.16.value_ref, f32[8,128]{1,0:T(8,128)S(1)} %get-tuple-element.43.norm_ref, f32[768,1024]{1,0:T(8,128)S(1)} %get-tuple-element.44.refs_0_, f32[256,1024]{1,0:T(8,128)S(1)} %get-tuple-element.45.refs_1_), custom_call_target="tpu_custom_call" | custom-call | flops 8388608 | bytes 4272128 | tf_op jit(solution)/shard_map/columns/pallas_call | solution.py:194
  57.9 1.2 %collective-permute-done.14 = f32[1,1024]{1,0:T(1,128)S(1)} collective-permute-done((f32[1,1024]{1,0:T(1,128)S(1)}, f32[1,1024]{1,0:T(1,128)S(1)}, u32[]{:S(2)}, u32[]{:S(2)}) %collective-permute-start.14) | collective-permute-done | bytes 4128 | tf_op jit(solution)/shard_map/ppermute | solution.py:335
  59.0 1.1 %rows.3 = f32[16,8,128]{2,1,0:T(8,128)S(1)} custom-call(s32[1]{0:T(128)} %bitcast.1.id_ref, f32[1,1024]{1,0:T(1,128)S(1)} %add_subtract_fusion.shift_ref, f32[768,1024]{1,0:T(8,128)S(1)} %get-tuple-element.44.refs_0_, f32[256,1024]{1,0:T(8,128)S(1)} %get-tuple-element.45.refs_1_), custom_call_target="tpu_custom_call" | custom-call | flops 8388608 | bytes 4263936 | tf_op jit(solution)/shard_map/rows/pallas_call | solution.py:194
  60.2 10.1 %all_to_all.17.value_ref = f32[16,8,128]{2,1,0:T(8,128)S(1)} all-to-all(f32[16,8,128]{2,1,0:T(8,128)S(1)} %rows.3), channel_id=1, replica_groups=mesh['grp'=1,'pool'=16,'samp'=2] {'pool'}, dimensions={0} | all-to-all | bytes 131072 | tf_op jit(solution)/shard_map/all_to_all | solution.py:324
  70.3 1.2 %columns.5 = (f32[1,1024]{1,0:T(1,128)S(1)}, f32[8,128]{1,0:T(8,128)S(1)}) custom-call(s32[1]{0:T(128)} %bitcast.1.id_ref, f32[16,8,128]{2,1,0:T(8,128)S(1)} %all_to_all.17.value_ref, f32[8,128]{1,0:T(8,128)S(1)} %get-tuple-element.43.norm_ref, f32[768,1024]{1,0:T(8,128)S(1)} %get-tuple-element.44.refs_0_, f32[256,1024]{1,0:T(8,128)S(1)} %get-tuple-element.45.refs_1_), custom_call_target="tpu_custom_call" | custom-call | flops 8388608 | bytes 4272128 | tf_op jit(solution)/shard_map/columns/pallas_call | solution.py:194
  (31 shorter events, 6.1 us)
Async XLA Ops:
  0.6 12.4 %collective-permute-start = (bf16[64,1024]{1,0:T(8,128)(2,1)}, bf16[64,1024]{1,0:T(8,128)(2,1)S(1)}, u32[]{:S(2)}, u32[]{:S(2)}) collective-permute-start(bf16[64,1024]{1,0:T(8,128)(2,1)} %bitcast.5), channel_id=1, source_target_pairs={{0,24},{1,25},{2,26},{3,27},{4,28},{5,29},{6,30},{7,31},{8,16},{9,... | collective-permute-start | bytes 393224 | tf_op jit(solution)/shard_map/ppermute | solution.py:253
  5.7 7.3 %collective-permute-start.9 = (bf16[64,1024]{1,0:T(8,128)(2,1)}, bf16[64,1024]{1,0:T(8,128)(2,1)S(1)}, u32[]{:S(2)}, u32[]{:S(2)}) collective-permute-start(bf16[64,1024]{1,0:T(8,128)(2,1)} %bitcast.6), channel_id=1, source_target_pairs={{0,8},{1,9},{2,10},{3,11},{4,12},{5,13},{6,14},{7,15},{8,0},{9,1},... | collective-permute-start | bytes 393224 | tf_op jit(solution)/shard_map/ppermute | solution.py:253
  5.7 11.4 %collective-permute-start.3 = (bf16[64,1024]{1,0:T(8,128)(2,1)}, bf16[64,1024]{1,0:T(8,128)(2,1)S(1)}, u32[]{:S(2)}, u32[]{:S(2)}) collective-permute-start(bf16[64,1024]{1,0:T(8,128)(2,1)} %bitcast.7), channel_id=1, source_target_pairs={{0,6},{1,7},{2,4},{3,5},{4,2},{5,3},{6,0},{7,1},{8,14},{9,15},{10,... | collective-permute-start | bytes 393224 | tf_op jit(solution)/shard_map/ppermute | solution.py:253
  8.2 10.5 %collective-permute-start.7 = (bf16[64,1024]{1,0:T(8,128)(2,1)}, bf16[64,1024]{1,0:T(8,128)(2,1)S(1)}, u32[]{:S(2)}, u32[]{:S(2)}) collective-permute-start(bf16[64,1024]{1,0:T(8,128)(2,1)} %bitcast.8), channel_id=1, source_target_pairs={{0,2},{1,5},{2,0},{3,7},{4,6},{5,1},{6,4},{7,3},{8,10},{9,13},{10,... | collective-permute-start | bytes 393224 | tf_op jit(solution)/shard_map/ppermute | solution.py:253
  9.4 1.6 %copy-start = (bf16[1024,1024]{1,0:T(8,128)(2,1)S(1)}, bf16[1024,1024]{1,0:T(8,128)(2,1)}, u32[]{:S(2)}) copy-start(bf16[1024,1024]{1,0:T(8,128)(2,1)} %pool_ref.1) | copy-start | bytes 6291460
  11.0 0.7 copy-start.1
  11.7 5.5 %copy-start.2 = (bf16[1,64,1024]{2,1,0:T(8,128)(2,1)S(1)}, bf16[1,64,1024]{2,1,0:T(8,128)(2,1)}, u32[]{:S(2)}) copy-start(bf16[1,64,1024]{2,1,0:T(8,128)(2,1)} %param.4) | copy-start | bytes 393220
  13.1 12.9 %collective-permute-start.10 = (bf16[128,1024]{1,0:T(8,128)(2,1)S(1)}, bf16[128,1024]{1,0:T(8,128)(2,1)S(1)}, u32[]{:S(2)}, u32[]{:S(2)}) collective-permute-start(bf16[128,1024]{1,0:T(8,128)(2,1)S(1)} %constant_dynamic-update-slice_fusion), channel_id=1, source_target_pairs={{0,2},{1,5},{2,0},{3,7},{4,6},{5,1},{6,4},{7,3},{8,10},{9,13},{10,... | collective-permute-start | bytes 786440 | tf_op jit(solution)/shard_map/ppermute | solution.py:253
  14.7 11.4 %collective-permute-start.11 = (bf16[128,1024]{1,0:T(8,128)(2,1)S(1)}, bf16[128,1024]{1,0:T(8,128)(2,1)S(1)}, u32[]{:S(2)}, u32[]{:S(2)}) collective-permute-start(bf16[128,1024]{1,0:T(8,128)(2,1)S(1)} %constant_dynamic-update-slice_fusion), channel_id=1, source_target_pairs={{0,4},{1,3},{2,6},{3,1},{4,0},{5,7},{6,2},{7,5},{8,12},{9,11},{10,... | collective-permute-start | bytes 786440 | tf_op jit(solution)/shard_map/ppermute | solution.py:253
  15.5 5.0 %collective-permute-start.1 = (bf16[64,1024]{1,0:T(8,128)(2,1)S(1)}, bf16[64,1024]{1,0:T(8,128)(2,1)S(1)}, u32[]{:S(2)}, u32[]{:S(2)}) collective-permute-start(bf16[64,1024]{1,0:T(8,128)(2,1)S(1)} %collective-permute-done.refs_5_), channel_id=1, source_target_pairs={{0,8},{1,9},{2,10},{3,11},{4,12},{5,13},{6,14},{7,15},{8,0},{9,1},... | collective-permute-start | bytes 393224 | tf_op jit(solution)/shard_map/ppermute | solution.py:253
  17.2 5.2 %collective-permute-start.8 = (bf16[64,1024]{1,0:T(8,128)(2,1)S(1)}, bf16[64,1024]{1,0:T(8,128)(2,1)S(1)}, u32[]{:S(2)}, u32[]{:S(2)}) collective-permute-start(bf16[64,1024]{1,0:T(8,128)(2,1)S(1)} %bitcast.9), channel_id=1, source_target_pairs={{0,4},{1,3},{2,6},{3,1},{4,0},{5,7},{6,2},{7,5},{8,12},{9,11},{10,... | collective-permute-start | bytes 393224 | tf_op jit(solution)/shard_map/ppermute | solution.py:253
  18.7 6.8 %collective-permute-start.5 = (bf16[64,1024]{1,0:T(8,128)(2,1)S(1)}, bf16[64,1024]{1,0:T(8,128)(2,1)S(1)}, u32[]{:S(2)}, u32[]{:S(2)}) collective-permute-start(bf16[64,1024]{1,0:T(8,128)(2,1)S(1)} %collective-permute-done.3.refs_3_), channel_id=1, source_target_pairs={{0,24},{1,25},{2,26},{3,27},{4,28},{5,29},{6,30},{7,31},{8,16},{9,... | collective-permute-start | bytes 393224 | tf_op jit(solution)/shard_map/ppermute | solution.py:253
  20.4 5.6 %collective-permute-start.12 = (bf16[64,1024]{1,0:T(8,128)(2,1)S(1)}, bf16[64,1024]{1,0:T(8,128)(2,1)S(1)}, u32[]{:S(2)}, u32[]{:S(2)}) collective-permute-start(bf16[64,1024]{1,0:T(8,128)(2,1)S(1)} %collective-permute-done.1.refs_6_), channel_id=1, source_target_pairs={{0,4},{1,3},{2,6},{3,1},{4,0},{5,7},{6,2},{7,5},{8,12},{9,11},{10,... | collective-permute-start | bytes 393224 | tf_op jit(solution)/shard_map/ppermute | solution.py:253
  22.4 6.3 %collective-permute-start.4 = (bf16[64,1024]{1,0:T(8,128)(2,1)S(1)}, bf16[64,1024]{1,0:T(8,128)(2,1)S(1)}, u32[]{:S(2)}, u32[]{:S(2)}) collective-permute-start(bf16[64,1024]{1,0:T(8,128)(2,1)S(1)} %collective-permute-done.3.refs_3_), channel_id=1, source_target_pairs={{0,8},{1,9},{2,10},{3,11},{4,12},{5,13},{6,14},{7,15},{8,0},{9,1},... | collective-permute-start | bytes 393224 | tf_op jit(solution)/shard_map/ppermute | solution.py:253
  25.5 5.0 %collective-permute-start.2 = (bf16[64,1024]{1,0:T(8,128)(2,1)S(1)}, bf16[64,1024]{1,0:T(8,128)(2,1)S(1)}, u32[]{:S(2)}, u32[]{:S(2)}) collective-permute-start(bf16[64,1024]{1,0:T(8,128)(2,1)S(1)} %collective-permute-done.1.refs_6_), channel_id=1, source_target_pairs={{0,2},{1,5},{2,0},{3,7},{4,6},{5,1},{6,4},{7,3},{8,10},{9,13},{10,... | collective-permute-start | bytes 393224 | tf_op jit(solution)/shard_map/ppermute | solution.py:253
  26.0 5.1 %collective-permute-start.6 = (bf16[64,1024]{1,0:T(8,128)(2,1)S(1)}, bf16[64,1024]{1,0:T(8,128)(2,1)S(1)}, u32[]{:S(2)}, u32[]{:S(2)}) collective-permute-start(bf16[64,1024]{1,0:T(8,128)(2,1)S(1)} %collective-permute-done.5.refs_2_), channel_id=1, source_target_pairs={{0,8},{1,9},{2,10},{3,11},{4,12},{5,13},{6,14},{7,15},{8,0},{9,1},... | collective-permute-start | bytes 393224 | tf_op jit(solution)/shard_map/ppermute | solution.py:253
  44.0 1.2 %collective-permute-start.13 = (f32[1,1024]{1,0:T(1,128)S(1)}, f32[1,1024]{1,0:T(1,128)S(1)}, u32[]{:S(2)}, u32[]{:S(2)}) collective-permute-start(f32[1,1024]{1,0:T(1,128)S(1)} %get-tuple-element.46), channel_id=1, source_target_pairs={{0,1},{1,0},{2,3},{3,2},{4,5},{5,4},{6,7},{7,6},{8,9},{9,8},{10,11... | collective-permute-start | bytes 12296 | tf_op jit(solution)/shard_map/ppermute | solution.py:335
  57.8 1.2 %collective-permute-start.14 = (f32[1,1024]{1,0:T(1,128)S(1)}, f32[1,1024]{1,0:T(1,128)S(1)}, u32[]{:S(2)}, u32[]{:S(2)}) collective-permute-start(f32[1,1024]{1,0:T(1,128)S(1)} %get-tuple-element.47), channel_id=1, source_target_pairs={{0,1},{1,0},{2,3},{3,2},{4,5},{5,4},{6,7},{7,6},{8,9},{9,8},{10,11... | collective-permute-start | bytes 12296 | tf_op jit(solution)/shard_map/ppermute | solution.py:335
  71.5 1.2 %collective-permute-start.15 = (f32[1,1024]{1,0:T(1,128)S(1)}, f32[1,1024]{1,0:T(1,128)S(1)}, u32[]{:S(2)}, u32[]{:S(2)}) collective-permute-start(f32[1,1024]{1,0:T(1,128)S(1)} %get-tuple-element.49), channel_id=1, source_target_pairs={{0,1},{1,0},{2,3},{3,2},{4,5},{5,4},{6,7},{7,6},{8,9},{9,8},{10,11... | collective-permute-start | bytes 12296 | tf_op jit(solution)/shard_map/ppermute | solution.py:335

commit v10 on v9

--- a/solution.py
+++ b/solution.py
@@ -180,11 +180,13 @@
         columns.append(jnp.sum(jnp.where(eye, row, 0.0), axis=1, keepdims=True))
         high = jnp.max((ref[rows, :] + columns[k]).reshape(folded), axis=0)
         peak = high if peak is None else jnp.maximum(peak, high)
-    peak = jnp.max(peak, axis=0, keepdims=True)
     total = jnp.zeros((SUBLANES, pool_rows), jnp.float32)
     for k, (ref, rows, _) in enumerate(blocks):
-        total += jnp.sum(jnp.exp2(ref[rows, :] + (columns[k] - peak)).reshape(folded), axis=0)
-    out_ref[...] = peak + log2(jnp.sum(total, axis=0, keepdims=True))
+        block = (ref[rows, :] + columns[k]).reshape(folded)
+        total += jnp.sum(jnp.exp2(block - peak), axis=0)
+    top = jnp.max(peak, axis=0, keepdims=True)
+    total = jnp.sum(total * jnp.exp2(peak - top), axis=0, keepdims=True)
+    out_ref[...] = top + log2(total)
 
 
 def call(kernel, shapes, scratch, scalars, arrays, flops, name):
@@ -269,9 +271,10 @@
     corner = swap(own, (3, 3))
     pairs = tile_list.swapaxes(2, 3)
     local = prepare(pairs, tile_count, pool, half_rows // TILE)
-    far12, ids[0], *local = lax.optimization_barrier((far12, ids[0], *local))
+    far12, far4, ids[0], *local = lax.optimization_barrier((far12, far4, ids[0], *local))
     pool_copy, pool_norm, mask = local
     far8 = far(far12, 4)
+    far4, corner = lax.optimization_barrier((far4, corner))
     pair = jnp.concatenate([far4, far12], axis=0)
     a_pair, b_pair = side_a(pair), side_b(pair)
     a8, b8 = side_a(far8), side_b(far8)

time: 73.6 us -> 73.5 us (level)
  transfers between devices with their start and end apart: 16 -> 16, of which waited for: 9 -> 8; matrix products, arithmetic and copies ran while one was open for 1% -> 1% of each run, Pallas kernels for 5% -> 5%
where the time goes in v10:
time: 73.5 us; the launch traced here: 73.2 us
  blocking collectives  30.8 us (42%)
  starting transfers between devices  18.4 us (25%)
  Pallas kernels  10.6 us (14%)
  waiting for transfers between devices  8.37 us (11%)
  local copies, waits for them, and re-layouts  2.8 us (4%)
  between operations  1.44 us (2%)
    all_to_all x3, blocking collectives, body(): value = lax.all_to_all(value, 'pool', 0, 0, tiled=True)  30.8 us
    ppermute x13, starting transfers between devices, swap(): return lax.ppermute(value, ('pool', 'samp'), pairs)  18.2 us
    pallas_call x7, Pallas kernels, call(): pl.pallas_call(kernel, out_shape=[jax.ShapeDtypeStruct(s, jnp.float32) fo...  9.24 us
    ppermute x13, waiting for transfers between devices, swap(): return lax.ppermute(value, ('pool', 'samp'), pairs)  5.43 us
    ppermute x3, waiting for transfers between devices, body(): shift = log_b - log2_sum([value, lax.ppermute(value, 'samp', pairs)])  2.94 us
    unnamed x7, local copies, waits for them, and re-layouts  2.28 us
  transfers between devices with their start and end apart: 16, of which 8 were waited for; matrix products, arithmetic and copies ran while one was open for 1% of the time, Pallas kernels for 5%

profile of v10, /device:TPU:0, one launch (start us, length us, event | category | flops | bytes accessed | tf_op | source)
XLA Modules:
  0.0 73.2 jit_solution(1335953948348082617)
XLA Ops:
  0.6 5.1 %collective-permute-start = (bf16[64,1024]{1,0:T(8,128)(2,1)}, bf16[64,1024]{1,0:T(8,128)(2,1)S(1)}, u32[]{:S(2)}, u32[]{:S(2)}) collective-permute-start(bf16[64,1024]{1,0:T(8,128)(2,1)} %bitcast.5), channel_id=1, source_target_pairs={{0,24},{1,25},{2,26},{3,27},{4,28},{5,29},{6,30},{7,31},{8,16},{9,... | collective-permute-start | bytes 393224 | tf_op jit(solution)/shard_map/ppermute | solution.py:255
  5.7 2.4 %collective-permute-start.4 = (bf16[64,1024]{1,0:T(8,128)(2,1)}, bf16[64,1024]{1,0:T(8,128)(2,1)S(1)}, u32[]{:S(2)}, u32[]{:S(2)}) collective-permute-start(bf16[64,1024]{1,0:T(8,128)(2,1)} %bitcast.7), channel_id=1, source_target_pairs={{0,6},{1,7},{2,4},{3,5},{4,2},{5,3},{6,0},{7,1},{8,14},{9,15},{10,... | collective-permute-start | bytes 393224 | tf_op jit(solution)/shard_map/ppermute | solution.py:255
  9.4 1.6 %copy-done = bf16[1024,1024]{1,0:T(8,128)(2,1)S(1)} copy-done((bf16[1024,1024]{1,0:T(8,128)(2,1)S(1)}, bf16[1024,1024]{1,0:T(8,128)(2,1)}, u32[]{:S(2)}) %copy-start) | copy-done | bytes 2097176
  11.7 1.4 %prepare.1 = (bf16[1024,1024]{1,0:T(8,128)(2,1)S(1)}, f32[1,1024]{1,0:T(1,128)S(1)}, f32[2,1024]{1,0:T(2,128)S(1)}) custom-call(s32[1,1,2,4]{3,2,1,0:T(2,128)S(1)} %bitcast.4, s32[1,1]{1,0:T(1,128)S(6)} %copy.7.count_hbm, bf16[1024,1024]{1,0:T(8,128)(2,1)S(1)} %copy-done), custom_call_target="tpu_custom_call" | custom-call | flops 2097152 | bytes 4194304 | tf_op jit(solution)/shard_map/prepare/pallas_call | solution.py:216
  13.1 1.6 %collective-permute-start.10 = (bf16[128,1024]{1,0:T(8,128)(2,1)S(1)}, bf16[128,1024]{1,0:T(8,128)(2,1)S(1)}, u32[]{:S(2)}, u32[]{:S(2)}) collective-permute-start(bf16[128,1024]{1,0:T(8,128)(2,1)S(1)} %constant_dynamic-update-slice_fusion), channel_id=1, source_target_pairs={{0,2},{1,5},{2,0},{3,7},{4,6},{5,1},{6,4},{7,3},{8,10},{9,13},{10,... | collective-permute-start | bytes 786440 | tf_op jit(solution)/shard_map/ppermute | solution.py:255
  15.5 1.7 %collective-permute-start.2 = (bf16[64,1024]{1,0:T(8,128)(2,1)S(1)}, bf16[64,1024]{1,0:T(8,128)(2,1)S(1)}, u32[]{:S(2)}, u32[]{:S(2)}) collective-permute-start(bf16[64,1024]{1,0:T(8,128)(2,1)S(1)} %collective-permute-done.refs_5_), channel_id=1, source_target_pairs={{0,8},{1,9},{2,10},{3,11},{4,12},{5,13},{6,14},{7,15},{8,0},{9,1},... | collective-permute-start | bytes 393224 | tf_op jit(solution)/shard_map/ppermute | solution.py:255
  17.2 1.5 %collective-permute-start.9 = (bf16[64,1024]{1,0:T(8,128)(2,1)S(1)}, bf16[64,1024]{1,0:T(8,128)(2,1)S(1)}, u32[]{:S(2)}, u32[]{:S(2)}) collective-permute-start(bf16[64,1024]{1,0:T(8,128)(2,1)S(1)} %bitcast.9), channel_id=1, source_target_pairs={{0,4},{1,3},{2,6},{3,1},{4,0},{5,7},{6,2},{7,5},{8,12},{9,11},{10,... | collective-permute-start | bytes 393224 | tf_op jit(solution)/shard_map/ppermute | solution.py:255
  19.0 1.5 %collective-permute-done.2.refs_6_ = bf16[64,1024]{1,0:T(8,128)(2,1)S(1)} collective-permute-done((bf16[64,1024]{1,0:T(8,128)(2,1)S(1)}, bf16[64,1024]{1,0:T(8,128)(2,1)S(1)}, u32[]{:S(2)}, u32[]{:S(2)}) %collective-permute-start.2) | collective-permute-done | bytes 131104 | tf_op jit(solution)/shard_map/ppermute | solution.py:255
  20.4 1.7 %collective-permute-start.12 = (bf16[64,1024]{1,0:T(8,128)(2,1)S(1)}, bf16[64,1024]{1,0:T(8,128)(2,1)S(1)}, u32[]{:S(2)}, u32[]{:S(2)}) collective-permute-start(bf16[64,1024]{1,0:T(8,128)(2,1)S(1)} %collective-permute-done.2.refs_6_), channel_id=1, source_target_pairs={{0,4},{1,3},{2,6},{3,1},{4,0},{5,7},{6,2},{7,5},{8,12},{9,11},{10,... | collective-permute-start | bytes 393224 | tf_op jit(solution)/shard_map/ppermute | solution.py:255
  22.4 2.0 %collective-permute-start.5 = (bf16[64,1024]{1,0:T(8,128)(2,1)S(1)}, bf16[64,1024]{1,0:T(8,128)(2,1)S(1)}, u32[]{:S(2)}, u32[]{:S(2)}) collective-permute-start(bf16[64,1024]{1,0:T(8,128)(2,1)S(1)} %collective-permute-done.4.refs_3_), channel_id=1, source_target_pairs={{0,8},{1,9},{2,10},{3,11},{4,12},{5,13},{6,14},{7,15},{8,0},{9,1},... | collective-permute-start | bytes 393224 | tf_op jit(solution)/shard_map/ppermute | solution.py:255
  24.5 1.0 %collective-permute-done.6.refs_2_ = bf16[64,1024]{1,0:T(8,128)(2,1)S(1)} collective-permute-done((bf16[64,1024]{1,0:T(8,128)(2,1)S(1)}, bf16[64,1024]{1,0:T(8,128)(2,1)S(1)}, u32[]{:S(2)}, u32[]{:S(2)}) %collective-permute-start.6) | collective-permute-done | bytes 131104 | tf_op jit(solution)/shard_map/ppermute | solution.py:255
  26.1 2.5 %early_scores.1 = (f32[768,1024]{1,0:T(8,128)S(1)}, f32[16,64]{1,0:T(8,128)S(1)}, f32[8,128]{1,0:T(8,128)S(1)}) custom-call(s32[1]{0:T(128)} %bitcast.1.id_ref, bf16[64,1024]{1,0:T(8,128)(2,1)S(1)} %bitcast.10, bf16[64,1024]{1,0:T(8,128)(2,1)S(1)} %collective-permute-done.8.refs_1_, bf16[64,1024]{1,0:T(8,128)(2,1)S(1)} %collective-permute-done.9.refs_2_, ...), custom_call_target="tpu_custom_call" | custom-call | flops 1610612736 | bytes 6836224 | tf_op jit(solution)/shard_map/early_scores/pallas_call | solution.py:196
  28.8 2.3 %collective-permute-done.7.refs_3_ = bf16[64,1024]{1,0:T(8,128)(2,1)S(1)} collective-permute-done((bf16[64,1024]{1,0:T(8,128)(2,1)S(1)}, bf16[64,1024]{1,0:T(8,128)(2,1)S(1)}, u32[]{:S(2)}, u32[]{:S(2)}) %collective-permute-start.7) | collective-permute-done | bytes 131104 | tf_op jit(solution)/shard_map/ppermute | solution.py:255
  31.1 1.1 %late_scores.1 = (f32[256,1024]{1,0:T(8,128)S(1)}, f32[16,8,128]{2,1,0:T(8,128)S(1)}) custom-call(s32[1]{0:T(128)} %bitcast.1.id_ref, bf16[64,1024]{1,0:T(8,128)(2,1)S(1)} %collective-permute-done.3.refs_0_, bf16[64,1024]{1,0:T(8,128)(2,1)S(1)} %collective-permute-done.5.refs_1_, bf16[64,1024]{1,0:T(8,128)(2,1)S(1)} %collective-permute-done.6.refs_2_, ...), custom_call_target="tpu_custom_call" | custom-call | flops 536870912 | bytes 3751936 | tf_op jit(solution)/shard_map/late_scores/pallas_call | solution.py:196
  32.2 10.6 %all_to_all.15.value_ref = f32[16,8,128]{2,1,0:T(8,128)S(1)} all-to-all(f32[16,8,128]{2,1,0:T(8,128)S(1)} %get-tuple-element.48), channel_id=1, replica_groups=mesh['grp'=1,'pool'=16,'samp'=2] {'pool'}, dimensions={0} | all-to-all | bytes 131072 | tf_op jit(solution)/shard_map/all_to_all | solution.py:327
  42.8 1.1 %columns.3 = (f32[1,1024]{1,0:T(1,128)S(1)}, f32[8,128]{1,0:T(8,128)}) custom-call(s32[1]{0:T(128)} %bitcast.1.id_ref, f32[16,8,128]{2,1,0:T(8,128)S(1)} %all_to_all.15.value_ref, f32[8,128]{1,0:T(8,128)S(1)} %get-tuple-element.49.norm_ref, f32[768,1024]{1,0:T(8,128)S(1)} %get-tuple-element.50.refs_0_, f32[256,1024]{1,0:T(8,128)S(1)} %get-tuple-element.51.refs_1_), custom_call_target="tpu_custom_call" | custom-call | flops 8388608 | bytes 4272128 | tf_op jit(solution)/shard_map/columns/pallas_call | solution.py:196
  44.1 1.2 %collective-permute-done.13 = f32[1,1024]{1,0:T(1,128)S(1)} collective-permute-done((f32[1,1024]{1,0:T(1,128)S(1)}, f32[1,1024]{1,0:T(1,128)S(1)}, u32[]{:S(2)}, u32[]{:S(2)}) %collective-permute-start.13) | collective-permute-done | bytes 4128 | tf_op jit(solution)/shard_map/ppermute | solution.py:338
  45.3 1.1 %rows.2 = f32[16,8,128]{2,1,0:T(8,128)S(1)} custom-call(s32[1]{0:T(128)} %bitcast.1.id_ref, f32[1,1024]{1,0:T(1,128)S(1)} %add_subtract_fusion.1.shift_ref, f32[768,1024]{1,0:T(8,128)S(1)} %get-tuple-element.50.refs_0_, f32[256,1024]{1,0:T(8,128)S(1)} %get-tuple-element.51.refs_1_), custom_call_target="tpu_custom_call" | custom-call | flops 8388608 | bytes 4263936 | tf_op jit(solution)/shard_map/rows/pallas_call | solution.py:196
  46.4 10.1 %all_to_all.16.value_ref = f32[16,8,128]{2,1,0:T(8,128)S(1)} all-to-all(f32[16,8,128]{2,1,0:T(8,128)S(1)} %rows.2), channel_id=1, replica_groups=mesh['grp'=1,'pool'=16,'samp'=2] {'pool'}, dimensions={0} | all-to-all | bytes 131072 | tf_op jit(solution)/shard_map/all_to_all | solution.py:327
  56.5 1.1 %columns.4 = (f32[1,1024]{1,0:T(1,128)S(1)}, f32[8,128]{1,0:T(8,128)}) custom-call(s32[1]{0:T(128)} %bitcast.1.id_ref, f32[16,8,128]{2,1,0:T(8,128)S(1)} %all_to_all.16.value_ref, f32[8,128]{1,0:T(8,128)S(1)} %get-tuple-element.49.norm_ref, f32[768,1024]{1,0:T(8,128)S(1)} %get-tuple-element.50.refs_0_, f32[256,1024]{1,0:T(8,128)S(1)} %get-tuple-element.51.refs_1_), custom_call_target="tpu_custom_call" | custom-call | flops 8388608 | bytes 4272128 | tf_op jit(solution)/shard_map/columns/pallas_call | solution.py:196
  57.7 1.2 %collective-permute-done.14 = f32[1,1024]{1,0:T(1,128)S(1)} collective-permute-done((f32[1,1024]{1,0:T(1,128)S(1)}, f32[1,1024]{1,0:T(1,128)S(1)}, u32[]{:S(2)}, u32[]{:S(2)}) %collective-permute-start.14) | collective-permute-done | bytes 4128 | tf_op jit(solution)/shard_map/ppermute | solution.py:338
  58.9 1.1 %rows.3 = f32[16,8,128]{2,1,0:T(8,128)S(1)} custom-call(s32[1]{0:T(128)} %bitcast.1.id_ref, f32[1,1024]{1,0:T(1,128)S(1)} %add_subtract_fusion.shift_ref, f32[768,1024]{1,0:T(8,128)S(1)} %get-tuple-element.50.refs_0_, f32[256,1024]{1,0:T(8,128)S(1)} %get-tuple-element.51.refs_1_), custom_call_target="tpu_custom_call" | custom-call | flops 8388608 | bytes 4263936 | tf_op jit(solution)/shard_map/rows/pallas_call | solution.py:196
  60.1 10.1 %all_to_all.17.value_ref = f32[16,8,128]{2,1,0:T(8,128)S(1)} all-to-all(f32[16,8,128]{2,1,0:T(8,128)S(1)} %rows.3), channel_id=1, replica_groups=mesh['grp'=1,'pool'=16,'samp'=2] {'pool'}, dimensions={0} | all-to-all | bytes 131072 | tf_op jit(solution)/shard_map/all_to_all | solution.py:327
  70.2 1.1 %columns.5 = (f32[1,1024]{1,0:T(1,128)S(1)}, f32[8,128]{1,0:T(8,128)S(1)}) custom-call(s32[1]{0:T(128)} %bitcast.1.id_ref, f32[16,8,128]{2,1,0:T(8,128)S(1)} %all_to_all.17.value_ref, f32[8,128]{1,0:T(8,128)S(1)} %get-tuple-element.49.norm_ref, f32[768,1024]{1,0:T(8,128)S(1)} %get-tuple-element.50.refs_0_, f32[256,1024]{1,0:T(8,128)S(1)} %get-tuple-element.51.refs_1_), custom_call_target="tpu_custom_call" | custom-call | flops 8388608 | bytes 4272128 | tf_op jit(solution)/shard_map/columns/pallas_call | solution.py:196
  (31 shorter events, 5.4 us)
Async XLA Ops:
  0.6 12.4 %collective-permute-start = (bf16[64,1024]{1,0:T(8,128)(2,1)}, bf16[64,1024]{1,0:T(8,128)(2,1)S(1)}, u32[]{:S(2)}, u32[]{:S(2)}) collective-permute-start(bf16[64,1024]{1,0:T(8,128)(2,1)} %bitcast.5), channel_id=1, source_target_pairs={{0,24},{1,25},{2,26},{3,27},{4,28},{5,29},{6,30},{7,31},{8,16},{9,... | collective-permute-start | bytes 393224 | tf_op jit(solution)/shard_map/ppermute | solution.py:255
  5.7 7.3 %collective-permute-start.1 = (bf16[64,1024]{1,0:T(8,128)(2,1)}, bf16[64,1024]{1,0:T(8,128)(2,1)S(1)}, u32[]{:S(2)}, u32[]{:S(2)}) collective-permute-start(bf16[64,1024]{1,0:T(8,128)(2,1)} %bitcast.6), channel_id=1, source_target_pairs={{0,8},{1,9},{2,10},{3,11},{4,12},{5,13},{6,14},{7,15},{8,0},{9,1},... | collective-permute-start | bytes 393224 | tf_op jit(solution)/shard_map/ppermute | solution.py:255
  5.7 7.3 %collective-permute-start.4 = (bf16[64,1024]{1,0:T(8,128)(2,1)}, bf16[64,1024]{1,0:T(8,128)(2,1)S(1)}, u32[]{:S(2)}, u32[]{:S(2)}) collective-permute-start(bf16[64,1024]{1,0:T(8,128)(2,1)} %bitcast.7), channel_id=1, source_target_pairs={{0,6},{1,7},{2,4},{3,5},{4,2},{5,3},{6,0},{7,1},{8,14},{9,15},{10,... | collective-permute-start | bytes 393224 | tf_op jit(solution)/shard_map/ppermute | solution.py:255
  8.2 10.5 %collective-permute-start.8 = (bf16[64,1024]{1,0:T(8,128)(2,1)}, bf16[64,1024]{1,0:T(8,128)(2,1)S(1)}, u32[]{:S(2)}, u32[]{:S(2)}) collective-permute-start(bf16[64,1024]{1,0:T(8,128)(2,1)} %bitcast.8), channel_id=1, source_target_pairs={{0,2},{1,5},{2,0},{3,7},{4,6},{5,1},{6,4},{7,3},{8,10},{9,13},{10,... | collective-permute-start | bytes 393224 | tf_op jit(solution)/shard_map/ppermute | solution.py:255
  9.4 1.6 %copy-start = (bf16[1024,1024]{1,0:T(8,128)(2,1)S(1)}, bf16[1024,1024]{1,0:T(8,128)(2,1)}, u32[]{:S(2)}) copy-start(bf16[1024,1024]{1,0:T(8,128)(2,1)} %pool_ref.1) | copy-start | bytes 6291460
  11.0 0.7 copy-start.1
  11.7 5.5 %copy-start.2 = (bf16[1,64,1024]{2,1,0:T(8,128)(2,1)S(1)}, bf16[1,64,1024]{2,1,0:T(8,128)(2,1)}, u32[]{:S(2)}) copy-start(bf16[1,64,1024]{2,1,0:T(8,128)(2,1)} %param.4) | copy-start | bytes 393220
  13.1 12.9 %collective-permute-start.10 = (bf16[128,1024]{1,0:T(8,128)(2,1)S(1)}, bf16[128,1024]{1,0:T(8,128)(2,1)S(1)}, u32[]{:S(2)}, u32[]{:S(2)}) collective-permute-start(bf16[128,1024]{1,0:T(8,128)(2,1)S(1)} %constant_dynamic-update-slice_fusion), channel_id=1, source_target_pairs={{0,2},{1,5},{2,0},{3,7},{4,6},{5,1},{6,4},{7,3},{8,10},{9,13},{10,... | collective-permute-start | bytes 786440 | tf_op jit(solution)/shard_map/ppermute | solution.py:255
  14.7 11.4 %collective-permute-start.11 = (bf16[128,1024]{1,0:T(8,128)(2,1)S(1)}, bf16[128,1024]{1,0:T(8,128)(2,1)S(1)}, u32[]{:S(2)}, u32[]{:S(2)}) collective-permute-start(bf16[128,1024]{1,0:T(8,128)(2,1)S(1)} %constant_dynamic-update-slice_fusion), channel_id=1, source_target_pairs={{0,4},{1,3},{2,6},{3,1},{4,0},{5,7},{6,2},{7,5},{8,12},{9,11},{10,... | collective-permute-start | bytes 786440 | tf_op jit(solution)/shard_map/ppermute | solution.py:255
  15.5 5.0 %collective-permute-start.2 = (bf16[64,1024]{1,0:T(8,128)(2,1)S(1)}, bf16[64,1024]{1,0:T(8,128)(2,1)S(1)}, u32[]{:S(2)}, u32[]{:S(2)}) collective-permute-start(bf16[64,1024]{1,0:T(8,128)(2,1)S(1)} %collective-permute-done.refs_5_), channel_id=1, source_target_pairs={{0,8},{1,9},{2,10},{3,11},{4,12},{5,13},{6,14},{7,15},{8,0},{9,1},... | collective-permute-start | bytes 393224 | tf_op jit(solution)/shard_map/ppermute | solution.py:255
  17.2 5.2 %collective-permute-start.9 = (bf16[64,1024]{1,0:T(8,128)(2,1)S(1)}, bf16[64,1024]{1,0:T(8,128)(2,1)S(1)}, u32[]{:S(2)}, u32[]{:S(2)}) collective-permute-start(bf16[64,1024]{1,0:T(8,128)(2,1)S(1)} %bitcast.9), channel_id=1, source_target_pairs={{0,4},{1,3},{2,6},{3,1},{4,0},{5,7},{6,2},{7,5},{8,12},{9,11},{10,... | collective-permute-start | bytes 393224 | tf_op jit(solution)/shard_map/ppermute | solution.py:255
  18.7 6.8 %collective-permute-start.6 = (bf16[64,1024]{1,0:T(8,128)(2,1)S(1)}, bf16[64,1024]{1,0:T(8,128)(2,1)S(1)}, u32[]{:S(2)}, u32[]{:S(2)}) collective-permute-start(bf16[64,1024]{1,0:T(8,128)(2,1)S(1)} %collective-permute-done.4.refs_3_), channel_id=1, source_target_pairs={{0,24},{1,25},{2,26},{3,27},{4,28},{5,29},{6,30},{7,31},{8,16},{9,... | collective-permute-start | bytes 393224 | tf_op jit(solution)/shard_map/ppermute | solution.py:255
  20.4 5.6 %collective-permute-start.12 = (bf16[64,1024]{1,0:T(8,128)(2,1)S(1)}, bf16[64,1024]{1,0:T(8,128)(2,1)S(1)}, u32[]{:S(2)}, u32[]{:S(2)}) collective-permute-start(bf16[64,1024]{1,0:T(8,128)(2,1)S(1)} %collective-permute-done.2.refs_6_), channel_id=1, source_target_pairs={{0,4},{1,3},{2,6},{3,1},{4,0},{5,7},{6,2},{7,5},{8,12},{9,11},{10,... | collective-permute-start | bytes 393224 | tf_op jit(solution)/shard_map/ppermute | solution.py:255
  22.4 6.3 %collective-permute-start.5 = (bf16[64,1024]{1,0:T(8,128)(2,1)S(1)}, bf16[64,1024]{1,0:T(8,128)(2,1)S(1)}, u32[]{:S(2)}, u32[]{:S(2)}) collective-permute-start(bf16[64,1024]{1,0:T(8,128)(2,1)S(1)} %collective-permute-done.4.refs_3_), channel_id=1, source_target_pairs={{0,8},{1,9},{2,10},{3,11},{4,12},{5,13},{6,14},{7,15},{8,0},{9,1},... | collective-permute-start | bytes 393224 | tf_op jit(solution)/shard_map/ppermute | solution.py:255
  25.5 5.6 %collective-permute-start.3 = (bf16[64,1024]{1,0:T(8,128)(2,1)S(1)}, bf16[64,1024]{1,0:T(8,128)(2,1)S(1)}, u32[]{:S(2)}, u32[]{:S(2)}) collective-permute-start(bf16[64,1024]{1,0:T(8,128)(2,1)S(1)} %collective-permute-done.2.refs_6_), channel_id=1, source_target_pairs={{0,2},{1,5},{2,0},{3,7},{4,6},{5,1},{6,4},{7,3},{8,10},{9,13},{10,... | collective-permute-start | bytes 393224 | tf_op jit(solution)/shard_map/ppermute | solution.py:255
  26.0 5.1 %collective-permute-start.7 = (bf16[64,1024]{1,0:T(8,128)(2,1)S(1)}, bf16[64,1024]{1,0:T(8,128)(2,1)S(1)}, u32[]{:S(2)}, u32[]{:S(2)}) collective-permute-start(bf16[64,1024]{1,0:T(8,128)(2,1)S(1)} %collective-permute-done.6.refs_2_), channel_id=1, source_target_pairs={{0,8},{1,9},{2,10},{3,11},{4,12},{5,13},{6,14},{7,15},{8,0},{9,1},... | collective-permute-start | bytes 393224 | tf_op jit(solution)/shard_map/ppermute | solution.py:255
  44.0 1.2 %collective-permute-start.13 = (f32[1,1024]{1,0:T(1,128)S(1)}, f32[1,1024]{1,0:T(1,128)S(1)}, u32[]{:S(2)}, u32[]{:S(2)}) collective-permute-start(f32[1,1024]{1,0:T(1,128)S(1)} %get-tuple-element.52), channel_id=1, source_target_pairs={{0,1},{1,0},{2,3},{3,2},{4,5},{5,4},{6,7},{7,6},{8,9},{9,8},{10,11... | collective-permute-start | bytes 12296 | tf_op jit(solution)/shard_map/ppermute | solution.py:338
  57.7 1.2 %collective-permute-start.14 = (f32[1,1024]{1,0:T(1,128)S(1)}, f32[1,1024]{1,0:T(1,128)S(1)}, u32[]{:S(2)}, u32[]{:S(2)}) collective-permute-start(f32[1,1024]{1,0:T(1,128)S(1)} %get-tuple-element.53), channel_id=1, source_target_pairs={{0,1},{1,0},{2,3},{3,2},{4,5},{5,4},{6,7},{7,6},{8,9},{9,8},{10,11... | collective-permute-start | bytes 12296 | tf_op jit(solution)/shard_map/ppermute | solution.py:338
  71.3 1.2 %collective-permute-start.15 = (f32[1,1024]{1,0:T(1,128)S(1)}, f32[1,1024]{1,0:T(1,128)S(1)}, u32[]{:S(2)}, u32[]{:S(2)}) collective-permute-start(f32[1,1024]{1,0:T(1,128)S(1)} %get-tuple-element.55), channel_id=1, source_target_pairs={{0,1},{1,0},{2,3},{3,2},{4,5},{5,4},{6,7},{7,6},{8,9},{9,8},{10,11... | collective-permute-start | bytes 12296 | tf_op jit(solution)/shard_map/ppermute | solution.py:338
